TPU v7x, 32 devices: a whole 2x2x4 slice. The times are simulated.
32 devices in a mesh: seq: 8 (over z, x), head: 4 (over y, core).
Axes of the slice: x: 2, y: 2, z: 4, core: 2. Of those that a mesh axis runs over, the one named last changes fastest.
Arguments:
- tokens: bfloat16 [8192, 1024], P(('seq', 'head')), may hold values from -6 to 6
- norm_gain: float32 [1024], replicated, may hold values from 0.5 to 1.5
- w_qkv: bfloat16 [1024, 8, 384], P(None, 'head'), may hold values from -0.1875 to 0.1875
- w_mem_gates: bfloat16 [8, 3, 128], P('head'), may hold values from -0.5 to 0.5
- persist_keys: bfloat16 [16, 1024], P(None, 'head'), may hold values from -6 to 6
- persist_values: bfloat16 [16, 1024], P(None, 'head'), may hold values from -6 to 6
- alpha_bias: float32 [8], P('head'), may hold values from -8 to -2
- eta_bias: float32 [8], P('head'), may hold values from -1 to 3
- w_out: bfloat16 [1024, 1024], P('head'), may hold values from -0.1875 to 0.1875
- ffn_gain: float32 [1024], replicated, may hold values from 0.5 to 1.5
- w_gate: bfloat16 [1024, 2816], replicated, may hold values from -0.1875 to 0.1875
- w_up: bfloat16 [1024, 2816], replicated, may hold values from -0.1875 to 0.1875
- w_down: bfloat16 [2816, 1024], replicated, may hold values from -0.109375 to 0.109375
- segment_ids: int32 [8192], replicated, may hold values from 0 to 3, as said below
- block_table: int32 [128], replicated, may hold values from 0 to 127, as said below
Outputs:
- mixed: bfloat16 [8192, 1024], P(('seq', 'head'))
- kv_cache: bfloat16 [128, 64, 2048], P('seq', None, 'head')
Inputs may be any that keep to these rules, and one draw needn't show every extreme that they name: `segment_ids`: segment numbers never fall along the stream and change only at multiples of 64 tokens; all 4 numbers occur, and one prompt holds exactly 4096 tokens. `block_table`: A permutation of the cache rows. Row r belongs to owner r // 16; the 16 blocks of each index of seq (blocks i * 16 to (i + 1) * 16 - 1) put exactly 2 blocks with every owner.
All inputs are finite; a program needn't handle non-finite values.
Results may differ from a plain program's by a relative error of at most 0.02.
Values may be sent and summed in bfloat16 or wider, within the bound.
No kernel may reach another device: no remote copies, remote signals or barrier semaphores. Data moves between devices by JAX's collectives and lax.ppermute only.
A program may use at most 128 MiB of HBM per device.

v0:
```python
import functools

import jax
import jax.numpy as jnp
from jax import lax
from jax.experimental import pallas as pl
from jax.experimental.pallas import tpu as pltpu
from jax.sharding import PartitionSpec as P

PERS = 16
SPAN = 64
EPS = 1e-05
TINY = 1e-06
BF = jnp.bfloat16
F32 = jnp.float32
SCALE = 0.001
VMEM_LIMIT = 12 * 1024 * 1024
MOST_VMEM = 60 * 1024 * 1024
CUTS = 2


def dot(a, b):
    return jnp.dot(a, b, preferred_element_type=F32)


def vmem():
    return pl.BlockSpec(memory_space=pltpu.VMEM)


def smem():
    return pl.BlockSpec(memory_space=pltpu.SMEM)


def loaded(shape):
    return pl.BlockSpec(shape, lambda i: (0,) * len(shape))


def exchange(value, axis, bit):
    count = lax.axis_size(axis)
    return lax.ppermute(value, axis, [(i, i ^ bit) for i in range(count)])


def params(limit=VMEM_LIMIT):
    return pltpu.CompilerParams(vmem_limit_bytes=limit)


def cost(flops, size):
    return pl.CostEstimate(flops=int(flops * SCALE), bytes_accessed=int(size * SCALE), transcendentals=0)


def compose(later, earlier):
    d = later.shape[0] // 2
    joined = dot(later[:, : 2 * d].astype(BF), earlier.astype(BF))
    shift = joined[:, 2 * d :] + later[:, 2 * d :].astype(F32)
    return jnp.concatenate([joined[:, : 2 * d], shift], axis=1)


def ordered(flag, one, other):
    swap = flag != 0
    return jnp.where(swap, other, one), jnp.where(swap, one, other)


def rms_plain(values):
    return values * lax.rsqrt(jnp.mean(values * values, axis=-1, keepdims=True) + TINY)


def pair_kernel(heads, d, blocks, rel, is_last, groups, parts, *refs):
    refs = list(refs)
    meta_ref, flat_ref = refs[:2]
    x_refs = [refs[2 : 2 + parts[0]], refs[2 + parts[0] : 2 + sum(parts)]]
    refs = refs[2 + sum(parts) :]
    gain_ref, w_ref, gates_ref, start_ref = refs[:4]
    others = refs[4 : 4 + groups - 1] if is_last else []
    outs = refs[4 + len(others) :]
    kv_out, r_ref, group_ref = outs[:3]
    total_refs = outs[3:-2]
    kv_ref, sem = outs[-2:]
    bias = flat_ref.shape[0] - 2 * heads
    me = meta_ref[0]
    gain = gain_ref[...]
    w = w_ref[...]
    kept = {}
    for s in range(2):
        x = jnp.concatenate([ref[...] for ref in x_refs[s]], axis=0).astype(F32)
        scale = lax.rsqrt(jnp.mean(x * x, axis=-1, keepdims=True) + EPS)
        projected = dot((x * scale * gain).astype(BF), w)
        base = (me ^ (rel + s)) * blocks
        for h in range(heads):
            q = projected[:, 3 * d * h : 3 * d * h + d]
            k = projected[:, 3 * d * h + d : 3 * d * h + 2 * d]
            v = projected[:, 3 * d * h + 2 * d : 3 * d * h + 3 * d]
            q = rms_plain(q) * d**-0.5
            k = rms_plain(k) * d**-0.5
            kb, vb = k.astype(BF), v.astype(BF)
            logits = dot(vb, gates_ref[h])
            theta = jax.nn.sigmoid(logits[:, :d]) * (1.0 / SPAN)
            weighted = (theta * k).astype(BF)
            both = jnp.concatenate([kb, vb], axis=1)
            items = []
            for c in range(blocks):
                part = slice(c * SPAN, (c + 1) * SPAN)
                kv_ref[s * blocks + c, :, 2 * d * h : 2 * d * (h + 1)] = both[part]
                products = lax.dot_general(
                    weighted[part], both[part], (((0,), (0,)), ((), ())), preferred_element_type=F32
                )
                alpha = jax.nn.sigmoid(jnp.mean(logits[part, d : 2 * d], axis=0, keepdims=True) + flat_ref[bias + h])
                eta = jax.nn.sigmoid(
                    jnp.mean(logits[part, 2 * d :], axis=0, keepdims=True) + flat_ref[bias + heads + h]
                )
                widen = lambda row: jnp.concatenate([row, row, row], axis=1)
                items.append((products, widen(1.0 - alpha), widen(eta), q[part].astype(BF), flat_ref[base + c]))
            kept[s, h] = items
    copies = [pltpu.make_async_copy(kv_ref, kv_out, sem.at[0])]
    copies[0].start()
    zero = jnp.zeros((d, d), F32)
    row = lax.broadcasted_iota(jnp.int32, (d, d), 0)
    column = lax.broadcasted_iota(jnp.int32, (d, d), 1)
    eye = jnp.where(row == column, 1.0, 0.0).astype(F32)
    state = {}
    starts = []
    for h in range(heads):
        first = start_ref[h]
        starts.append(jnp.concatenate([zero, zero, first], axis=1))
    for key in kept:
        state[key] = (jnp.concatenate([eye, zero, zero], axis=1), jnp.concatenate([zero, eye, zero], axis=1))
    for c in range(blocks):
        for s in range(2):
            for h in range(heads):
                products, stay, eta, q, keep = kept[s, h][c]
                memory, moment = state[s, h]
                held = keep * memory + (1.0 - keep) * starts[h]
                held_low = held.astype(BF)
                recalled = dot(q, held_low)
                part = slice(c * SPAN, (c + 1) * SPAN)
                r_ref[s, h, part, :] = recalled
                cross = jnp.concatenate([zero, zero, products[:, d:]], axis=1)
                moment = eta * (keep * moment) - dot(products[:, :d].astype(BF), held_low) + cross
                state[s, h] = (stay * held + moment, moment)
    late = 1 - (me & 1)
    for h in range(heads):
        maps = [jnp.concatenate(state[s, h], axis=0) for s in range(2)]
        earlier, later = ordered(me & 1, maps[0], maps[1])
        low = earlier.astype(BF)
        total = compose(later, low)
        group_ref[h] = total.astype(BF)
        if is_last:
            level = [others[g][h] for g in range(groups - 1)] + [total]
            bit = 2
            while len(level) > 1:
                joined = []
                for i in range(0, len(level), 2):
                    earlier, later = ordered(me & bit, level[i].astype(F32), level[i + 1].astype(F32))
                    joined.append(compose(later, earlier))
                level = joined
                bit *= 2
            for i in range(2):
                total_refs[2 * h + i][...] = level[0][i * d : (i + 1) * d].astype(BF)
        recalled = r_ref[late, h]
        folded = dot(recalled[:, : 2 * d].astype(BF), low)
        r_ref[late, h, :, : 2 * d] = folded[:, : 2 * d]
        r_ref[late, h, :, 2 * d :] = folded[:, 2 * d :] + recalled[:, 2 * d :]
    for one in copies:
        one.wait()


def pair_call(meta, flat, xs, gain, w, gates, initial, rel, before, is_last):
    heads, d = gates.shape[0], gates.shape[1]
    parts = [len(x) for x in xs]
    rows = sum(x.shape[0] for x in xs[0])
    blocks = rows // SPAN
    groups = len(before) + 1
    extra = [b["map"] for b in before] if is_last else []
    hbm = pl.BlockSpec(memory_space=pltpu.HBM)
    row = heads * 2 * d
    shapes = [
        jax.ShapeDtypeStruct((2 * blocks, SPAN, row), BF),
        jax.ShapeDtypeStruct((2, heads, rows, 3 * d), F32),
        jax.ShapeDtypeStruct((heads, 2 * d, 3 * d), BF),
    ]
    specs = [hbm, vmem(), vmem()]
    if is_last:
        shapes += [jax.ShapeDtypeStruct((d, 3 * d), BF)] * (2 * heads)
        specs += [vmem()] * (2 * heads)
    out = pl.pallas_call(
        functools.partial(pair_kernel, heads, d, blocks, rel, is_last, groups, parts),
        out_shape=shapes,
        grid=(1,),
        in_specs=[smem()] * 2
        + [vmem()] * (sum(parts) + 4)
        + [vmem()] * len(extra),
        out_specs=specs,
        scratch_shapes=[
            pltpu.VMEM((2 * blocks, SPAN, row), BF),
            pltpu.SemaphoreType.DMA((1,)),
        ],
        compiler_params=params(),
        cost_estimate=cost(2.5e9, 8e6),
        name="pair_last" if is_last else "pair_first",
    )(meta, flat, *xs[0], *xs[1], gain, w, gates, initial, *extra)
    names = ["kv", "r", "map"]
    return dict(zip(names, out), total=out[3:])


def join_kernel(heads, d, seq_ref, *refs):
    own_refs, got_refs, (a_ref, b_ref, got_ref) = refs[: 2 * heads], refs[2 * heads : 4 * heads], refs[4 * heads :]
    for h in range(heads):
        own, got = (
            jnp.concatenate([ref[...] for ref in side[2 * h : 2 * h + 2]], axis=0) for side in (own_refs, got_refs)
        )
        earlier, later = ordered(seq_ref[0] & 1, own.astype(F32), got.astype(F32))
        joined = compose(later, earlier).astype(BF)
        a_ref[h] = joined[:, : 2 * d]
        b_ref[h] = joined[:, 2 * d :]
        got_ref[h] = got


def join(seq, own, got):
    heads, d = len(own) // 2, own[0].shape[0]
    shapes = [(heads, 2 * d, 2 * d), (heads, 2 * d, d), (heads, 2 * d, 3 * d)]
    return pl.pallas_call(
        functools.partial(join_kernel, heads, d),
        out_shape=[jax.ShapeDtypeStruct(shape, BF) for shape in shapes],
        in_specs=[smem()] + [vmem()] * (4 * heads),
        out_specs=[vmem()] * 3,
        compiler_params=params(),
        cost_estimate=cost(1e8, 1.2e6),
        name="join",
    )(seq, *own, *got)


def step_kernel(heads, a_ref, b_ref, state_ref, out_ref):
    for h in range(heads):
        out_ref[h] = (dot(a_ref[h], state_ref[h]) + b_ref[h].astype(F32)).astype(BF)


def step(a, b, state):
    return pl.pallas_call(
        functools.partial(step_kernel, a.shape[0]),
        out_shape=jax.ShapeDtypeStruct(b.shape, BF),
        in_specs=[vmem()] * 3,
        out_specs=vmem(),
        compiler_params=params(),
        cost_estimate=cost(1e8, 6e5),
        name="step",
    )(a, b, state)


def fold_kernel(heads, d, groups, *refs):
    meta_ref, seq_ref, got_ref = refs[:3]
    map_refs, r_refs = (refs[3 + i * groups : 3 + (i + 1) * groups] for i in range(2))
    out_ref, out0_ref = refs[3 + 2 * groups :]
    me, odd = meta_ref[0], (seq_ref[0] & 1) != 0
    d2 = 2 * d
    shape = (d2, 3 * d)
    identity = jnp.where(
        lax.broadcasted_iota(jnp.int32, shape, 0) == lax.broadcasted_iota(jnp.int32, shape, 1), 1.0, 0.0
    ).astype(F32)
    fronts = []
    for h in range(heads):
        before = [jnp.where(odd, got_ref[h].astype(F32), identity)] * groups
        own = [identity] * groups
        level = [map_refs[g][h].astype(F32) for g in range(groups)]
        bit, span = 2, 1
        while len(level) > 1:
            joined = []
            for i in range(0, len(level), 2):
                for side in range(2):
                    active = (me & bit) != side * bit
                    sibling = level[i + 1 - side]
                    for g in range((i + side) * span, (i + side + 1) * span):
                        after = sibling if span == 1 else compose(own[g], sibling)
                        own[g] = jnp.where(active, after, own[g])
                if len(level) > 2:
                    earlier, later = ordered(me & bit, level[i], level[i + 1])
                    joined.append(compose(later, earlier))
                else:
                    joined.append(None)
            level = joined
            bit, span = bit * 2, span * 2
        fronts.append([compose(own[g], before[g]).astype(BF) for g in range(groups)])
    for g in range(groups):
        for s in range(2):
            r = 2 * g + s
            for h in range(heads):
                folded = dot(r_refs[g][s, h, :, :d2].astype(BF), fronts[h][g])
                out_ref[r, h] = folded[:, :d2].astype(BF)
                out0_ref[r, h] = folded[:, d2:] + r_refs[g][s, h, :, d2:]


def fold(meta, seq, got, pairs):
    groups = len(pairs)
    _, heads, rows, width = pairs[0]["r"].shape
    d = width // 3
    shapes = [(2 * groups, heads, rows, 2 * d), (2 * groups, heads, rows, d)]
    return pl.pallas_call(
        functools.partial(fold_kernel, heads, d, groups),
        out_shape=[jax.ShapeDtypeStruct(shapes[0], BF), jax.ShapeDtypeStruct(shapes[1], F32)],
        in_specs=[smem(), smem(), vmem()] + [vmem()] * (2 * groups),
        out_specs=[vmem()] * 2,
        compiler_params=params(),
        cost_estimate=cost(1.2e9, 6e6),
        name="fold",
    )(meta, seq, got, *[p["map"] for p in pairs], *[p["r"] for p in pairs])


def recall_kernel(heads, d, shards, r_ref, r0_ref, state_ref, *out_refs):
    for r in reversed(range(shards)):
        for h in range(heads):
            recalled = dot(r_ref[r, h], state_ref[h]) + r0_ref[r, h]
            out_refs[r][:, h * d : (h + 1) * d] = rms_plain(recalled).astype(BF)


def recall(r, r0, state):
    shards, heads, rows, width = r.shape
    d = width // 2
    return pl.pallas_call(
        functools.partial(recall_kernel, heads, d, shards),
        out_shape=[jax.ShapeDtypeStruct((rows, heads * d), BF)] * shards,
        in_specs=[vmem()] * 3,
        out_specs=[vmem()] * shards,
        compiler_params=params(),
        cost_estimate=cost(2e8, 3e6),
        name="recall",
    )(r, r0, state)


def ffn_kernel(shards, tile, *refs):
    sources, out_ref, targets = refs[: 2 * shards + 5], refs[2 * shards + 5], refs[2 * shards + 6 : -3]
    hidden_ref, residual_ref, sem = refs[-3:]
    wg_ref, wu_ref, wd_ref = targets[-3:]
    small = [
        pltpu.make_async_copy(source, target, sem.at[i])
        for i, (source, target) in enumerate(zip(sources[:-3], targets[:-3]))
    ]
    down = pltpu.make_async_copy(sources[-1], wd_ref, sem.at[len(small)])
    columns = []
    for i in range(wg_ref.shape[1] // tile):
        part = pl.ds(i * tile, tile)
        at = len(small) + 1 + 2 * i
        columns.append(
            [
                pltpu.make_async_copy(sources[-3].at[:, part], wg_ref.at[:, part], sem.at[at]),
                pltpu.make_async_copy(sources[-2].at[:, part], wu_ref.at[:, part], sem.at[at + 1]),
            ]
        )
    for one in small + [one for pair in columns for one in pair] + [down]:
        one.start()
    for one in small:
        one.wait()
    x_ref, gain_ref = targets[:2]
    residual = x_ref[...].astype(F32)
    for r in range(shards):
        residual += dot(targets[2 + r][...], targets[2 + shards + r][...])
    residual_ref[...] = residual
    scale = lax.rsqrt(jnp.mean(residual * residual, axis=-1, keepdims=True) + EPS)
    low = (residual * scale * gain_ref[...]).astype(BF)
    for i, pair in enumerate(columns):
        for one in pair:
            one.wait()
        part = slice(i * tile, (i + 1) * tile)
        gate = dot(low, wg_ref[:, part])
        up = dot(low, wu_ref[:, part])
        hidden_ref[:, part] = (gate / (1.0 + jnp.exp(-gate)) * up).astype(BF)
    down.wait()
    out_ref[...] = (residual_ref[...] + dot(hidden_ref[...], wd_ref[...])).astype(BF)


def ffn(x, gain, w_out, pieces, w_gate, w_up, w_down):
    rows, width = x.shape
    hidden = w_gate.shape[1]
    tile = 256
    while hidden % tile:
        tile //= 2
    shards = len(pieces)
    sources = [x, gain, *pieces, *w_out, w_gate, w_up, w_down]
    return pl.pallas_call(
        functools.partial(ffn_kernel, shards, tile),
        out_shape=jax.ShapeDtypeStruct((rows, width), BF),
        in_specs=[pl.BlockSpec(memory_space=pl.ANY)] * len(sources),
        out_specs=vmem(),
        scratch_shapes=[pltpu.VMEM(a.shape, a.dtype) for a in sources]
        + [
            pltpu.VMEM((rows, hidden), BF),
            pltpu.VMEM((rows, width), F32),
            pltpu.SemaphoreType.DMA((2 * shards + 3 + 2 * (hidden // tile),)),
        ],
        compiler_params=params(MOST_VMEM),
        cost_estimate=cost(5e9, 2.2e7),
        name="ffn",
    )(*sources)


def pack_kernel(groups, order_ref, *refs):
    kv_refs, targets, (stage, sem_in, sem_out) = refs[:groups], refs[groups:-3], refs[-3:]
    count = kv_refs[0].shape[0]
    into = [
        pltpu.make_async_copy(kv_refs[g], stage.at[pl.ds(g * count, count)], sem_in.at[g]) for g in range(groups)
    ]
    out = []
    for target in targets:
        for i in range(target.shape[0]):
            n = len(out)
            out.append(pltpu.make_async_copy(stage.at[order_ref[n]], target.at[i], sem_out.at[n]))
    for one in into:
        one.start()
    for one in into:
        one.wait()
    for one in out:
        one.start()
    for one in out:
        one.wait()


def pack(order, kv, counts):
    hbm = pl.BlockSpec(memory_space=pltpu.HBM)
    blocks = sum(counts)
    block = kv[0].shape[1:]
    return pl.pallas_call(
        functools.partial(pack_kernel, len(kv)),
        out_shape=[jax.ShapeDtypeStruct((n,) + block, BF) for n in counts],
        in_specs=[smem()] + [hbm] * len(kv),
        out_specs=[hbm] * len(counts),
        scratch_shapes=[
            pltpu.VMEM((blocks,) + block, BF),
            pltpu.SemaphoreType.DMA((len(kv),)),
            pltpu.SemaphoreType.DMA((blocks,)),
        ],
        compiler_params=params(),
        cost_estimate=cost(0, 4e6),
        name="pack",
    )(order, *kv)


def place_kernel(rows_ref, *refs):
    sources, (out_ref, stage, sem_in, sem_out) = refs[:-4], refs[-4:]
    into, out = [], []
    for source in sources:
        for i in range(source.shape[0]):
            n = len(into)
            into.append(pltpu.make_async_copy(source.at[i], stage.at[n], sem_in.at[n]))
            out.append(pltpu.make_async_copy(stage.at[n], out_ref.at[rows_ref[n]], sem_out.at[n]))
    for one in into:
        one.start()
    for first, second in zip(into, out):
        first.wait()
        second.start()
    for one in out:
        one.wait()


def place(rows, sources):
    anywhere = pl.BlockSpec(memory_space=pl.ANY)
    count = rows.shape[0]
    shape = (count,) + sources[0].shape[1:]
    return pl.pallas_call(
        place_kernel,
        out_shape=jax.ShapeDtypeStruct(shape, sources[0].dtype),
        in_specs=[smem()] + [anywhere] * len(sources),
        out_specs=anywhere,
        scratch_shapes=[
            pltpu.VMEM(shape, sources[0].dtype),
            pltpu.SemaphoreType.DMA((count,)),
            pltpu.SemaphoreType.DMA((count,)),
        ],
        compiler_params=params(MOST_VMEM),
        cost_estimate=cost(0, 4 * sources[0].size * len(sources)),
        name="place",
    )(rows, *sources)


def per_device(
    tokens,
    norm_gain,
    w_qkv,
    w_mem_gates,
    persist_keys,
    persist_values,
    alpha_bias,
    eta_bias,
    w_out,
    ffn_gain,
    w_gate,
    w_up,
    w_down,
    segment_ids,
    block_table,
):
    model_dim = tokens.shape[1]
    heads, d = w_qkv.shape[1], w_mem_gates.shape[2]
    shards = lax.axis_size("head")
    n_seq = lax.axis_size("seq")
    seq_index, head_index = lax.axis_index("seq"), lax.axis_index("head")
    blocks_here = shards * tokens.shape[0] // SPAN
    per_owner = blocks_here // n_seq

    count = tokens.shape[0] // SPAN
    cut = tokens.shape[0] // CUTS
    parts = [tokens[i * cut : (i + 1) * cut] for i in range(CUTS)]
    far = [[exchange(part, "head", 2 * g) for part in parts] for g in range(1, shards // 2)]
    xs = {0: [parts, [exchange(tokens, "head", 1)]]}

    int32 = jnp.int32
    half = blocks_here // 2
    parity, place_in_line = seq_index & 1, seq_index >> 1
    id_blocks = segment_ids.reshape(-1, SPAN)[:, 0]
    keep_all = jnp.concatenate([jnp.zeros((1,), F32), (id_blocks[1:] == id_blocks[:-1]).astype(F32)])
    keep = lax.dynamic_slice_in_dim(keep_all, seq_index * blocks_here, blocks_here)
    flat = jnp.concatenate([keep, alpha_bias, eta_bias])
    meta = head_index.astype(int32)[None]
    seq = seq_index.astype(int32)[None]

    gates = jnp.broadcast_to(
        jnp.transpose(w_mem_gates, (0, 2, 1))[:, :, :, None], (heads, d, 3, d)
    ).reshape(heads, d, 3 * d)
    w = w_qkv.reshape(model_dim, heads * 3 * d)
    gain = norm_gain.reshape(1, -1)
    pkeys = persist_keys.reshape(PERS, heads, d)
    pvalues = persist_values.reshape(PERS, heads, d)
    initial = jnp.einsum("phd,phe->hde", pkeys, pvalues, preferred_element_type=F32) / PERS

    pairs = []
    groups = shards // 2
    for g in range(groups):
        if g > 0:
            far[g - 1], pairs[0]["map"] = lax.optimization_barrier((far[g - 1], pairs[0]["map"]))
            xs[g] = [far[g - 1], [exchange(part, "head", 1) for part in far[g - 1]]]
        pairs.append(pair_call(meta, flat, xs[g], gain, w, gates, initial, 2 * g, pairs, g == groups - 1))
    total, block_table, w_out = lax.optimization_barrier((pairs[-1]["total"], block_table, w_out))
    w_outs = [w_out] + [exchange(w_out, "head", 2 * g) for g in range(1, groups)]
    got = [exchange(part, "seq", 1) for part in total]

    mine = lax.dynamic_slice_in_dim(block_table, seq_index * blocks_here, blocks_here)
    owners = mine // blocks_here
    slots = jnp.arange(blocks_here, dtype=int32)
    same_owner = (owners[:, None] == owners[None, :]) & (slots[None, :] < slots[:, None])
    rank = jnp.sum(same_owner.astype(int32), axis=1)
    position = ((owners & 1) ^ parity ^ 1) * half + ((owners >> 1) ^ place_in_line) * per_owner + rank
    relative = ((slots // count) ^ head_index) * count + slots % count
    order = jnp.sum(jnp.where(position[None, :] == slots[:, None], relative[None, :], 0), axis=1).astype(int32)
    to_me = (block_table // blocks_here == seq_index).reshape(n_seq, blocks_here)
    earlier = to_me[:, None, :] & (slots[None, None, :] < slots[None, :, None])
    sources = jnp.arange(n_seq, dtype=int32)[:, None]
    arrival = (
        jnp.sum(earlier.astype(int32), axis=2)
        + ((sources & 1) ^ parity ^ 1) * half
        + ((sources >> 1) ^ place_in_line) * per_owner
    )
    landed = (arrival.reshape(1, -1) == slots[:, None]) & to_me.reshape(1, -1)
    rows = jnp.sum(jnp.where(landed, (block_table % blocks_here)[None, :], 0), axis=1).astype(int32)

    line = n_seq // 2
    packed = pack(order, [p["kv"] for p in pairs], (half,) + (per_owner,) * line)
    cross, same = packed[0], list(packed[1:])
    got, cross, same = lax.optimization_barrier((got, cross, same))
    a, b, got = join(seq, total, got)
    b, cross = lax.optimization_barrier((b, cross))
    cross = exchange(cross, "seq", 1)
    r, r0 = fold(meta, seq, got, pairs)
    onward = [(i, i + 2) for i in range(n_seq - 2)]
    hops = n_seq // 4
    state = b
    for hop in range(hops):
        state = lax.ppermute(state, "seq", onward)
        if hop == 0:
            state, r, w_outs = lax.optimization_barrier((state, r, w_outs))
        if hop < hops - 1:
            state = step(a, b, state)
    state, cross = lax.optimization_barrier((state, cross))
    w_outs = [w for one in w_outs for w in (one, exchange(one, "head", 1))]
    retrieved = list(recall(r, r0, state))
    pieces = [retrieved[0]] + [exchange(retrieved[i], "head", i) for i in range(1, shards)]
    cross = [cross[m * per_owner : (m + 1) * per_owner] for m in range(line)]
    cross = cross[:1] + [exchange(cross[m], "seq", 2 * m) for m in range(1, line)]
    same = [same[m] if m == 0 else exchange(same[m], "seq", 2 * m) for m in range(line)]
    mixed = ffn(tokens, ffn_gain.reshape(1, -1), w_outs, pieces, w_gate, w_up, w_down)
    mixed, cross, same = lax.optimization_barrier((mixed, cross, same))
    kv_cache = place(rows, cross + same)
    return mixed, kv_cache


def solution(mesh):
    return jax.shard_map(
        per_device,
        mesh=mesh,
        in_specs=(
            P(("seq", "head"), None),
            P(),
            P(None, "head", None),
            P("head", None, None),
            P(None, "head"),
            P(None, "head"),
            P("head"),
            P("head"),
            P("head", None),
            P(),
            P(),
            P(),
            P(),
            P(),
            P(),
        ),
        out_specs=(P(("seq", "head"), None), P("seq", None, "head")),
        check_vma=False,
    )
```

profile of v0, /device:TPU:0, one launch (start us, length us, event | category | flops | bytes accessed | tf_op | source)
XLA Modules:
  0.0 90.8 jit_solution(4006670485285367047)
XLA Ops:
  0.6 0.5 collective-permute-start.2
  1.2 1.1 %fusion.11 = (bf16[128,1024]{1,0:T(8,128)(2,1)S(1)}, bf16[128,1024]{1,0:T(8,128)(2,1)S(1)}) fusion(bf16[256,1024]{1,0:T(8,128)(2,1)} %refs_0_.1), kind=kLoop, calls=%fused_computation.40 | loop fusion | bytes 1048576 | tf_op jit(solution)/shard_map/slice | solution.py:498
  2.2 2.6 %collective-permute-start = (bf16[128,1024]{1,0:T(8,128)(2,1)S(1)}, bf16[128,1024]{1,0:T(8,128)(2,1)}, u32[]{:S(2)}, u32[]{:S(2)}) collective-permute-start(bf16[128,1024]{1,0:T(8,128)(2,1)S(1)} %get-tuple-element.125.refs_2_), channel_id=1, source_target_pairs={{0,2},{1,3},{2,0},{3,1},{4,6},{5,7},{6,4},{7,5},{8,10},{9,11},{10,... | collective-permute-start | bytes 786440 | tf_op jit(solution)/shard_map/ppermute | solution.py:40
  4.9 0.8 reshape.117
  6.0 0.8 pad_maximum_fusion.refs_1_
  6.8 1.8 %copy.37 = bf16[128,8,2,384]{3,1,2,0:T(8,128)(2,1)S(1)} copy(bf16[128,8,2,384]{3,2,1,0:T(2,128)(2,1)} %bitcast.26) | data formatting | bytes 3145728
  9.0 0.8 copy-done.5
  9.8 1.0 %copy-done.6 = bf16[256,1024]{1,0:T(8,128)(2,1)S(1)} copy-done((bf16[256,1024]{1,0:T(8,128)(2,1)S(1)}, bf16[256,1024]{1,0:T(8,128)(2,1)}, u32[]{:S(2)}) %copy-start.6) | copy-done | bytes 524312
  10.9 4.5 %pair_first.1 = (bf16[8,64,512]{2,1,0:T(8,128)(2,1)S(1)}, f32[2,2,256,384]{3,2,1,0:T(8,128)S(1)}, bf16[2,256,384]{2,1,0:T(8,128)(2,1)S(1)}) custom-call(s32[1]{0:T(128)} %bitcast.2.refs_0_, f32[20]{0:T(128)S(1)} %pad_maximum_fusion.refs_1_, bf16[128,1024]{1,0:T(8,128)(2,1)S(1)} %get-tuple-element.125.refs_2_, ...), custom_call_target="tpu_custom_call" | custom-call | flops 2500000 | bytes 8000 | tf_op jit(solution)/shard_map/pair_first/pallas_call | solution.py:184
  15.3 1.2 %copy-done.1 = f32[2,2,256,384]{3,2,1,0:T(8,128)} copy-done((f32[2,2,256,384]{3,2,1,0:T(8,128)}, f32[2,2,256,384]{3,2,1,0:T(8,128)S(1)}, u32[]{:S(2)}) %copy-start.1) | copy-done | bytes 1572888
  16.5 1.0 %collective-permute-done.1.refs_3_ = bf16[128,1024]{1,0:T(8,128)(2,1)} collective-permute-done((bf16[128,1024]{1,0:T(8,128)(2,1)S(1)}, bf16[128,1024]{1,0:T(8,128)(2,1)}, u32[]{:S(2)}, u32[]{:S(2)}) %collective-permute-start.1) | collective-permute-done | bytes 262176 | tf_op jit(solution)/shard_map/ppermute | solution.py:40
  17.5 0.5 collective-permute-start.4
  18.1 1.2 %collective-permute-done.3.refs_4_ = bf16[128,1024]{1,0:T(8,128)(2,1)S(1)} collective-permute-done((bf16[128,1024]{1,0:T(8,128)(2,1)}, bf16[128,1024]{1,0:T(8,128)(2,1)S(1)}, u32[]{:S(2)}, u32[]{:S(2)}) %collective-permute-start.3) | collective-permute-done | bytes 262176 | tf_op jit(solution)/shard_map/ppermute | solution.py:40
  19.3 0.7 copy-done.7
  20.0 0.7 copy-done.9
  20.7 0.9 %copy-done.8 = bf16[128,1024]{1,0:T(8,128)(2,1)S(1)} copy-done((bf16[128,1024]{1,0:T(8,128)(2,1)S(1)}, bf16[128,1024]{1,0:T(8,128)(2,1)}, u32[]{:S(2)}) %copy-start.8) | copy-done | bytes 262168
  21.6 0.9 %copy-done.10 = bf16[128,1024]{1,0:T(8,128)(2,1)S(1)} copy-done((bf16[128,1024]{1,0:T(8,128)(2,1)S(1)}, bf16[128,1024]{1,0:T(8,128)(2,1)}, u32[]{:S(2)}) %copy-start.10) | copy-done | bytes 262168
  22.6 5.4 %pair_last.1 = (bf16[8,64,512]{2,1,0:T(8,128)(2,1)S(1)}, f32[2,2,256,384]{3,2,1,0:T(8,128)S(1)}, bf16[2,256,384]{2,1,0:T(8,128)(2,1)S(1)}, bf16[128,384]{1,0:T(8...) custom-call(s32[1]{0:T(128)} %bitcast.2.refs_0_, ...), custom_call_target="tpu_custom_call" | custom-call | flops 2500000 | bytes 8000 | tf_op jit(solution)/shard_map/pair_last/pallas_call | solution.py:184
  28.0 1.1 %copy-done.3 = f32[2,2,256,384]{3,2,1,0:T(8,128)} copy-done((f32[2,2,256,384]{3,2,1,0:T(8,128)}, f32[2,2,256,384]{3,2,1,0:T(8,128)S(1)}, u32[]{:S(2)}) %copy-start.3) | copy-done | bytes 1572888
  29.4 1.8 %collective-permute-start.5 = (bf16[128,384]{1,0:T(8,128)(2,1)S(1)}, bf16[128,384]{1,0:T(8,128)(2,1)S(1)}, u32[]{:S(2)}, u32[]{:S(2)}) collective-permute-start(bf16[128,384]{1,0:T(8,128)(2,1)S(1)} %get-tuple-element.69.refs_0_), channel_id=1, source_target_pairs={{0,4},{4,0},{8,12},{12,8},{16,20},{20,16},{24,28},{28,24},{1,5},{5... | collective-permute-start | bytes 294920 | tf_op jit(solution)/shard_map/ppermute | solution.py:40
  31.5 1.7 %collective-permute-start.7 = (bf16[128,384]{1,0:T(8,128)(2,1)S(1)}, bf16[128,384]{1,0:T(8,128)(2,1)S(1)}, u32[]{:S(2)}, u32[]{:S(2)}) collective-permute-start(bf16[128,384]{1,0:T(8,128)(2,1)S(1)} %get-tuple-element.71.refs_2_), channel_id=1, source_target_pairs={{0,4},{4,0},{8,12},{12,8},{16,20},{20,16},{24,28},{28,24},{1,5},{5... | collective-permute-start | bytes 294920 | tf_op jit(solution)/shard_map/ppermute | solution.py:40
  33.5 1.8 %collective-permute-start.10 = (bf16[256,1024]{1,0:T(8,128)(2,1)}, bf16[256,1024]{1,0:T(8,128)(2,1)}, u32[]{:S(2)}, u32[]{:S(2)}) collective-permute-start(bf16[256,1024]{1,0:T(8,128)(2,1)} %refs_6_), channel_id=1, source_target_pairs={{0,2},{1,3},{2,0},{3,1},{4,6},{5,7},{6,4},{7,5},{8,10},{9,11},{10,... | collective-permute-start | bytes 1572872 | tf_op jit(solution)/shard_map/ppermute | solution.py:40
  35.5 1.6 %pack.1 = (bf16[8,64,512]{2,1,0:T(8,128)(2,1)}, bf16[2,64,512]{2,1,0:T(8,128)(2,1)S(1)}, bf16[2,64,512]{2,1,0:T(8,128)(2,1)S(1)}, bf16[2,64,512]{2,1,0:T(8,128)(2,1)S(1)}, bf16[2,64,512]{2,1,0:T(8,128)(2,1)S(1)}) custom-call(s32[16]{0:T(128)S(1)} %select_reduce_fusion.1.order_ref, bf16[8,64,512]{2,1,0:T(8,128)(2,1)S(1)} %get-tuple-element.74.refs_0_, ...), custom_call_target="tpu_custom_call" | custom-call | bytes 4000 | tf_op jit(solution)/shard_map/pack/pallas_call | solution.py:418
  37.0 0.6 copy-done.12
  37.7 0.6 copy-done.14
  38.3 0.7 copy-done.16
  39.2 1.4 %collective-permute-done.8.refs_7_ = bf16[128,384]{1,0:T(8,128)(2,1)S(1)} collective-permute-done((bf16[128,384]{1,0:T(8,128)(2,1)S(1)}, bf16[128,384]{1,0:T(8,128)(2,1)S(1)}, u32[]{:S(2)}, u32[]{:S(2)}) %collective-permute-start.8) | collective-permute-done | bytes 98336 | tf_op jit(solution)/shard_map/ppermute | solution.py:40
  41.0 3.7 %collective-permute-start.9 = (bf16[2,256,128]{2,1,0:T(8,128)(2,1)S(1)}, bf16[2,256,128]{2,1,0:T(8,128)(2,1)S(1)}, u32[]{:S(2)}, u32[]{:S(2)}) collective-permute-start(bf16[2,256,128]{2,1,0:T(8,128)(2,1)S(1)} %get-tuple-element.87.b_ref), channel_id=1, source_target_pairs={{0,8},{4,12},{8,16},{12,20},{16,24},{20,28},{1,9},{5,13},{9,17},{1... | collective-permute-start | bytes 393224 | tf_op jit(solution)/shard_map/ppermute | solution.py:563
  44.7 1.6 %collective-permute-start.12 = (bf16[8,64,512]{2,1,0:T(8,128)(2,1)}, bf16[8,64,512]{2,1,0:T(8,128)(2,1)}, u32[]{:S(2)}, u32[]{:S(2)}) collective-permute-start(bf16[8,64,512]{2,1,0:T(8,128)(2,1)} %get-tuple-element.98), channel_id=1, source_target_pairs={{0,4},{4,0},{8,12},{12,8},{16,20},{20,16},{24,28},{28,24},{1,5},{5... | collective-permute-start | bytes 1572872 | tf_op jit(solution)/shard_map/ppermute | solution.py:40
  46.3 1.4 %copy-done.4 = f32[2,2,256,384]{3,2,1,0:T(8,128)S(1)} copy-done((f32[2,2,256,384]{3,2,1,0:T(8,128)S(1)}, f32[2,2,256,384]{3,2,1,0:T(8,128)}, u32[]{:S(2)}) %copy-start.4) | copy-done | bytes 1572888
  47.7 1.0 %fold.1 = (bf16[4,2,256,256]{3,2,1,0:T(8,128)(2,1)S(1)}, f32[4,2,256,128]{3,2,1,0:T(8,128)S(1)}) custom-call(s32[1]{0:T(128)} %bitcast.2.refs_0_, s32[1]{0:T(128)} %bitcast.1.seq_ref.refs_1_, bf16[2,256,384]{2,1,0:T(8,128)(2,1)S(1)} %get-tuple-element.88.refs_2_, bf16[2,256,384]{2,1,0:T(8,128)(2,1)S(1)} %get-tuple-element.64.refs_10_.refs_3_, ...), custom_call_target="tpu_custom_call" | custom-call | flops 1200000 | bytes 6000 | tf_op jit(solution)/shard_map/fold/pallas_call | solution.py:295
  49.6 1.6 %collective-permute-start.21 = (bf16[2,64,512]{2,1,0:T(8,128)(2,1)S(1)}, bf16[2,64,512]{2,1,0:T(8,128)(2,1)S(1)}, u32[]{:S(2)}, u32[]{:S(2)}) collective-permute-start(bf16[2,64,512]{2,1,0:T(8,128)(2,1)S(1)} %copy-done.17), channel_id=1, source_target_pairs={{0,8},{4,12},{8,0},{12,4},{16,24},{20,28},{24,16},{28,20},{1,9},{5... | collective-permute-start | bytes 393224 | tf_op jit(solution)/shard_map/ppermute | solution.py:40
  51.4 2.5 %collective-permute-start.11 = (bf16[2,256,128]{2,1,0:T(8,128)(2,1)S(1)}, bf16[2,256,128]{2,1,0:T(8,128)(2,1)S(1)}, u32[]{:S(2)}, u32[]{:S(2)}) collective-permute-start(bf16[2,256,128]{2,1,0:T(8,128)(2,1)S(1)} %step.1), channel_id=1, source_target_pairs={{0,8},{4,12},{8,16},{12,20},{16,24},{20,28},{1,9},{5,13},{9,17},{1... | collective-permute-start | bytes 393224 | tf_op jit(solution)/shard_map/ppermute | solution.py:563
  54.0 4.0 %collective-permute-done.12 = bf16[8,64,512]{2,1,0:T(8,128)(2,1)} collective-permute-done((bf16[8,64,512]{2,1,0:T(8,128)(2,1)}, bf16[8,64,512]{2,1,0:T(8,128)(2,1)}, u32[]{:S(2)}, u32[]{:S(2)}) %collective-permute-start.12) | collective-permute-done | bytes 524320 | tf_op jit(solution)/shard_map/ppermute | solution.py:40
  58.0 0.5 recall.1
  58.6 0.6 copy-done.11
  59.2 1.5 %collective-permute-start.14 = (bf16[256,256]{1,0:T(8,128)(2,1)S(1)}, bf16[256,256]{1,0:T(8,128)(2,1)S(1)}, u32[]{:S(2)}, u32[]{:S(2)}) collective-permute-start(bf16[256,256]{1,0:T(8,128)(2,1)S(1)} %get-tuple-element.102), channel_id=1, source_target_pairs={{0,2},{1,3},{2,0},{3,1},{4,6},{5,7},{6,4},{7,5},{8,10},{9,11},{10,... | collective-permute-start | bytes 393224 | tf_op jit(solution)/shard_map/ppermute | solution.py:40
  61.1 1.8 %fusion.10 = (bf16[2,64,512]{2,1,0:T(8,128)(2,1)S(1)}, bf16[2,64,512]{2,1,0:T(8,128)(2,1)S(1)}, bf16[2,64,512]{2,1,0:T(8,128)(2,1)S(1)}, bf16[2,64,512]{2,1,0:T(8,128)(2,1)}) fusion(bf16[8,64,512]{2,1,0:T(8,128)(2,1)} %collective-permute-done.12), kind=kLoop, calls=%fused_computation.39 | loop fusion | bytes 1048576 | tf_op jit(solution)/shard_map/slice | solution.py:572
  62.9 2.7 %collective-permute-start.22 = (bf16[2,64,512]{2,1,0:T(8,128)(2,1)S(1)}, bf16[2,64,512]{2,1,0:T(8,128)(2,1)S(1)}, u32[]{:S(2)}, u32[]{:S(2)}) collective-permute-start(bf16[2,64,512]{2,1,0:T(8,128)(2,1)S(1)} %copy-done.15), channel_id=1, source_target_pairs={{0,16},{4,20},{8,24},{12,28},{16,0},{20,4},{24,8},{28,12},{1,17},{... | collective-permute-start | bytes 393224 | tf_op jit(solution)/shard_map/ppermute | solution.py:40
  65.6 2.9 %collective-permute-start.23 = (bf16[2,64,512]{2,1,0:T(8,128)(2,1)S(1)}, bf16[2,64,512]{2,1,0:T(8,128)(2,1)S(1)}, u32[]{:S(2)}, u32[]{:S(2)}) collective-permute-start(bf16[2,64,512]{2,1,0:T(8,128)(2,1)S(1)} %get-tuple-element.110), channel_id=1, source_target_pairs={{0,24},{4,28},{8,16},{12,20},{16,8},{20,12},{24,0},{28,4},{1,25},{... | collective-permute-start | bytes 393224 | tf_op jit(solution)/shard_map/ppermute | solution.py:40
  68.5 0.6 collective-permute-start.18
  69.1 2.0 %collective-permute-start.19 = (bf16[2,64,512]{2,1,0:T(8,128)(2,1)S(1)}, bf16[2,64,512]{2,1,0:T(8,128)(2,1)S(1)}, u32[]{:S(2)}, u32[]{:S(2)}) collective-permute-start(bf16[2,64,512]{2,1,0:T(8,128)(2,1)S(1)} %get-tuple-element.121), channel_id=1, source_target_pairs={{0,16},{4,20},{8,24},{12,28},{16,0},{20,4},{24,8},{28,12},{1,17},{... | collective-permute-start | bytes 393224 | tf_op jit(solution)/shard_map/ppermute | solution.py:40
  71.1 1.8 %collective-permute-start.20 = (bf16[2,64,512]{2,1,0:T(8,128)(2,1)S(1)}, bf16[2,64,512]{2,1,0:T(8,128)(2,1)S(1)}, u32[]{:S(2)}, u32[]{:S(2)}) collective-permute-start(bf16[2,64,512]{2,1,0:T(8,128)(2,1)S(1)} %get-tuple-element.120), channel_id=1, source_target_pairs={{0,24},{4,28},{8,16},{12,20},{16,8},{20,12},{24,0},{28,4},{1,25},{... | collective-permute-start | bytes 393224 | tf_op jit(solution)/shard_map/ppermute | solution.py:40
  73.0 0.7 select_reduce_fusion.rows_ref
  73.7 10.5 %ffn.1 = bf16[256,1024]{1,0:T(8,128)(2,1)} custom-call(bf16[256,1024]{1,0:T(8,128)(2,1)} %refs_0_.1, f32[1,1024]{1,0:T(1,128)} %bitcast.28, bf16[256,256]{1,0:T(8,128)(2,1)} %copy-done.11, bf16[256,256]{1,0:T(8,128)(2,1)} %copy-done.20, bf16[256,256]{1,0:T(8,128)(2,1)} %copy-done.21, bf16[256,256]{1,0:T(8,128)(2,1)} %copy-done.22, bf16[256,1024]{1,0:T(8,128)(2,1)} %refs_6_, ...), custom_call_target="tpu_custom_call" | custom-call | flops 5000000 | bytes 22000 | tf_op jit(solution)/shard_map/ffn/pallas_call | solution.py:376
  84.3 2.8 %collective-permute-done.19.refs_2_ = bf16[2,64,512]{2,1,0:T(8,128)(2,1)S(1)} collective-permute-done((bf16[2,64,512]{2,1,0:T(8,128)(2,1)S(1)}, bf16[2,64,512]{2,1,0:T(8,128)(2,1)S(1)}, u32[]{:S(2)}, u32[]{:S(2)}) %collective-permute-start.19) | collective-permute-done | bytes 131104 | tf_op jit(solution)/shard_map/ppermute | solution.py:40
  87.1 0.6 copy-done.27
  87.8 2.8 %place.1 = bf16[16,64,512]{2,1,0:T(8,128)(2,1)} custom-call(s32[16]{0:T(128)} %select_reduce_fusion.rows_ref, bf16[2,64,512]{2,1,0:T(8,128)(2,1)} %get-tuple-element.112.refs_0_, bf16[2,64,512]{2,1,0:T(8,128)(2,1)} %copy-done.26, bf16[2,64,512]{2,1,0:T(8,128)(2,1)} %copy-done.27, bf16[2,64,512]{2,1,0:T(8,128)(2,1)} %copy-done.28, ...), custom_call_target="tpu_custom_call" | custom-call | bytes 2097 | tf_op jit(solution)/shard_map/place/pallas_call | solution.py:455
  (99 shorter events, 4.2 us)
Async XLA Ops:
  0.6 8.1 %copy-start = (bf16[16,256]{1,0:T(8,128)(2,1)S(1)}, bf16[16,256]{1,0:T(8,128)(2,1)}, u32[]{:S(2)}) copy-start(bf16[16,256]{1,0:T(8,128)(2,1)} %param.20) | copy-start | bytes 24580
  0.6 8.4 %collective-permute-start.2 = (bf16[256,1024]{1,0:T(8,128)(2,1)}, bf16[256,1024]{1,0:T(8,128)(2,1)S(1)}, u32[]{:S(2)}, u32[]{:S(2)}) collective-permute-start(bf16[256,1024]{1,0:T(8,128)(2,1)} %refs_0_.1), channel_id=1, source_target_pairs={{0,1},{1,0},{2,3},{3,2},{4,5},{5,4},{6,7},{7,6},{8,9},{9,8},{10,11... | collective-permute-start | bytes 1572872 | tf_op jit(solution)/shard_map/ppermute | solution.py:40
  2.2 14.3 %collective-permute-start = (bf16[128,1024]{1,0:T(8,128)(2,1)S(1)}, bf16[128,1024]{1,0:T(8,128)(2,1)}, u32[]{:S(2)}, u32[]{:S(2)}) collective-permute-start(bf16[128,1024]{1,0:T(8,128)(2,1)S(1)} %get-tuple-element.125.refs_2_), channel_id=1, source_target_pairs={{0,2},{1,3},{2,0},{3,1},{4,6},{5,7},{6,4},{7,5},{8,10},{9,11},{10,... | collective-permute-start | bytes 786440 | tf_op jit(solution)/shard_map/ppermute | solution.py:40
  4.8 12.7 %collective-permute-start.1 = (bf16[128,1024]{1,0:T(8,128)(2,1)S(1)}, bf16[128,1024]{1,0:T(8,128)(2,1)}, u32[]{:S(2)}, u32[]{:S(2)}) collective-permute-start(bf16[128,1024]{1,0:T(8,128)(2,1)S(1)} %get-tuple-element.124.refs_3_), channel_id=1, source_target_pairs={{0,2},{1,3},{2,0},{3,1},{4,6},{5,7},{6,4},{7,5},{8,10},{9,11},{10,... | collective-permute-start | bytes 786440 | tf_op jit(solution)/shard_map/ppermute | solution.py:40
  6.8 1.8 %copy-start.30 = (bf16[2,3,128]{2,0,1:T(2,128)(2,1)S(1)}, bf16[2,3,128]{2,0,1:T(2,128)(2,1)}, u32[]{:S(2)}) copy-start(bf16[2,3,128]{2,0,1:T(2,128)(2,1)} %param.18) | copy-start | bytes 4612
  6.8 2.0 %copy-start.29 = (bf16[16,256]{1,0:T(8,128)(2,1)S(1)}, bf16[16,256]{1,0:T(8,128)(2,1)}, u32[]{:S(2)}) copy-start(bf16[16,256]{1,0:T(8,128)(2,1)} %param.19) | copy-start | bytes 24580
  6.8 3.0 %copy-start.13 = (f32[1024]{0:T(1024)S(1)}, f32[1024]{0:T(1024)}, u32[]{:S(2)}) copy-start(f32[1024]{0:T(1024)} %param.16) | copy-start | bytes 12292
  9.0 0.8 copy-start.5
  9.8 1.0 %copy-start.6 = (bf16[256,1024]{1,0:T(8,128)(2,1)S(1)}, bf16[256,1024]{1,0:T(8,128)(2,1)}, u32[]{:S(2)}) copy-start(bf16[256,1024]{1,0:T(8,128)(2,1)} %copy-done.5) | copy-start | bytes 1572868
  15.3 1.2 %copy-start.1 = (f32[2,2,256,384]{3,2,1,0:T(8,128)}, f32[2,2,256,384]{3,2,1,0:T(8,128)S(1)}, u32[]{:S(2)}) copy-start(f32[2,2,256,384]{3,2,1,0:T(8,128)S(1)} %get-tuple-element.90.refs_5_) | copy-start | bytes 4718596
  17.5 1.7 %collective-permute-start.3 = (bf16[128,1024]{1,0:T(8,128)(2,1)}, bf16[128,1024]{1,0:T(8,128)(2,1)S(1)}, u32[]{:S(2)}, u32[]{:S(2)}) collective-permute-start(bf16[128,1024]{1,0:T(8,128)(2,1)} %collective-permute-done.refs_2_), channel_id=1, source_target_pairs={{0,1},{1,0},{2,3},{3,2},{4,5},{5,4},{6,7},{7,6},{8,9},{9,8},{10,11... | collective-permute-start | bytes 786440 | tf_op jit(solution)/shard_map/ppermute | solution.py:40
  17.5 2.4 %collective-permute-start.4 = (bf16[128,1024]{1,0:T(8,128)(2,1)}, bf16[128,1024]{1,0:T(8,128)(2,1)S(1)}, u32[]{:S(2)}, u32[]{:S(2)}) collective-permute-start(bf16[128,1024]{1,0:T(8,128)(2,1)} %collective-permute-done.1.refs_3_), channel_id=1, source_target_pairs={{0,1},{1,0},{2,3},{3,2},{4,5},{5,4},{6,7},{7,6},{8,9},{9,8},{10,11... | collective-permute-start | bytes 786440 | tf_op jit(solution)/shard_map/ppermute | solution.py:40
  18.0 11.1 %copy-start.31 = (s32[128]{0:T(128)S(1)}, s32[128]{0:T(128)}, u32[]{:S(2)}) copy-start(s32[128]{0:T(128)} %param.29) | copy-start | bytes 1540
  20.7 0.9 %copy-start.8 = (bf16[128,1024]{1,0:T(8,128)(2,1)S(1)}, bf16[128,1024]{1,0:T(8,128)(2,1)}, u32[]{:S(2)}) copy-start(bf16[128,1024]{1,0:T(8,128)(2,1)} %copy-done.7) | copy-start | bytes 786436
  21.6 0.9 %copy-start.10 = (bf16[128,1024]{1,0:T(8,128)(2,1)S(1)}, bf16[128,1024]{1,0:T(8,128)(2,1)}, u32[]{:S(2)}) copy-start(bf16[128,1024]{1,0:T(8,128)(2,1)} %copy-done.9) | copy-start | bytes 786436
  28.0 1.1 %copy-start.3 = (f32[2,2,256,384]{3,2,1,0:T(8,128)}, f32[2,2,256,384]{3,2,1,0:T(8,128)S(1)}, u32[]{:S(2)}) copy-start(f32[2,2,256,384]{3,2,1,0:T(8,128)S(1)} %get-tuple-element.91.refs_6_) | copy-start | bytes 4718596
  29.1 17.2 %copy-start.2 = (f32[2,2,256,384]{3,2,1,0:T(8,128)S(1)}, f32[2,2,256,384]{3,2,1,0:T(8,128)}, u32[]{:S(2)}) copy-start(f32[2,2,256,384]{3,2,1,0:T(8,128)} %copy-done.1) | copy-start | bytes 4718596
  29.4 9.6 %collective-permute-start.5 = (bf16[128,384]{1,0:T(8,128)(2,1)S(1)}, bf16[128,384]{1,0:T(8,128)(2,1)S(1)}, u32[]{:S(2)}, u32[]{:S(2)}) collective-permute-start(bf16[128,384]{1,0:T(8,128)(2,1)S(1)} %get-tuple-element.69.refs_0_), channel_id=1, source_target_pairs={{0,4},{4,0},{8,12},{12,8},{16,20},{20,16},{24,28},{28,24},{1,5},{5... | collective-permute-start | bytes 294920 | tf_op jit(solution)/shard_map/ppermute | solution.py:40
  31.2 7.9 %collective-permute-start.6 = (bf16[128,384]{1,0:T(8,128)(2,1)S(1)}, bf16[128,384]{1,0:T(8,128)(2,1)S(1)}, u32[]{:S(2)}, u32[]{:S(2)}) collective-permute-start(bf16[128,384]{1,0:T(8,128)(2,1)S(1)} %get-tuple-element.70.refs_1_), channel_id=1, source_target_pairs={{0,4},{4,0},{8,12},{12,8},{16,20},{20,16},{24,28},{28,24},{1,5},{5... | collective-permute-start | bytes 294920 | tf_op jit(solution)/shard_map/ppermute | solution.py:40
  31.5 7.8 %collective-permute-start.7 = (bf16[128,384]{1,0:T(8,128)(2,1)S(1)}, bf16[128,384]{1,0:T(8,128)(2,1)S(1)}, u32[]{:S(2)}, u32[]{:S(2)}) collective-permute-start(bf16[128,384]{1,0:T(8,128)(2,1)S(1)} %get-tuple-element.71.refs_2_), channel_id=1, source_target_pairs={{0,4},{4,0},{8,12},{12,8},{16,20},{20,16},{24,28},{28,24},{1,5},{5... | collective-permute-start | bytes 294920 | tf_op jit(solution)/shard_map/ppermute | solution.py:40
  33.2 7.4 %collective-permute-start.8 = (bf16[128,384]{1,0:T(8,128)(2,1)S(1)}, bf16[128,384]{1,0:T(8,128)(2,1)S(1)}, u32[]{:S(2)}, u32[]{:S(2)}) collective-permute-start(bf16[128,384]{1,0:T(8,128)(2,1)S(1)} %get-tuple-element.72.refs_3_), channel_id=1, source_target_pairs={{0,4},{4,0},{8,12},{12,8},{16,20},{20,16},{24,28},{28,24},{1,5},{5... | collective-permute-start | bytes 294920 | tf_op jit(solution)/shard_map/ppermute | solution.py:40
  33.5 15.3 %collective-permute-start.10 = (bf16[256,1024]{1,0:T(8,128)(2,1)}, bf16[256,1024]{1,0:T(8,128)(2,1)}, u32[]{:S(2)}, u32[]{:S(2)}) collective-permute-start(bf16[256,1024]{1,0:T(8,128)(2,1)} %refs_6_), channel_id=1, source_target_pairs={{0,2},{1,3},{2,0},{3,1},{4,6},{5,7},{6,4},{7,5},{8,10},{9,11},{10,... | collective-permute-start | bytes 1572872 | tf_op jit(solution)/shard_map/ppermute | solution.py:40
  41.0 7.8 %collective-permute-start.9 = (bf16[2,256,128]{2,1,0:T(8,128)(2,1)S(1)}, bf16[2,256,128]{2,1,0:T(8,128)(2,1)S(1)}, u32[]{:S(2)}, u32[]{:S(2)}) collective-permute-start(bf16[2,256,128]{2,1,0:T(8,128)(2,1)S(1)} %get-tuple-element.87.b_ref), channel_id=1, source_target_pairs={{0,8},{4,12},{8,16},{12,20},{16,24},{20,28},{1,9},{5,13},{9,17},{1... | collective-permute-start | bytes 393224 | tf_op jit(solution)/shard_map/ppermute | solution.py:563
  44.7 13.3 %collective-permute-start.12 = (bf16[8,64,512]{2,1,0:T(8,128)(2,1)}, bf16[8,64,512]{2,1,0:T(8,128)(2,1)}, u32[]{:S(2)}, u32[]{:S(2)}) collective-permute-start(bf16[8,64,512]{2,1,0:T(8,128)(2,1)} %get-tuple-element.98), channel_id=1, source_target_pairs={{0,4},{4,0},{8,12},{12,8},{16,20},{20,16},{24,28},{28,24},{1,5},{5... | collective-permute-start | bytes 1572872 | tf_op jit(solution)/shard_map/ppermute | solution.py:40
  46.3 1.4 %copy-start.4 = (f32[2,2,256,384]{3,2,1,0:T(8,128)S(1)}, f32[2,2,256,384]{3,2,1,0:T(8,128)}, u32[]{:S(2)}) copy-start(f32[2,2,256,384]{3,2,1,0:T(8,128)} %copy-done.3) | copy-start | bytes 4718596
  47.7 1.8 %copy-start.17 = (bf16[2,64,512]{2,1,0:T(8,128)(2,1)S(1)}, bf16[2,64,512]{2,1,0:T(8,128)(2,1)}, u32[]{:S(2)}) copy-start(bf16[2,64,512]{2,1,0:T(8,128)(2,1)} %copy-done.16) | copy-start | bytes 393220
  48.8 20.4 %collective-permute-start.16 = (bf16[256,1024]{1,0:T(8,128)(2,1)}, bf16[256,1024]{1,0:T(8,128)(2,1)S(1)}, u32[]{:S(2)}, u32[]{:S(2)}) collective-permute-start(bf16[256,1024]{1,0:T(8,128)(2,1)} %refs_6_), channel_id=1, source_target_pairs={{0,1},{1,0},{2,3},{3,2},{4,5},{5,4},{6,7},{7,6},{8,9},{9,8},{10,11... | collective-permute-start | bytes 1572872 | tf_op jit(solution)/shard_map/ppermute | solution.py:40
  48.8 22.3 %collective-permute-start.17 = (bf16[256,1024]{1,0:T(8,128)(2,1)}, bf16[256,1024]{1,0:T(8,128)(2,1)S(1)}, u32[]{:S(2)}, u32[]{:S(2)}) collective-permute-start(bf16[256,1024]{1,0:T(8,128)(2,1)} %collective-permute-done.10.refs_8_), channel_id=1, source_target_pairs={{0,1},{1,0},{2,3},{3,2},{4,5},{5,4},{6,7},{7,6},{8,9},{9,8},{10,11... | collective-permute-start | bytes 1572872 | tf_op jit(solution)/shard_map/ppermute | solution.py:40
  49.6 11.2 %collective-permute-start.21 = (bf16[2,64,512]{2,1,0:T(8,128)(2,1)S(1)}, bf16[2,64,512]{2,1,0:T(8,128)(2,1)S(1)}, u32[]{:S(2)}, u32[]{:S(2)}) collective-permute-start(bf16[2,64,512]{2,1,0:T(8,128)(2,1)S(1)} %copy-done.17), channel_id=1, source_target_pairs={{0,8},{4,12},{8,0},{12,4},{16,24},{20,28},{24,16},{28,20},{1,9},{5... | collective-permute-start | bytes 393224 | tf_op jit(solution)/shard_map/ppermute | solution.py:40
  51.4 6.6 %collective-permute-start.11 = (bf16[2,256,128]{2,1,0:T(8,128)(2,1)S(1)}, bf16[2,256,128]{2,1,0:T(8,128)(2,1)S(1)}, u32[]{:S(2)}, u32[]{:S(2)}) collective-permute-start(bf16[2,256,128]{2,1,0:T(8,128)(2,1)S(1)} %step.1), channel_id=1, source_target_pairs={{0,8},{4,12},{8,16},{12,20},{16,24},{20,28},{1,9},{5,13},{9,17},{1... | collective-permute-start | bytes 393224 | tf_op jit(solution)/shard_map/ppermute | solution.py:563
  58.0 4.9 %copy-start.15 = (bf16[2,64,512]{2,1,0:T(8,128)(2,1)S(1)}, bf16[2,64,512]{2,1,0:T(8,128)(2,1)}, u32[]{:S(2)}) copy-start(bf16[2,64,512]{2,1,0:T(8,128)(2,1)} %copy-done.14) | copy-start | bytes 393220
  59.2 3.7 %collective-permute-start.13 = (bf16[256,256]{1,0:T(8,128)(2,1)S(1)}, bf16[256,256]{1,0:T(8,128)(2,1)S(1)}, u32[]{:S(2)}, u32[]{:S(2)}) collective-permute-start(bf16[256,256]{1,0:T(8,128)(2,1)S(1)} %get-tuple-element.101), channel_id=1, source_target_pairs={{0,1},{1,0},{2,3},{3,2},{4,5},{5,4},{6,7},{7,6},{8,9},{9,8},{10,11... | collective-permute-start | bytes 393224 | tf_op jit(solution)/shard_map/ppermute | solution.py:40
  59.2 6.3 %collective-permute-start.14 = (bf16[256,256]{1,0:T(8,128)(2,1)S(1)}, bf16[256,256]{1,0:T(8,128)(2,1)S(1)}, u32[]{:S(2)}, u32[]{:S(2)}) collective-permute-start(bf16[256,256]{1,0:T(8,128)(2,1)S(1)} %get-tuple-element.102), channel_id=1, source_target_pairs={{0,2},{1,3},{2,0},{3,1},{4,6},{5,7},{6,4},{7,5},{8,10},{9,11},{10,... | collective-permute-start | bytes 393224 | tf_op jit(solution)/shard_map/ppermute | solution.py:40
  60.7 23.5 %copy-start.23 = (bf16[2,64,512]{2,1,0:T(8,128)(2,1)}, bf16[2,64,512]{2,1,0:T(8,128)(2,1)S(1)}, u32[]{:S(2)}) copy-start(bf16[2,64,512]{2,1,0:T(8,128)(2,1)S(1)} %collective-permute-done.21.refs_5_) | copy-start | bytes 393220
  60.7 7.8 %collective-permute-start.15 = (bf16[256,256]{1,0:T(8,128)(2,1)S(1)}, bf16[256,256]{1,0:T(8,128)(2,1)S(1)}, u32[]{:S(2)}, u32[]{:S(2)}) collective-permute-start(bf16[256,256]{1,0:T(8,128)(2,1)S(1)} %get-tuple-element.103), channel_id=1, source_target_pairs={{0,3},{1,2},{2,1},{3,0},{4,7},{5,6},{6,5},{7,4},{8,11},{9,10},{10,... | collective-permute-start | bytes 393224 | tf_op jit(solution)/shard_map/ppermute | solution.py:40
  62.9 10.8 %copy-start.20 = (bf16[256,256]{1,0:T(8,128)(2,1)}, bf16[256,256]{1,0:T(8,128)(2,1)S(1)}, u32[]{:S(2)}) copy-start(bf16[256,256]{1,0:T(8,128)(2,1)S(1)} %collective-permute-done.13.refs_3_) | copy-start | bytes 393220
  62.9 21.4 %collective-permute-start.22 = (bf16[2,64,512]{2,1,0:T(8,128)(2,1)S(1)}, bf16[2,64,512]{2,1,0:T(8,128)(2,1)S(1)}, u32[]{:S(2)}, u32[]{:S(2)}) collective-permute-start(bf16[2,64,512]{2,1,0:T(8,128)(2,1)S(1)} %copy-done.15), channel_id=1, source_target_pairs={{0,16},{4,20},{8,24},{12,28},{16,0},{20,4},{24,8},{28,12},{1,17},{... | collective-permute-start | bytes 393224 | tf_op jit(solution)/shard_map/ppermute | solution.py:40
  65.6 8.1 %copy-start.21 = (bf16[256,256]{1,0:T(8,128)(2,1)}, bf16[256,256]{1,0:T(8,128)(2,1)S(1)}, u32[]{:S(2)}) copy-start(bf16[256,256]{1,0:T(8,128)(2,1)S(1)} %collective-permute-done.14.refs_4_) | copy-start | bytes 393220
  65.6 18.7 %collective-permute-start.23 = (bf16[2,64,512]{2,1,0:T(8,128)(2,1)S(1)}, bf16[2,64,512]{2,1,0:T(8,128)(2,1)S(1)}, u32[]{:S(2)}, u32[]{:S(2)}) collective-permute-start(bf16[2,64,512]{2,1,0:T(8,128)(2,1)S(1)} %get-tuple-element.110), channel_id=1, source_target_pairs={{0,24},{4,28},{8,16},{12,20},{16,8},{20,12},{24,0},{28,4},{1,25},{... | collective-permute-start | bytes 393224 | tf_op jit(solution)/shard_map/ppermute | solution.py:40
  68.5 5.2 %copy-start.22 = (bf16[256,256]{1,0:T(8,128)(2,1)}, bf16[256,256]{1,0:T(8,128)(2,1)S(1)}, u32[]{:S(2)}) copy-start(bf16[256,256]{1,0:T(8,128)(2,1)S(1)} %collective-permute-done.15.refs_5_) | copy-start | bytes 393220
  68.5 15.8 %collective-permute-start.18 = (bf16[2,64,512]{2,1,0:T(8,128)(2,1)S(1)}, bf16[2,64,512]{2,1,0:T(8,128)(2,1)S(1)}, u32[]{:S(2)}, u32[]{:S(2)}) collective-permute-start(bf16[2,64,512]{2,1,0:T(8,128)(2,1)S(1)} %get-tuple-element.122), channel_id=1, source_target_pairs={{0,8},{4,12},{8,0},{12,4},{16,24},{20,28},{24,16},{28,20},{1,9},{5... | collective-permute-start | bytes 393224 | tf_op jit(solution)/shard_map/ppermute | solution.py:40
  69.1 4.6 %copy-start.18 = (bf16[256,1024]{1,0:T(8,128)(2,1)}, bf16[256,1024]{1,0:T(8,128)(2,1)S(1)}, u32[]{:S(2)}) copy-start(bf16[256,1024]{1,0:T(8,128)(2,1)S(1)} %collective-permute-done.16.refs_7_) | copy-start | bytes 1572868
  69.1 18.0 %collective-permute-start.19 = (bf16[2,64,512]{2,1,0:T(8,128)(2,1)S(1)}, bf16[2,64,512]{2,1,0:T(8,128)(2,1)S(1)}, u32[]{:S(2)}, u32[]{:S(2)}) collective-permute-start(bf16[2,64,512]{2,1,0:T(8,128)(2,1)S(1)} %get-tuple-element.121), channel_id=1, source_target_pairs={{0,16},{4,20},{8,24},{12,28},{16,0},{20,4},{24,8},{28,12},{1,17},{... | collective-permute-start | bytes 393224 | tf_op jit(solution)/shard_map/ppermute | solution.py:40
  71.1 2.6 %copy-start.19 = (bf16[256,1024]{1,0:T(8,128)(2,1)}, bf16[256,1024]{1,0:T(8,128)(2,1)S(1)}, u32[]{:S(2)}) copy-start(bf16[256,1024]{1,0:T(8,128)(2,1)S(1)} %collective-permute-done.17.refs_9_) | copy-start | bytes 1572868
  71.1 16.0 %collective-permute-start.20 = (bf16[2,64,512]{2,1,0:T(8,128)(2,1)S(1)}, bf16[2,64,512]{2,1,0:T(8,128)(2,1)S(1)}, u32[]{:S(2)}, u32[]{:S(2)}) collective-permute-start(bf16[2,64,512]{2,1,0:T(8,128)(2,1)S(1)} %get-tuple-element.120), channel_id=1, source_target_pairs={{0,24},{4,28},{8,16},{12,20},{16,8},{20,12},{24,0},{28,4},{1,25},{... | collective-permute-start | bytes 393224 | tf_op jit(solution)/shard_map/ppermute | solution.py:40
  84.3 2.8 %copy-start.24 = (bf16[2,64,512]{2,1,0:T(8,128)(2,1)}, bf16[2,64,512]{2,1,0:T(8,128)(2,1)S(1)}, u32[]{:S(2)}) copy-start(bf16[2,64,512]{2,1,0:T(8,128)(2,1)S(1)} %collective-permute-done.22.refs_6_) | copy-start | bytes 393220
  84.3 2.8 %copy-start.25 = (bf16[2,64,512]{2,1,0:T(8,128)(2,1)}, bf16[2,64,512]{2,1,0:T(8,128)(2,1)S(1)}, u32[]{:S(2)}) copy-start(bf16[2,64,512]{2,1,0:T(8,128)(2,1)S(1)} %collective-permute-done.23.refs_7_) | copy-start | bytes 393220
  84.3 2.8 %copy-start.26 = (bf16[2,64,512]{2,1,0:T(8,128)(2,1)}, bf16[2,64,512]{2,1,0:T(8,128)(2,1)S(1)}, u32[]{:S(2)}) copy-start(bf16[2,64,512]{2,1,0:T(8,128)(2,1)S(1)} %collective-permute-done.18.refs_1_) | copy-start | bytes 393220
  (8 other events, 5.4 us)
where the time goes:
time: 91.5 us; the launch traced here: 90.8 us
  starting transfers between devices  31.4 us (34%)
  Pallas kernels  26.8 us (29%)
  local copies, waits for them, and re-layouts  18.1 us (20%)
  waiting for transfers between devices  10.6 us (12%)
  other arithmetic  2.43 us (3%)
  between operations  1.17 us (1%)
    ppermute x22, starting transfers between devices, exchange(): return lax.ppermute(value, axis, [(i, i ^ bit) for i in range(count)])  25.2 us
    unnamed x65, local copies, waits for them, and re-layouts  14 us
    ppermute x22, waiting for transfers between devices, exchange(): return lax.ppermute(value, axis, [(i, i ^ bit) for i in range(count)])  10.6 us
    pallas_call x1, Pallas kernels, ffn(): pl.pallas_call(functools.partial(ffn_kernel, shards, tile), out_shape=jax...  10.5 us
    pallas_call x2, Pallas kernels, pair_call(): pl.pallas_call(functools.partial(pair_kernel, heads, d, blocks, rel, is_l...  9.84 us
    ppermute x2, starting transfers between devices, per_device(): state = lax.ppermute(state, 'seq', onward)  6.25 us
    pallas_call x1, Pallas kernels, place(): pl.pallas_call(place_kernel, out_shape=jax.ShapeDtypeStruct(shape, source...  2.82 us
  transfers between devices with their start and end apart: 24, of which 6 were waited for; matrix products, arithmetic and copies ran while one was open for 9% of the time, Pallas kernels for 21%

commit v1 on v0

v1 whole, which is shorter than its diff:
```python
import functools

import jax
import jax.numpy as jnp
from jax import lax
from jax.experimental import pallas as pl
from jax.experimental.pallas import tpu as pltpu
from jax.sharding import PartitionSpec as P

PERS = 16
PER_OWNER = 2
SPAN = 64
EPS = 1e-05
TINY = 1e-06
BF = jnp.bfloat16
F32 = jnp.float32
SCALE = 0.001
VMEM_LIMIT = 12 * 1024 * 1024
MOST_VMEM = 60 * 1024 * 1024
STORE_BYTES = 56 * 1024 * 1024
CUTS = 1


def dot(a, b):
    return jnp.dot(a, b, preferred_element_type=F32)


def vmem():
    return pl.BlockSpec(memory_space=pltpu.VMEM)


def smem():
    return pl.BlockSpec(memory_space=pltpu.SMEM)


def loaded(shape):
    return pl.BlockSpec(shape, lambda i: (0,) * len(shape))


def exchange(value, axis, bit):
    count = lax.axis_size(axis)
    return lax.ppermute(value, axis, [(i, i ^ bit) for i in range(count)])


def params(limit=VMEM_LIMIT):
    return pltpu.CompilerParams(vmem_limit_bytes=limit)


def cost(flops, size):
    return pl.CostEstimate(flops=int(flops * SCALE), bytes_accessed=int(size * SCALE), transcendentals=0)


def compose(later, earlier):
    d = later.shape[0] // 2
    joined = dot(later[:, : 2 * d].astype(BF), earlier.astype(BF))
    shift = joined[:, 2 * d :] + later[:, 2 * d :].astype(F32)
    return jnp.concatenate([joined[:, : 2 * d], shift], axis=1)


def ordered(flag, one, other):
    swap = flag != 0
    return jnp.where(swap, other, one), jnp.where(swap, one, other)


def rms_plain(values):
    return values * lax.rsqrt(jnp.mean(values * values, axis=-1, keepdims=True) + TINY)


def pair_kernel(heads, d, blocks, rel, is_last, groups, parts, packs, *refs):
    refs = list(refs)
    meta_ref, flat_ref, slot_ref = refs[:3]
    refs = refs[3:]
    x_refs = [refs[: parts[0]], refs[parts[0] : sum(parts)]]
    refs = refs[sum(parts) :]
    gain_ref, w_ref, gates_ref, start_ref = refs[:4]
    others = refs[4 : 4 + groups - 1] if is_last else []
    kv_before = refs[4 + len(others) : 4 + 2 * len(others)]
    outs = refs[4 + 2 * len(others) + (rel > 0) :]
    store_ref, group_ref = outs[:2]
    kv_outs = outs[2 : 2 + packs]
    total_refs = outs[2 + packs : -3]
    kv_ref, r_ref, sem = outs[-3:]
    bias = flat_ref.shape[0] - 2 * heads
    me = meta_ref[0]
    if rel == 0:
        table_ref, (slot_out,) = slot_ref, total_refs
        here, total_blocks = meta_ref[1], slot_out.shape[0]
        owners = [lax.div(table_ref[here * total_blocks + c], total_blocks) for c in range(total_blocks)]
        for c, owner in enumerate(owners):
            rank = sum([jnp.where(owners[e] == owner, 1, 0) for e in range(c)], jnp.int32(0))
            place = lax.shift_right_logical(owner, 1) ^ lax.shift_right_logical(here, 1)
            cross = (owner & 1) ^ (here & 1)
            slot_out[c] = (1 - cross) * (total_blocks // 2) + place * PER_OWNER + rank
    if is_last:
        for g, source in enumerate(kv_before):
            for i in range(2 * blocks):
                kv_ref[slot_ref[(me ^ (2 * g + i // blocks)) * blocks + i % blocks]] = source[i]
    gain = gain_ref[...]
    w = w_ref[...]
    kept = {}
    for s in range(2):
        x = jnp.concatenate([ref[...] for ref in x_refs[s]], axis=0).astype(F32)
        scale = lax.rsqrt(jnp.mean(x * x, axis=-1, keepdims=True) + EPS)
        projected = dot((x * scale * gain).astype(BF), w)
        base = (me ^ (rel + s)) * blocks
        for h in range(heads):
            q = projected[:, 3 * d * h : 3 * d * h + d]
            k = projected[:, 3 * d * h + d : 3 * d * h + 2 * d]
            v = projected[:, 3 * d * h + 2 * d : 3 * d * h + 3 * d]
            q = rms_plain(q) * d**-0.5
            k = rms_plain(k) * d**-0.5
            kb, vb = k.astype(BF), v.astype(BF)
            logits = dot(vb, gates_ref[h])
            theta = jax.nn.sigmoid(logits[:, :d]) * (1.0 / SPAN)
            weighted = (theta * k).astype(BF)
            both = jnp.concatenate([kb, vb], axis=1)
            items = []
            for c in range(blocks):
                part = slice(c * SPAN, (c + 1) * SPAN)
                where = slot_ref[base + c] if is_last else s * blocks + c
                kv_ref[where, :, 2 * d * h : 2 * d * (h + 1)] = both[part]
                products = lax.dot_general(
                    weighted[part], both[part], (((0,), (0,)), ((), ())), preferred_element_type=F32
                )
                alpha = jax.nn.sigmoid(jnp.mean(logits[part, d : 2 * d], axis=0, keepdims=True) + flat_ref[bias + h])
                eta = jax.nn.sigmoid(
                    jnp.mean(logits[part, 2 * d :], axis=0, keepdims=True) + flat_ref[bias + heads + h]
                )
                widen = lambda row: jnp.concatenate([row, row, row], axis=1)
                items.append((products, widen(1.0 - alpha), widen(eta), q[part].astype(BF), flat_ref[base + c]))
            kept[s, h] = items
    copies, at = [], 0
    for target in kv_outs:
        count = target.shape[0]
        copies.append(pltpu.make_async_copy(kv_ref.at[pl.ds(at, count)], target, sem.at[len(copies)]))
        at += count
    for one in copies:
        one.start()
    zero = jnp.zeros((d, d), F32)
    row = lax.broadcasted_iota(jnp.int32, (d, d), 0)
    column = lax.broadcasted_iota(jnp.int32, (d, d), 1)
    eye = jnp.where(row == column, 1.0, 0.0).astype(F32)
    state = {}
    starts = []
    for h in range(heads):
        first = start_ref[h]
        starts.append(jnp.concatenate([zero, zero, first], axis=1))
    for key in kept:
        state[key] = (jnp.concatenate([eye, zero, zero], axis=1), jnp.concatenate([zero, eye, zero], axis=1))
    for c in range(blocks):
        for s in range(2):
            for h in range(heads):
                products, stay, eta, q, keep = kept[s, h][c]
                memory, moment = state[s, h]
                held = keep * memory + (1.0 - keep) * starts[h]
                held_low = held.astype(BF)
                recalled = dot(q, held_low)
                part = slice(c * SPAN, (c + 1) * SPAN)
                high = recalled[:, 2 * d :].astype(BF)
                r_ref[s, h, part, : 2 * d] = recalled[:, : 2 * d].astype(BF)
                r_ref[s, h, part, 2 * d : 3 * d] = high
                r_ref[s, h, part, 3 * d :] = (recalled[:, 2 * d :] - high.astype(F32)).astype(BF)
                cross = jnp.concatenate([zero, zero, products[:, d:]], axis=1)
                moment = eta * (keep * moment) - dot(products[:, :d].astype(BF), held_low) + cross
                state[s, h] = (stay * held + moment, moment)
    late = 1 - (me & 1)
    for h in range(heads):
        maps = [jnp.concatenate(state[s, h], axis=0) for s in range(2)]
        earlier, later = ordered(me & 1, maps[0], maps[1])
        low = earlier.astype(BF)
        total = compose(later, low)
        group_ref[h] = total.astype(BF)
        if is_last:
            level = [others[g][h] for g in range(groups - 1)] + [total]
            bit = 2
            while len(level) > 1:
                joined = []
                for i in range(0, len(level), 2):
                    earlier, later = ordered(me & bit, level[i].astype(F32), level[i + 1].astype(F32))
                    joined.append(compose(later, earlier))
                level = joined
                bit *= 2
            total_refs[0][h] = level[0].astype(BF)
        recalled = r_ref[late, h]
        folded = dot(recalled[:, : 2 * d], low)
        shift = folded[:, 2 * d :] + recalled[:, 2 * d : 3 * d].astype(F32) + recalled[:, 3 * d :].astype(F32)
        high = shift.astype(BF)
        r_ref[late, h, :, : 2 * d] = folded[:, : 2 * d].astype(BF)
        r_ref[late, h, :, 2 * d : 3 * d] = high
        r_ref[late, h, :, 3 * d :] = (shift - high.astype(F32)).astype(BF)
    copies.append(pltpu.make_async_copy(r_ref, store_ref.at[pl.ds(rel, 2)], sem.at[packs]))
    copies[-1].start()
    for one in copies:
        one.wait()


def pair_call(meta, flat, table, xs, gain, w, gates, initial, rel, before, is_last, counts):
    total_blocks = sum(counts)
    heads, d = gates.shape[0], gates.shape[1]
    parts = [len(x) for x in xs]
    rows = sum(x.shape[0] for x in xs[0])
    blocks = rows // SPAN
    groups = len(before) + 1
    extra = [b["map"] for b in before] + [b["kv"][0] for b in before] if is_last else []
    hbm = pl.BlockSpec(memory_space=pltpu.HBM)
    aliases = {}
    extra_specs = [vmem()] * len(extra)
    if rel > 0:
        aliases = {3 + sum(parts) + 4 + len(extra): 0}
        extra.append(before[-1]["r"])
        extra_specs.append(hbm)
    row = heads * 2 * d
    shapes = [
        jax.ShapeDtypeStruct((STORE_BYTES // (heads * rows * 8 * d), heads, rows, 4 * d), BF),
        jax.ShapeDtypeStruct((heads, 2 * d, 3 * d), BF),
    ]
    counts = counts if is_last else (2 * blocks,)
    shapes += [jax.ShapeDtypeStruct((n, SPAN, row), BF) for n in counts]
    specs = [hbm, vmem()] + [hbm] * len(counts)
    if is_last:
        shapes.append(jax.ShapeDtypeStruct((heads, 2 * d, 3 * d), BF))
        specs.append(vmem())
    if rel == 0:
        shapes.append(jax.ShapeDtypeStruct((total_blocks,), jnp.int32))
        specs.append(smem())
    out = pl.pallas_call(
        functools.partial(pair_kernel, heads, d, blocks, rel, is_last, groups, parts, len(counts)),
        out_shape=shapes,
        grid=(1,),
        in_specs=[smem()] * 3
        + [vmem()] * (sum(parts) + 4)
        + extra_specs,
        out_specs=specs,
        input_output_aliases=aliases,
        scratch_shapes=[
            pltpu.VMEM((sum(counts), SPAN, row), BF),
            pltpu.VMEM((2, heads, rows, 4 * d), BF),
            pltpu.SemaphoreType.DMA((len(counts) + 1,)),
        ],
        compiler_params=params(),
        cost_estimate=cost(2.5e9, 8e6),
        name="pair_last" if is_last else "pair_first",
    )(meta, flat, table, *xs[0], *xs[1], gain, w, gates, initial, *extra)
    return {"r": out[0], "map": out[1], "kv": list(out[2 : 2 + len(counts)]), "total": out[-1]}


def join_kernel(heads, d, meta_ref, own_ref, got_ref, a_ref, b_ref):
    for h in range(heads):
        earlier, later = ordered(meta_ref[1] & 1, own_ref[h].astype(F32), got_ref[h].astype(F32))
        joined = compose(later, earlier).astype(BF)
        a_ref[h] = joined[:, : 2 * d]
        b_ref[h] = joined[:, 2 * d :]


def join(meta, own, got):
    heads, rows, _ = own.shape
    d = rows // 2
    return pl.pallas_call(
        functools.partial(join_kernel, heads, d),
        out_shape=[jax.ShapeDtypeStruct((heads, rows, n), BF) for n in (rows, d)],
        in_specs=[smem(), vmem(), vmem()],
        out_specs=[vmem()] * 2,
        compiler_params=params(),
        cost_estimate=cost(1e8, 1.2e6),
        name="join",
    )(meta, own, got)


def step_kernel(heads, a_ref, b_ref, state_ref, out_ref):
    for h in range(heads):
        out_ref[h] = (dot(a_ref[h], state_ref[h]) + b_ref[h].astype(F32)).astype(BF)


def step(a, b, state):
    return pl.pallas_call(
        functools.partial(step_kernel, a.shape[0]),
        out_shape=jax.ShapeDtypeStruct(b.shape, BF),
        in_specs=[vmem()] * 3,
        out_specs=vmem(),
        compiler_params=params(),
        cost_estimate=cost(1e8, 6e5),
        name="step",
    )(a, b, state)


def recall_kernel(heads, d, groups, *refs):
    meta_ref, got_ref, state_ref = refs[:3]
    map_refs, store_ref = refs[3 : 3 + groups], refs[3 + groups]
    out_refs, (r_ref, sem) = refs[4 + groups : -2], refs[-2:]
    shards = 2 * groups
    loads = [pltpu.make_async_copy(store_ref.at[r], r_ref.at[r], sem.at[r]) for r in range(shards)]
    for one in reversed(loads):
        one.start()
    me, odd = meta_ref[0], (meta_ref[1] & 1) != 0
    d2 = 2 * d
    apply = lambda m, e: dot(m[:, :d2], e.astype(BF)) + m[:, d2:].astype(F32)
    entering = []
    for h in range(heads):
        state = state_ref[h].astype(F32)
        state = jnp.where(odd, apply(got_ref[h], state), state)
        levels = [[map_refs[g][h] for g in range(groups)]]
        bit = 2
        while len(levels[-1]) > 2:
            level, joined = levels[-1], []
            for i in range(0, len(level), 2):
                earlier, later = ordered(me & bit, level[i].astype(F32), level[i + 1].astype(F32))
                joined.append(compose(later, earlier).astype(BF))
            levels.append(joined)
            bit *= 2
        states = [state]
        for level in reversed(levels):
            spread = []
            for i, one in enumerate(states):
                swap = (me & bit) != 0
                after = apply(jnp.where(swap, level[2 * i + 1], level[2 * i]), one)
                spread += [jnp.where(swap, after, one), jnp.where(swap, one, after)]
            states = spread
            bit //= 2
        entering.append([one.astype(BF) for one in states])
    for r in reversed(range(shards)):
        loads[r].wait()
        for h in range(heads):
            recalled = dot(r_ref[r, h, :, :d2], entering[h][r // 2])
            recalled += r_ref[r, h, :, d2 : 3 * d].astype(F32) + r_ref[r, h, :, 3 * d :].astype(F32)
            out_refs[r][:, h * d : (h + 1) * d] = rms_plain(recalled).astype(BF)


def recall(meta, got, state, pairs):
    groups = len(pairs)
    _, heads, rows, width = pairs[-1]["r"].shape
    d = width // 4
    return pl.pallas_call(
        functools.partial(recall_kernel, heads, d, groups),
        out_shape=[jax.ShapeDtypeStruct((rows, heads * d), BF)] * (2 * groups),
        in_specs=[smem()] + [vmem()] * (2 + groups) + [pl.BlockSpec(memory_space=pltpu.HBM)],
        out_specs=[vmem()] * (2 * groups),
        scratch_shapes=[
            pltpu.VMEM((2 * groups, heads, rows, width), BF),
            pltpu.SemaphoreType.DMA((2 * groups,)),
        ],
        compiler_params=params(),
        cost_estimate=cost(2e8, 3e6),
        name="recall",
    )(meta, got, state, *[p["map"] for p in pairs], pairs[-1]["r"])


def ffn_kernel(shards, tile, *refs):
    sources, out_ref, targets = refs[: 2 * shards + 5], refs[2 * shards + 5], refs[2 * shards + 6 : -3]
    hidden_ref, residual_ref, sem = refs[-3:]
    wg_ref, wu_ref, wd_ref = targets[-3:]
    small = [
        pltpu.make_async_copy(source, target, sem.at[i])
        for i, (source, target) in enumerate(zip(sources[:-3], targets[:-3]))
    ]
    down = pltpu.make_async_copy(sources[-1], wd_ref, sem.at[len(small)])
    columns = []
    for i in range(wg_ref.shape[1] // tile):
        part = pl.ds(i * tile, tile)
        at = len(small) + 1 + 2 * i
        columns.append(
            [
                pltpu.make_async_copy(sources[-3].at[:, part], wg_ref.at[:, part], sem.at[at]),
                pltpu.make_async_copy(sources[-2].at[:, part], wu_ref.at[:, part], sem.at[at + 1]),
            ]
        )
    for one in small + [one for pair in columns for one in pair] + [down]:
        one.start()
    for one in small:
        one.wait()
    x_ref, gain_ref = targets[:2]
    residual = x_ref[...].astype(F32)
    for r in range(shards):
        residual += dot(targets[2 + r][...], targets[2 + shards + r][...])
    residual_ref[...] = residual
    scale = lax.rsqrt(jnp.mean(residual * residual, axis=-1, keepdims=True) + EPS)
    low = (residual * scale * gain_ref[...]).astype(BF)
    for i, pair in enumerate(columns):
        for one in pair:
            one.wait()
        part = slice(i * tile, (i + 1) * tile)
        gate = dot(low, wg_ref[:, part])
        up = dot(low, wu_ref[:, part])
        hidden_ref[:, part] = (gate / (1.0 + jnp.exp(-gate)) * up).astype(BF)
    down.wait()
    out_ref[...] = (residual_ref[...] + dot(hidden_ref[...], wd_ref[...])).astype(BF)


def ffn(x, gain, w_out, pieces, w_gate, w_up, w_down):
    rows, width = x.shape
    hidden = w_gate.shape[1]
    tile = 256
    while hidden % tile:
        tile //= 2
    shards = len(pieces)
    sources = [x, gain, *pieces, *w_out, w_gate, w_up, w_down]
    return pl.pallas_call(
        functools.partial(ffn_kernel, shards, tile),
        out_shape=jax.ShapeDtypeStruct((rows, width), BF),
        in_specs=[pl.BlockSpec(memory_space=pl.ANY)] * len(sources),
        out_specs=vmem(),
        scratch_shapes=[pltpu.VMEM(a.shape, a.dtype) for a in sources]
        + [
            pltpu.VMEM((rows, hidden), BF),
            pltpu.VMEM((rows, width), F32),
            pltpu.SemaphoreType.DMA((2 * shards + 3 + 2 * (hidden // tile),)),
        ],
        compiler_params=params(MOST_VMEM),
        cost_estimate=cost(5e9, 2.2e7),
        name="ffn",
    )(*sources)


def regroup_kernel(plan, *refs):
    sources, targets, (stage, sem_in, sem_out) = refs[: plan.sources], refs[plan.sources : -3], refs[-3:]
    into, out, starts = [], [], []
    at = 0
    for i, source in enumerate(sources):
        starts.append(at)
        into.append(pltpu.make_async_copy(source, stage.at[pl.ds(at, source.shape[0])], sem_in.at[i]))
        at += source.shape[0]
    for target, pieces in zip(targets, plan.targets):
        place = 0
        for which, first, count in pieces:
            out.append(
                pltpu.make_async_copy(
                    stage.at[pl.ds(starts[which] + first, count)], target.at[pl.ds(place, count)], sem_out.at[len(out)]
                )
            )
            place += count
    for one in into:
        one.start()
    for one in into:
        one.wait()
    for one in out:
        one.start()
    for one in out:
        one.wait()


class Plan:
    def __init__(self, sources, targets):
        self.sources, self.targets = sources, targets


def regroup(sources, targets):
    block = sources[0].shape[1:]
    hbm = pl.BlockSpec(memory_space=pltpu.HBM)
    return pl.pallas_call(
        functools.partial(regroup_kernel, Plan(len(sources), targets)),
        out_shape=[jax.ShapeDtypeStruct((sum(c for _, _, c in pieces),) + block, BF) for pieces in targets],
        in_specs=[hbm] * len(sources),
        out_specs=[hbm] * len(targets),
        scratch_shapes=[
            pltpu.VMEM((sum(a.shape[0] for a in sources),) + block, BF),
            pltpu.SemaphoreType.DMA((len(sources),)),
            pltpu.SemaphoreType.DMA((sum(len(pieces) for pieces in targets),)),
        ],
        compiler_params=params(),
        cost_estimate=cost(0, 4e6),
        name="regroup",
    )(*sources)


def place_kernel(slots, rows_ref, *refs):
    sources, (out_ref, stage, sem_in, sem_out) = refs[:-4], refs[-4:]
    into, out = [], []
    for source, held in zip(sources, slots):
        for i in range(source.shape[0]):
            n = held[i]
            into.append(pltpu.make_async_copy(source.at[i], stage.at[n], sem_in.at[n]))
            out.append(pltpu.make_async_copy(stage.at[n], out_ref.at[rows_ref[n]], sem_out.at[n]))
    for one in into:
        one.start()
    for first, second in zip(into, out):
        first.wait()
        second.start()
    for one in out:
        one.wait()


def place(rows, sources, slots):
    anywhere = pl.BlockSpec(memory_space=pl.ANY)
    count = rows.shape[0]
    shape = (count,) + sources[0].shape[1:]
    return pl.pallas_call(
        functools.partial(place_kernel, slots),
        out_shape=jax.ShapeDtypeStruct(shape, sources[0].dtype),
        in_specs=[smem()] + [anywhere] * len(sources),
        out_specs=anywhere,
        scratch_shapes=[
            pltpu.VMEM(shape, sources[0].dtype),
            pltpu.SemaphoreType.DMA((count,)),
            pltpu.SemaphoreType.DMA((count,)),
        ],
        compiler_params=params(MOST_VMEM),
        cost_estimate=cost(0, 4 * sources[0].size * len(sources)),
        name="place",
    )(rows, *sources)


def per_device(
    tokens,
    norm_gain,
    w_qkv,
    w_mem_gates,
    persist_keys,
    persist_values,
    alpha_bias,
    eta_bias,
    w_out,
    ffn_gain,
    w_gate,
    w_up,
    w_down,
    segment_ids,
    block_table,
):
    model_dim = tokens.shape[1]
    heads, d = w_qkv.shape[1], w_mem_gates.shape[2]
    shards = lax.axis_size("head")
    n_seq = lax.axis_size("seq")
    seq_index, head_index = lax.axis_index("seq"), lax.axis_index("head")
    blocks_here = shards * tokens.shape[0] // SPAN
    per_owner = PER_OWNER

    count = tokens.shape[0] // SPAN
    cut = tokens.shape[0] // CUTS
    parts = [tokens[i * cut : (i + 1) * cut] for i in range(CUTS)] if CUTS > 1 else [tokens]
    far = [[exchange(part, "head", 2 * g) for part in parts] for g in range(1, shards // 2)]
    xs = {0: [parts, [exchange(tokens, "head", 1)]]}
    w_core = exchange(w_out, "head", 1)

    int32 = jnp.int32
    half = blocks_here // 2
    parity, place_in_line = seq_index & 1, seq_index >> 1
    id_blocks = segment_ids.reshape(-1, SPAN)[:, 0]
    keep_all = jnp.concatenate([jnp.zeros((1,), F32), (id_blocks[1:] == id_blocks[:-1]).astype(F32)])
    keep = lax.dynamic_slice_in_dim(keep_all, seq_index * blocks_here, blocks_here)
    flat = jnp.concatenate([keep, alpha_bias, eta_bias])
    seq = seq_index.astype(int32)[None]

    meta = jnp.stack([head_index, seq_index]).astype(int32)
    slots = jnp.arange(blocks_here, dtype=int32)
    line = n_seq // 2
    early = list(range(line // 2, line))
    others = list(range(1, line // 2))

    gates = jnp.broadcast_to(
        jnp.transpose(w_mem_gates, (0, 2, 1))[:, :, :, None], (heads, d, 3, d)
    ).reshape(heads, d, 3 * d)
    w = w_qkv.reshape(model_dim, heads * 3 * d)
    gain = norm_gain.reshape(1, -1)
    pkeys = persist_keys.reshape(PERS, heads, d)
    pvalues = persist_values.reshape(PERS, heads, d)
    initial = jnp.einsum("phd,phe->hde", pkeys, pvalues, preferred_element_type=F32) / PERS

    pairs = []
    groups = shards // 2
    for g in range(groups):
        if g > 0:
            far[g - 1], pairs[0]["map"], w_core = lax.optimization_barrier((far[g - 1], pairs[0]["map"], w_core))
            xs[g] = [far[g - 1], [exchange(part, "head", 1) for part in far[g - 1]]]
        pairs.append(pair_call(meta, flat, block_table if g == 0 else pairs[0]["total"], xs[g], gain, w, gates, initial, 2 * g, pairs, g == groups - 1, (half,) + (per_owner,) * line))
    total, block_table, w_out = lax.optimization_barrier((pairs[-1]["total"], block_table, w_out))
    w_outs_far = [exchange(w_out, "head", 2 * g) for g in range(1, groups)]
    got = exchange(total, "seq", 1)

    to_me = (block_table // blocks_here == seq_index).reshape(n_seq, blocks_here)
    earlier = to_me[:, None, :] & (slots[None, None, :] < slots[None, :, None])
    sources = jnp.arange(n_seq, dtype=int32)[:, None]
    arrival = (
        jnp.sum(earlier.astype(int32), axis=2)
        + ((sources & 1) ^ parity ^ 1) * half
        + ((sources >> 1) ^ place_in_line) * per_owner
    )
    landed = (arrival.reshape(1, -1) == slots[:, None]) & to_me.reshape(1, -1)
    rows = jnp.sum(jnp.where(landed, (block_table % blocks_here)[None, :], 0), axis=1).astype(int32)

    cross, home, *same = pairs[-1]["kv"]
    far_same = [exchange(same[m - 1], "seq", 2 * m) for m in early]
    a, b = join(meta, total, got)
    b, cross = lax.optimization_barrier((b, cross))
    cross = exchange(cross, "seq", 1)
    onward = [(i, i + 2) for i in range(n_seq - 2)]
    hops = n_seq // 4
    state = b
    for hop in range(hops):
        state = lax.ppermute(state, "seq", onward)
        if hop == 0:
            state, far_same, w_outs_far = lax.optimization_barrier((state, far_same, w_outs_far))
        if hop < hops - 1:
            state = step(a, b, state)
    w_outs = [w_out, w_core] + [w for one in w_outs_far for w in (one, exchange(one, "head", 1))]
    cut = lambda m: (0, m * per_owner, per_owner)
    regrouped = regroup(
        [cross] + [same[m - 1] for m in others],
        [[(1 + i, 0, per_owner), cut(m)] for i, m in enumerate(others)] + [[cut(m)] for m in early] + [[cut(0)]],
    )
    regrouped = list(regrouped)
    retrieved = list(recall(meta, got, state, pairs))
    pieces = [retrieved[0]] + [exchange(retrieved[i], "head", i) for i in range(1, shards)]
    pieces[1], regrouped = lax.optimization_barrier((pieces[1], regrouped))
    arrived = [exchange(one, "seq", 2 * m) for one, m in zip(regrouped, others + early)]
    mixed = ffn(tokens, ffn_gain.reshape(1, -1), w_outs, pieces, w_gate, w_up, w_down)
    held = [regrouped[-1], home] + far_same + arrived
    mixed, held = lax.optimization_barrier((mixed, held))
    of = lambda e, m: [e * half + m * per_owner + i for i in range(per_owner)]
    taken = [of(0, 0), of(1, 0)] + [of(1, m) for m in early]
    taken += [of(1, m) + of(0, m) for m in others] + [of(0, m) for m in early]
    return mixed, place(rows, held, taken)


def solution(mesh):
    return jax.shard_map(
        per_device,
        mesh=mesh,
        in_specs=(
            P(("seq", "head"), None),
            P(),
            P(None, "head", None),
            P("head", None, None),
            P(None, "head"),
            P(None, "head"),
            P("head"),
            P("head"),
            P("head", None),
            P(),
            P(),
            P(),
            P(),
            P(),
            P(),
        ),
        out_specs=(P(("seq", "head"), None), P("seq", None, "head")),
        check_vma=False,
    )
```

time: 91.5 us -> 85.6 us (0.936)
  local copies, waits for them, and re-layouts: 18.1 us -> 11.6 us
  Pallas kernels: 26.8 us -> 31.3 us
  starting transfers between devices: 31.4 us -> 28.3 us
    ppermute x22 -> x16, starting transfers between devices: 25.2 us -> 20.3 us  [exchange(): return lax.ppermute(value, axis, [(i, i ^ bit) for i in range(count)])]
    unnamed x65 -> x47, local copies, waits for them, and re-layouts: 14 us -> 9.63 us
    ppermute x22 -> x16, waiting for transfers between devices: 10.6 us -> 7.03 us  [exchange(): return lax.ppermute(value, axis, [(i, i ^ bit) for i in range(count)])]
    pallas_call x2, Pallas kernels: 9.84 us -> 12.8 us  [pair_call(): pl.pallas_call(functools.partial(pair_kernel, heads, d, blocks, rel, is_l...]
    slice x2 -> x0, local copies, waits for them, and re-layouts: 2.87 us -> none  [the longest x1 1.81 us: per_device(): cross = [cross[m * per_owner:(m + 1) * per_owner] for m in range(line)]]
    ppermute x2, waiting for transfers between devices: 0.01 us -> 2.78 us  [per_device(): state = lax.ppermute(state, 'seq', onward)]
    ppermute x2, starting transfers between devices: 6.25 us -> 8.02 us  [per_device(): state = lax.ppermute(state, 'seq', onward)]
    pallas_call x4 -> x3, Pallas kernels: 5.9 us -> 6.8 us  [the longest x1 2.87 us: recall(): pl.pallas_call(functools.partial(recall_kernel, heads, d, groups), out_sh...]
  transfers between devices with their start and end apart: 24 -> 18, of which waited for: 6 -> 4; matrix products, arithmetic and copies ran while one was open for 9% -> 8% of each run, Pallas kernels for 21% -> 26%
where the time goes in v1:
time: 85.6 us; the launch traced here: 85.1 us
  Pallas kernels  31.3 us (37%)
  starting transfers between devices  28.3 us (33%)
  local copies, waits for them, and re-layouts  11.6 us (14%)
  waiting for transfers between devices  9.81 us (11%)
  other arithmetic  2.06 us (2%)
  between operations  1.13 us (1%)
  matrix products  0.91 us (1%)
    ppermute x16, starting transfers between devices, exchange(): return lax.ppermute(value, axis, [(i, i ^ bit) for i in range(count)])  20.3 us
    pallas_call x2, Pallas kernels, pair_call(): pl.pallas_call(functools.partial(pair_kernel, heads, d, blocks, rel, is_l...  12.8 us
    pallas_call x1, Pallas kernels, ffn(): pl.pallas_call(functools.partial(ffn_kernel, shards, tile), out_shape=jax...  10.5 us
    unnamed x47, local copies, waits for them, and re-layouts  9.63 us
    ppermute x2, starting transfers between devices, per_device(): state = lax.ppermute(state, 'seq', onward)  8.02 us
    ppermute x16, waiting for transfers between devices, exchange(): return lax.ppermute(value, axis, [(i, i ^ bit) for i in range(count)])  7.03 us
    pallas_call x1, Pallas kernels, recall(): pl.pallas_call(functools.partial(recall_kernel, heads, d, groups), out_sh...  2.87 us
    pallas_call x1, Pallas kernels, place(): pl.pallas_call(functools.partial(place_kernel, slots), out_shape=jax.Shap...  2.82 us
  transfers between devices with their start and end apart: 18, of which 4 were waited for; matrix products, arithmetic and copies ran while one was open for 8% of the time, Pallas kernels for 26%

profile of v1, /device:TPU:0, one launch (start us, length us, event | category | flops | bytes accessed | tf_op | source)
XLA Modules:
  0.0 85.1 jit_solution(13286561271887822655)
XLA Ops:
  0.6 0.5 collective-permute-start
  1.2 2.6 %collective-permute-start.1 = (bf16[256,1024]{1,0:T(8,128)(2,1)}, bf16[256,1024]{1,0:T(8,128)(2,1)S(1)}, u32[]{:S(2)}, u32[]{:S(2)}) collective-permute-start(bf16[256,1024]{1,0:T(8,128)(2,1)} %refs_0_.1), channel_id=1, source_target_pairs={{0,2},{1,3},{2,0},{3,1},{4,6},{5,7},{6,4},{7,5},{8,10},{9,11},{10,... | collective-permute-start | bytes 1572872 | tf_op jit(solution)/shard_map/ppermute | solution.py:42
  3.8 0.2 collective-permute-start.2
  3.9 0.8 reshape.91
  4.8 0.1 fusion
  4.9 1.7 %copy.38 = bf16[128,8,2,384]{3,1,2,0:T(8,128)(2,1)S(1)} copy(bf16[128,8,2,384]{3,2,1,0:T(2,128)(2,1)} %bitcast.26) | data formatting | bytes 3145728
  6.6 0.7 copy.31
  7.3 0.2 copy.34.refs_7_
  7.7 0.7 pad_maximum_fusion.refs_1_
  8.5 0.9 %convolution_multiply_fusion.refs_8_ = f32[2,128,128]{2,1,0:T(8,128)S(1)} fusion(bf16[16,256]{1,0:T(8,128)(2,1)S(1)} %copy-done, bf16[16,256]{1,0:T(8,128)(2,1)} %param.19), kind=kOutput, calls=%fused_computation | convolution fusion | flops 1081344 | bytes 147456 | tf_op jit(solution)/shard_map/phd,phe->hde/dot_general | solution.py:555
  9.4 1.0 %copy-done.2 = bf16[256,1024]{1,0:T(8,128)(2,1)S(1)} copy-done((bf16[256,1024]{1,0:T(8,128)(2,1)S(1)}, bf16[256,1024]{1,0:T(8,128)(2,1)}, u32[]{:S(2)}) %copy-start.2) | copy-done | bytes 524312
  10.5 0.7 copy-done.8
  11.1 0.7 copy-done.9
  11.8 6.2 %pair_first.1 = (bf16[112,2,256,512]{3,2,1,0:T(8,128)(2,1)}, bf16[2,256,384]{2,1,0:T(8,128)(2,1)S(1)}, bf16[8,64,512]{2,1,0:T(8,128)(2,1)S(1)}, s32[16]{0:T(128)S(1)}) custom-call(s32[2]{0:T(128)S(1)} %pad_add_fusion.refs_0_.meta_ref, f32[20]{0:T(128)S(1)} %pad_maximum_fusion.refs_1_, s32[128]{0:T(128)S(1)} %copy-done.9, bf16[256,1024]{1,0:T(8,128)(2,1)S(1)} %copy-done.2, ...), custom_call_target="tpu_custom_call" | custom-call | flops 2500000 | bytes 8000 | tf_op jit(solution)/shard_map/pair_first/pallas_call | solution.py:226
  18.0 0.4 collective-permute-start.3
  18.4 1.6 %collective-permute-done.3.refs_4_ = bf16[256,1024]{1,0:T(8,128)(2,1)S(1)} collective-permute-done((bf16[256,1024]{1,0:T(8,128)(2,1)S(1)}, bf16[256,1024]{1,0:T(8,128)(2,1)S(1)}, u32[]{:S(2)}, u32[]{:S(2)}) %collective-permute-start.3) | collective-permute-done | bytes 524320 | tf_op jit(solution)/shard_map/ppermute | solution.py:42
  20.0 6.7 %pair_last.1 = (bf16[112,2,256,512]{3,2,1,0:T(8,128)(2,1)}, bf16[2,256,384]{2,1,0:T(8,128)(2,1)S(1)}, bf16[8,64,512]{2,1,0:T(8,128)(2,1)S(1)}, bf16[2,64,512]{2,...) custom-call(s32[2]{0:T(128)S(1)} %pad_add_fusion.refs_0_.meta_ref, ...), custom_call_target="tpu_custom_call", output_to_operand_aliasing={{0}: (11, {})} | custom-call | flops 2500000 | bytes 8000 | tf_op jit(solution)/shard_map/pair_last/pallas_call | solution.py:226
  26.7 0.6 copy-done.4
  27.3 0.7 copy-done.5
  28.0 0.8 copy-done.11
  28.7 0.7 copy-done.12
  29.4 0.7 copy-done.13
  30.1 1.5 %collective-permute-start.4 = (bf16[2,256,384]{2,1,0:T(8,128)(2,1)S(1)}, bf16[2,256,384]{2,1,0:T(8,128)(2,1)S(1)}, u32[]{:S(2)}, u32[]{:S(2)}) collective-permute-start(bf16[2,256,384]{2,1,0:T(8,128)(2,1)S(1)} %get-tuple-element.56.own_ref), channel_id=1, source_target_pairs={{0,4},{4,0},{8,12},{12,8},{16,20},{20,16},{24,28},{28,24},{1,5},{5... | collective-permute-start | bytes 1179656 | tf_op jit(solution)/shard_map/ppermute | solution.py:42
  31.6 0.5 collective-permute-start.8
  32.1 2.6 %collective-permute-start.6 = (bf16[2,64,512]{2,1,0:T(8,128)(2,1)}, bf16[2,64,512]{2,1,0:T(8,128)(2,1)S(1)}, u32[]{:S(2)}, u32[]{:S(2)}) collective-permute-start(bf16[2,64,512]{2,1,0:T(8,128)(2,1)} %copy-done.13), channel_id=1, source_target_pairs={{0,16},{4,20},{8,24},{12,28},{16,0},{20,4},{24,8},{28,12},{1,17},{... | collective-permute-start | bytes 393224 | tf_op jit(solution)/shard_map/ppermute | solution.py:42
  34.7 1.3 %collective-permute-start.7 = (bf16[2,64,512]{2,1,0:T(8,128)(2,1)}, bf16[2,64,512]{2,1,0:T(8,128)(2,1)S(1)}, u32[]{:S(2)}, u32[]{:S(2)}) collective-permute-start(bf16[2,64,512]{2,1,0:T(8,128)(2,1)} %copy-done.12), channel_id=1, source_target_pairs={{0,24},{4,28},{8,16},{12,20},{16,8},{20,12},{24,0},{28,4},{1,25},{... | collective-permute-start | bytes 393224 | tf_op jit(solution)/shard_map/ppermute | solution.py:42
  36.0 5.4 %collective-permute-done.4.got_ref.refs_1_ = bf16[2,256,384]{2,1,0:T(8,128)(2,1)S(1)} collective-permute-done((bf16[2,256,384]{2,1,0:T(8,128)(2,1)S(1)}, bf16[2,256,384]{2,1,0:T(8,128)(2,1)S(1)}, u32[]{:S(2)}, u32[]{:S(2)}) %collective-permute-start.4) | collective-permute-done | bytes 393248 | tf_op jit(solution)/shard_map/ppermute | solution.py:42
  41.4 0.9 %join.1 = (bf16[2,256,256]{2,1,0:T(8,128)(2,1)S(1)}, bf16[2,256,128]{2,1,0:T(8,128)(2,1)S(1)}) custom-call(s32[2]{0:T(128)S(1)} %pad_add_fusion.refs_0_.meta_ref, bf16[2,256,384]{2,1,0:T(8,128)(2,1)S(1)} %get-tuple-element.56.own_ref, bf16[2,256,384]{2,1,0:T(8,128)(2,1)S(1)} %collective-permute-done.4.got_ref.refs_1_), custom_call_target="tpu_custom_call" | custom-call | flops 100000 | bytes 1200 | tf_op jit(solution)/shard_map/join/pallas_call | solution.py:258
  42.3 3.5 %collective-permute-start.5 = (bf16[2,256,128]{2,1,0:T(8,128)(2,1)S(1)}, bf16[2,256,128]{2,1,0:T(8,128)(2,1)S(1)}, u32[]{:S(2)}, u32[]{:S(2)}) collective-permute-start(bf16[2,256,128]{2,1,0:T(8,128)(2,1)S(1)} %get-tuple-element.60.b_ref), channel_id=1, source_target_pairs={{0,8},{4,12},{8,16},{12,20},{16,24},{20,28},{1,9},{5,13},{9,17},{1... | collective-permute-start | bytes 393224 | tf_op jit(solution)/shard_map/ppermute | solution.py:588
  45.9 1.6 %collective-permute-start.11 = (bf16[8,64,512]{2,1,0:T(8,128)(2,1)}, bf16[8,64,512]{2,1,0:T(8,128)(2,1)S(1)}, u32[]{:S(2)}, u32[]{:S(2)}) collective-permute-start(bf16[8,64,512]{2,1,0:T(8,128)(2,1)} %copy-done.11), channel_id=1, source_target_pairs={{0,4},{4,0},{8,12},{12,8},{16,20},{20,16},{24,28},{28,24},{1,5},{5... | collective-permute-start | bytes 1572872 | tf_op jit(solution)/shard_map/ppermute | solution.py:42
  47.4 0.9 %collective-permute-done.5.state_ref = bf16[2,256,128]{2,1,0:T(8,128)(2,1)S(1)} collective-permute-done((bf16[2,256,128]{2,1,0:T(8,128)(2,1)S(1)}, bf16[2,256,128]{2,1,0:T(8,128)(2,1)S(1)}, u32[]{:S(2)}, u32[]{:S(2)}) %collective-permute-start.5) | collective-permute-done | bytes 131104 | tf_op jit(solution)/shard_map/ppermute | solution.py:588
  48.3 0.2 step.1
  48.5 4.5 %collective-permute-start.9 = (bf16[2,256,128]{2,1,0:T(8,128)(2,1)S(1)}, bf16[2,256,128]{2,1,0:T(8,128)(2,1)S(1)}, u32[]{:S(2)}, u32[]{:S(2)}) collective-permute-start(bf16[2,256,128]{2,1,0:T(8,128)(2,1)S(1)} %step.1), channel_id=1, source_target_pairs={{0,8},{4,12},{8,16},{12,20},{16,24},{20,28},{1,9},{5,13},{9,17},{1... | collective-permute-start | bytes 393224 | tf_op jit(solution)/shard_map/ppermute | solution.py:588
  53.2 0.2 convert_reduce_fusion
  53.5 1.9 %collective-permute-done.9.refs_2_ = bf16[2,256,128]{2,1,0:T(8,128)(2,1)S(1)} collective-permute-done((bf16[2,256,128]{2,1,0:T(8,128)(2,1)S(1)}, bf16[2,256,128]{2,1,0:T(8,128)(2,1)S(1)}, u32[]{:S(2)}, u32[]{:S(2)}) %collective-permute-start.9) | collective-permute-done | bytes 131104 | tf_op jit(solution)/shard_map/ppermute | solution.py:588
  55.4 2.9 %recall.1 = (bf16[256,256]{1,0:T(8,128)(2,1)S(1)}, bf16[256,256]{1,0:T(8,128)(2,1)S(1)}, bf16[256,256]{1,0:T(8,128)(2,1)S(1)}, bf16[256,256]{1,0:T(8,128)(2,1)S(1)}) custom-call(s32[2]{0:T(128)S(1)} %pad_add_fusion.refs_0_.meta_ref, bf16[2,256,384]{2,1,0:T(8,128)(2,1)S(1)} %collective-permute-done.4.got_ref.refs_1_, ...), custom_call_target="tpu_custom_call" | custom-call | flops 200000 | bytes 3000 | tf_op jit(solution)/shard_map/recall/pallas_call | solution.py:332
  58.4 1.5 %collective-permute-start.12 = (bf16[256,256]{1,0:T(8,128)(2,1)S(1)}, bf16[256,256]{1,0:T(8,128)(2,1)S(1)}, u32[]{:S(2)}, u32[]{:S(2)}) collective-permute-start(bf16[256,256]{1,0:T(8,128)(2,1)S(1)} %get-tuple-element.76), channel_id=1, source_target_pairs={{0,2},{1,3},{2,0},{3,1},{4,6},{5,7},{6,4},{7,5},{8,10},{9,11},{10,... | collective-permute-start | bytes 393224 | tf_op jit(solution)/shard_map/ppermute | solution.py:42
  60.0 0.3 collective-permute-start.13
  60.3 1.1 %regroup.1 = (bf16[4,64,512]{2,1,0:T(8,128)(2,1)S(1)}, bf16[2,64,512]{2,1,0:T(8,128)(2,1)S(1)}, bf16[2,64,512]{2,1,0:T(8,128)(2,1)S(1)}, bf16[2,64,512]{2,1,0:T(8,128)(2,1)S(1)}) custom-call(bf16[8,64,512]{2,1,0:T(8,128)(2,1)S(1)} %collective-permute-done.11.refs_0_, bf16[2,64,512]{2,1,0:T(8,128)(2,1)S(1)} %copy-done.6), custom_call_target="tpu_custom_call" | custom-call | bytes 4000 | tf_op jit(solution)/shard_map/regroup/pallas_call | solution.py:448
  61.5 0.6 copy-done.7
  62.1 2.4 %collective-permute-start.15 = (bf16[4,64,512]{2,1,0:T(8,128)(2,1)S(1)}, bf16[4,64,512]{2,1,0:T(8,128)(2,1)S(1)}, u32[]{:S(2)}, u32[]{:S(2)}) collective-permute-start(bf16[4,64,512]{2,1,0:T(8,128)(2,1)S(1)} %get-tuple-element.84), channel_id=1, source_target_pairs={{0,8},{4,12},{8,0},{12,4},{16,24},{20,28},{24,16},{28,20},{1,9},{5... | collective-permute-start | bytes 786440 | tf_op jit(solution)/shard_map/ppermute | solution.py:42
  64.6 2.6 %collective-permute-start.16 = (bf16[2,64,512]{2,1,0:T(8,128)(2,1)S(1)}, bf16[2,64,512]{2,1,0:T(8,128)(2,1)S(1)}, u32[]{:S(2)}, u32[]{:S(2)}) collective-permute-start(bf16[2,64,512]{2,1,0:T(8,128)(2,1)S(1)} %get-tuple-element.85), channel_id=1, source_target_pairs={{0,16},{4,20},{8,24},{12,28},{16,0},{20,4},{24,8},{28,12},{1,17},{... | collective-permute-start | bytes 393224 | tf_op jit(solution)/shard_map/ppermute | solution.py:42
  67.2 2.1 %collective-permute-start.17 = (bf16[2,64,512]{2,1,0:T(8,128)(2,1)S(1)}, bf16[2,64,512]{2,1,0:T(8,128)(2,1)S(1)}, u32[]{:S(2)}, u32[]{:S(2)}) collective-permute-start(bf16[2,64,512]{2,1,0:T(8,128)(2,1)S(1)} %get-tuple-element.86), channel_id=1, source_target_pairs={{0,24},{4,28},{8,16},{12,20},{16,8},{20,12},{24,0},{28,4},{1,25},{... | collective-permute-start | bytes 393224 | tf_op jit(solution)/shard_map/ppermute | solution.py:42
  69.3 0.7 select_reduce_fusion.rows_ref
  70.1 0.6 copy-done.18
  70.7 10.5 %ffn.1 = bf16[256,1024]{1,0:T(8,128)(2,1)} custom-call(bf16[256,1024]{1,0:T(8,128)(2,1)} %refs_0_.1, f32[1,1024]{1,0:T(1,128)} %bitcast.28, bf16[256,256]{1,0:T(8,128)(2,1)} %copy-done.3, bf16[256,256]{1,0:T(8,128)(2,1)} %copy-done.16, bf16[256,256]{1,0:T(8,128)(2,1)} %copy-done.17, bf16[256,256]{1,0:T(8,128)(2,1)} %copy-done.18, bf16[256,1024]{1,0:T(8,128)(2,1)} %refs_6_, ...), custom_call_target="tpu_custom_call" | custom-call | flops 5000000 | bytes 22000 | tf_op jit(solution)/shard_map/ffn/pallas_call | solution.py:396
  81.3 0.6 copy-done.21
  82.1 2.8 %place.1 = bf16[16,64,512]{2,1,0:T(8,128)(2,1)} custom-call(s32[16]{0:T(128)} %select_reduce_fusion.rows_ref, bf16[2,64,512]{2,1,0:T(8,128)(2,1)} %copy-done.7, bf16[2,64,512]{2,1,0:T(8,128)(2,1)} %copy-done.4, bf16[2,64,512]{2,1,0:T(8,128)(2,1)} %copy-done.19, bf16[2,64,512]{2,1,0:T(8,128)(2,1)} %copy-done.20, bf16[4,64,512]{2,1,0:T(8,128)(2,1)} %copy-done.15, ...), custom_call_target="tpu_custom_call" | custom-call | bytes 1835 | tf_op jit(solution)/shard_map/place/pallas_call | solution.py:485
  (62 shorter events, 1.0 us)
Async XLA Ops:
  0.6 7.9 %copy-start = (bf16[16,256]{1,0:T(8,128)(2,1)S(1)}, bf16[16,256]{1,0:T(8,128)(2,1)}, u32[]{:S(2)}) copy-start(bf16[16,256]{1,0:T(8,128)(2,1)} %param.20) | copy-start | bytes 24580
  0.6 8.8 %collective-permute-start = (bf16[256,1024]{1,0:T(8,128)(2,1)}, bf16[256,1024]{1,0:T(8,128)(2,1)S(1)}, u32[]{:S(2)}, u32[]{:S(2)}) collective-permute-start(bf16[256,1024]{1,0:T(8,128)(2,1)} %refs_0_.1), channel_id=1, source_target_pairs={{0,1},{1,0},{2,3},{3,2},{4,5},{5,4},{6,7},{7,6},{8,9},{9,8},{10,11... | collective-permute-start | bytes 1572872 | tf_op jit(solution)/shard_map/ppermute | solution.py:42
  1.2 16.8 %collective-permute-start.1 = (bf16[256,1024]{1,0:T(8,128)(2,1)}, bf16[256,1024]{1,0:T(8,128)(2,1)S(1)}, u32[]{:S(2)}, u32[]{:S(2)}) collective-permute-start(bf16[256,1024]{1,0:T(8,128)(2,1)} %refs_0_.1), channel_id=1, source_target_pairs={{0,2},{1,3},{2,0},{3,1},{4,6},{5,7},{6,4},{7,5},{8,10},{9,11},{10,... | collective-permute-start | bytes 1572872 | tf_op jit(solution)/shard_map/ppermute | solution.py:42
  3.8 14.2 %collective-permute-start.2 = (bf16[256,1024]{1,0:T(8,128)(2,1)}, bf16[256,1024]{1,0:T(8,128)(2,1)}, u32[]{:S(2)}, u32[]{:S(2)}) collective-permute-start(bf16[256,1024]{1,0:T(8,128)(2,1)} %refs_6_), channel_id=1, source_target_pairs={{0,1},{1,0},{2,3},{3,2},{4,5},{5,4},{6,7},{7,6},{8,9},{9,8},{10,11... | collective-permute-start | bytes 1572872 | tf_op jit(solution)/shard_map/ppermute | solution.py:42
  9.4 1.0 %copy-start.2 = (bf16[256,1024]{1,0:T(8,128)(2,1)S(1)}, bf16[256,1024]{1,0:T(8,128)(2,1)}, u32[]{:S(2)}) copy-start(bf16[256,1024]{1,0:T(8,128)(2,1)} %refs_0_.1) | copy-start | bytes 1572868
  10.5 0.7 copy-start.8
  11.1 0.7 copy-start.9
  18.0 2.0 %collective-permute-start.3 = (bf16[256,1024]{1,0:T(8,128)(2,1)S(1)}, bf16[256,1024]{1,0:T(8,128)(2,1)S(1)}, u32[]{:S(2)}, u32[]{:S(2)}) collective-permute-start(bf16[256,1024]{1,0:T(8,128)(2,1)S(1)} %collective-permute-done.1.refs_3_), channel_id=1, source_target_pairs={{0,1},{1,0},{2,3},{3,2},{4,5},{5,4},{6,7},{7,6},{8,9},{9,8},{10,11... | collective-permute-start | bytes 1572872 | tf_op jit(solution)/shard_map/ppermute | solution.py:42
  20.0 33.1 %copy-start.10 = (s32[128]{0:T(128)S(1)}, s32[128]{0:T(128)}, u32[]{:S(2)}) copy-start(s32[128]{0:T(128)} %refs_2_.1) | copy-start | bytes 1540
  26.6 0.7 copy-start.4
  27.3 0.7 copy-start.5
  28.0 0.8 copy-start.11
  28.7 0.7 copy-start.12
  29.4 0.7 copy-start.13
  30.1 11.4 %collective-permute-start.4 = (bf16[2,256,384]{2,1,0:T(8,128)(2,1)S(1)}, bf16[2,256,384]{2,1,0:T(8,128)(2,1)S(1)}, u32[]{:S(2)}, u32[]{:S(2)}) collective-permute-start(bf16[2,256,384]{2,1,0:T(8,128)(2,1)S(1)} %get-tuple-element.56.own_ref), channel_id=1, source_target_pairs={{0,4},{4,0},{8,12},{12,8},{16,20},{20,16},{24,28},{28,24},{1,5},{5... | collective-permute-start | bytes 1179656 | tf_op jit(solution)/shard_map/ppermute | solution.py:42
  31.6 16.8 %collective-permute-start.8 = (bf16[256,1024]{1,0:T(8,128)(2,1)}, bf16[256,1024]{1,0:T(8,128)(2,1)S(1)}, u32[]{:S(2)}, u32[]{:S(2)}) collective-permute-start(bf16[256,1024]{1,0:T(8,128)(2,1)} %refs_6_), channel_id=1, source_target_pairs={{0,2},{1,3},{2,0},{3,1},{4,6},{5,7},{6,4},{7,5},{8,10},{9,11},{10,... | collective-permute-start | bytes 1572872 | tf_op jit(solution)/shard_map/ppermute | solution.py:42
  32.1 15.3 %collective-permute-start.6 = (bf16[2,64,512]{2,1,0:T(8,128)(2,1)}, bf16[2,64,512]{2,1,0:T(8,128)(2,1)S(1)}, u32[]{:S(2)}, u32[]{:S(2)}) collective-permute-start(bf16[2,64,512]{2,1,0:T(8,128)(2,1)} %copy-done.13), channel_id=1, source_target_pairs={{0,16},{4,20},{8,24},{12,28},{16,0},{20,4},{24,8},{28,12},{1,17},{... | collective-permute-start | bytes 393224 | tf_op jit(solution)/shard_map/ppermute | solution.py:42
  34.7 12.8 %collective-permute-start.7 = (bf16[2,64,512]{2,1,0:T(8,128)(2,1)}, bf16[2,64,512]{2,1,0:T(8,128)(2,1)S(1)}, u32[]{:S(2)}, u32[]{:S(2)}) collective-permute-start(bf16[2,64,512]{2,1,0:T(8,128)(2,1)} %copy-done.12), channel_id=1, source_target_pairs={{0,24},{4,28},{8,16},{12,20},{16,8},{20,12},{24,0},{28,4},{1,25},{... | collective-permute-start | bytes 393224 | tf_op jit(solution)/shard_map/ppermute | solution.py:42
  42.3 6.0 %collective-permute-start.5 = (bf16[2,256,128]{2,1,0:T(8,128)(2,1)S(1)}, bf16[2,256,128]{2,1,0:T(8,128)(2,1)S(1)}, u32[]{:S(2)}, u32[]{:S(2)}) collective-permute-start(bf16[2,256,128]{2,1,0:T(8,128)(2,1)S(1)} %get-tuple-element.60.b_ref), channel_id=1, source_target_pairs={{0,8},{4,12},{8,16},{12,20},{16,24},{20,28},{1,9},{5,13},{9,17},{1... | collective-permute-start | bytes 393224 | tf_op jit(solution)/shard_map/ppermute | solution.py:588
  45.9 14.5 %collective-permute-start.11 = (bf16[8,64,512]{2,1,0:T(8,128)(2,1)}, bf16[8,64,512]{2,1,0:T(8,128)(2,1)S(1)}, u32[]{:S(2)}, u32[]{:S(2)}) collective-permute-start(bf16[8,64,512]{2,1,0:T(8,128)(2,1)} %copy-done.11), channel_id=1, source_target_pairs={{0,4},{4,0},{8,12},{12,8},{16,20},{20,16},{24,28},{28,24},{1,5},{5... | collective-permute-start | bytes 1572872 | tf_op jit(solution)/shard_map/ppermute | solution.py:42
  47.4 10.9 %copy-start.19 = (bf16[2,64,512]{2,1,0:T(8,128)(2,1)}, bf16[2,64,512]{2,1,0:T(8,128)(2,1)S(1)}, u32[]{:S(2)}) copy-start(bf16[2,64,512]{2,1,0:T(8,128)(2,1)S(1)} %collective-permute-done.6.refs_2_) | copy-start | bytes 393220
  47.4 10.9 %copy-start.20 = (bf16[2,64,512]{2,1,0:T(8,128)(2,1)}, bf16[2,64,512]{2,1,0:T(8,128)(2,1)S(1)}, u32[]{:S(2)}) copy-start(bf16[2,64,512]{2,1,0:T(8,128)(2,1)S(1)} %collective-permute-done.7.refs_3_) | copy-start | bytes 393220
  48.3 10.0 %copy-start.14 = (bf16[256,1024]{1,0:T(8,128)(2,1)}, bf16[256,1024]{1,0:T(8,128)(2,1)S(1)}, u32[]{:S(2)}) copy-start(bf16[256,1024]{1,0:T(8,128)(2,1)S(1)} %collective-permute-done.8.refs_8_) | copy-start | bytes 1572868
  48.5 6.9 %collective-permute-start.9 = (bf16[2,256,128]{2,1,0:T(8,128)(2,1)S(1)}, bf16[2,256,128]{2,1,0:T(8,128)(2,1)S(1)}, u32[]{:S(2)}, u32[]{:S(2)}) collective-permute-start(bf16[2,256,128]{2,1,0:T(8,128)(2,1)S(1)} %step.1), channel_id=1, source_target_pairs={{0,8},{4,12},{8,16},{12,20},{16,24},{20,28},{1,9},{5,13},{9,17},{1... | collective-permute-start | bytes 393224 | tf_op jit(solution)/shard_map/ppermute | solution.py:588
  53.4 16.6 %collective-permute-start.14 = (bf16[256,1024]{1,0:T(8,128)(2,1)S(1)}, bf16[256,1024]{1,0:T(8,128)(2,1)}, u32[]{:S(2)}, u32[]{:S(2)}) collective-permute-start(bf16[256,1024]{1,0:T(8,128)(2,1)S(1)} %collective-permute-done.8.refs_8_), channel_id=1, source_target_pairs={{0,1},{1,0},{2,3},{3,2},{4,5},{5,4},{6,7},{7,6},{8,9},{9,8},{10,11... | collective-permute-start | bytes 1572872 | tf_op jit(solution)/shard_map/ppermute | solution.py:42
  55.4 4.9 %copy-start.6 = (bf16[2,64,512]{2,1,0:T(8,128)(2,1)S(1)}, bf16[2,64,512]{2,1,0:T(8,128)(2,1)}, u32[]{:S(2)}) copy-start(bf16[2,64,512]{2,1,0:T(8,128)(2,1)} %copy-done.5) | copy-start | bytes 393220
  58.3 3.2 %copy-start.3 = (bf16[256,256]{1,0:T(8,128)(2,1)}, bf16[256,256]{1,0:T(8,128)(2,1)S(1)}, u32[]{:S(2)}) copy-start(bf16[256,256]{1,0:T(8,128)(2,1)S(1)} %get-tuple-element.67.refs_2_) | copy-start | bytes 393220
  58.3 3.8 %collective-permute-start.10 = (bf16[256,256]{1,0:T(8,128)(2,1)S(1)}, bf16[256,256]{1,0:T(8,128)(2,1)S(1)}, u32[]{:S(2)}, u32[]{:S(2)}) collective-permute-start(bf16[256,256]{1,0:T(8,128)(2,1)S(1)} %get-tuple-element.68), channel_id=1, source_target_pairs={{0,1},{1,0},{2,3},{3,2},{4,5},{5,4},{6,7},{7,6},{8,9},{9,8},{10,11... | collective-permute-start | bytes 393224 | tf_op jit(solution)/shard_map/ppermute | solution.py:42
  58.4 8.8 %collective-permute-start.12 = (bf16[256,256]{1,0:T(8,128)(2,1)S(1)}, bf16[256,256]{1,0:T(8,128)(2,1)S(1)}, u32[]{:S(2)}, u32[]{:S(2)}) collective-permute-start(bf16[256,256]{1,0:T(8,128)(2,1)S(1)} %get-tuple-element.76), channel_id=1, source_target_pairs={{0,2},{1,3},{2,0},{3,1},{4,6},{5,7},{6,4},{7,5},{8,10},{9,11},{10,... | collective-permute-start | bytes 393224 | tf_op jit(solution)/shard_map/ppermute | solution.py:42
  60.0 10.1 %collective-permute-start.13 = (bf16[256,256]{1,0:T(8,128)(2,1)S(1)}, bf16[256,256]{1,0:T(8,128)(2,1)S(1)}, u32[]{:S(2)}, u32[]{:S(2)}) collective-permute-start(bf16[256,256]{1,0:T(8,128)(2,1)S(1)} %get-tuple-element.77), channel_id=1, source_target_pairs={{0,3},{1,2},{2,1},{3,0},{4,7},{5,6},{6,5},{7,4},{8,11},{9,10},{10,... | collective-permute-start | bytes 393224 | tf_op jit(solution)/shard_map/ppermute | solution.py:42
  61.5 0.7 copy-start.7
  62.1 7.9 %copy-start.16 = (bf16[256,256]{1,0:T(8,128)(2,1)}, bf16[256,256]{1,0:T(8,128)(2,1)S(1)}, u32[]{:S(2)}) copy-start(bf16[256,256]{1,0:T(8,128)(2,1)S(1)} %collective-permute-done.10.refs_3_) | copy-start | bytes 393220
  62.1 19.2 %collective-permute-start.15 = (bf16[4,64,512]{2,1,0:T(8,128)(2,1)S(1)}, bf16[4,64,512]{2,1,0:T(8,128)(2,1)S(1)}, u32[]{:S(2)}, u32[]{:S(2)}) collective-permute-start(bf16[4,64,512]{2,1,0:T(8,128)(2,1)S(1)} %get-tuple-element.84), channel_id=1, source_target_pairs={{0,8},{4,12},{8,0},{12,4},{16,24},{20,28},{24,16},{28,20},{1,9},{5... | collective-permute-start | bytes 786440 | tf_op jit(solution)/shard_map/ppermute | solution.py:42
  64.6 16.7 %collective-permute-start.16 = (bf16[2,64,512]{2,1,0:T(8,128)(2,1)S(1)}, bf16[2,64,512]{2,1,0:T(8,128)(2,1)S(1)}, u32[]{:S(2)}, u32[]{:S(2)}) collective-permute-start(bf16[2,64,512]{2,1,0:T(8,128)(2,1)S(1)} %get-tuple-element.85), channel_id=1, source_target_pairs={{0,16},{4,20},{8,24},{12,28},{16,0},{20,4},{24,8},{28,12},{1,17},{... | collective-permute-start | bytes 393224 | tf_op jit(solution)/shard_map/ppermute | solution.py:42
  67.2 2.9 %copy-start.17 = (bf16[256,256]{1,0:T(8,128)(2,1)}, bf16[256,256]{1,0:T(8,128)(2,1)S(1)}, u32[]{:S(2)}) copy-start(bf16[256,256]{1,0:T(8,128)(2,1)S(1)} %collective-permute-done.12.refs_4_) | copy-start | bytes 393220
  67.2 14.1 %collective-permute-start.17 = (bf16[2,64,512]{2,1,0:T(8,128)(2,1)S(1)}, bf16[2,64,512]{2,1,0:T(8,128)(2,1)S(1)}, u32[]{:S(2)}, u32[]{:S(2)}) collective-permute-start(bf16[2,64,512]{2,1,0:T(8,128)(2,1)S(1)} %get-tuple-element.86), channel_id=1, source_target_pairs={{0,24},{4,28},{8,16},{12,20},{16,8},{20,12},{24,0},{28,4},{1,25},{... | collective-permute-start | bytes 393224 | tf_op jit(solution)/shard_map/ppermute | solution.py:42
  70.1 0.7 copy-start.18
  70.7 14.2 %copy-start.1 = (bf16[16,256]{1,0:T(8,128)(2,1)S(1)}, bf16[16,256]{1,0:T(8,128)(2,1)}, u32[]{:S(2)}) copy-start(bf16[16,256]{1,0:T(8,128)(2,1)} %param.20) | copy-start | bytes 24580
  81.3 0.6 copy-start.21
  81.3 0.7 copy-start.22
  81.3 0.8 copy-start.15

commit v2 on v1

--- a/solution.py
+++ b/solution.py
@@ -465,8 +465,7 @@
     sources, (out_ref, stage, sem_in, sem_out) = refs[:-4], refs[-4:]
     into, out = [], []
     for source, held in zip(sources, slots):
-        for i in range(source.shape[0]):
-            n = held[i]
+        for i, n in enumerate(held):
             into.append(pltpu.make_async_copy(source.at[i], stage.at[n], sem_in.at[n]))
             out.append(pltpu.make_async_copy(stage.at[n], out_ref.at[rows_ref[n]], sem_out.at[n]))
     for one in into:
@@ -560,7 +559,7 @@
         if g > 0:
             far[g - 1], pairs[0]["map"], w_core = lax.optimization_barrier((far[g - 1], pairs[0]["map"], w_core))
             xs[g] = [far[g - 1], [exchange(part, "head", 1) for part in far[g - 1]]]
-        pairs.append(pair_call(meta, flat, block_table if g == 0 else pairs[0]["total"], xs[g], gain, w, gates, initial, 2 * g, pairs, g == groups - 1, (half,) + (per_owner,) * line))
+        pairs.append(pair_call(meta, flat, block_table if g == 0 else pairs[0]["total"], xs[g], gain, w, gates, initial, 2 * g, pairs, g == groups - 1, (half,) + (per_owner,) * (line // 2) + (half // 2,)))
     total, block_table, w_out = lax.optimization_barrier((pairs[-1]["total"], block_table, w_out))
     w_outs_far = [exchange(w_out, "head", 2 * g) for g in range(1, groups)]
     got = exchange(total, "seq", 1)
@@ -576,8 +575,8 @@
     landed = (arrival.reshape(1, -1) == slots[:, None]) & to_me.reshape(1, -1)
     rows = jnp.sum(jnp.where(landed, (block_table % blocks_here)[None, :], 0), axis=1).astype(int32)
 
-    cross, home, *same = pairs[-1]["kv"]
-    far_same = [exchange(same[m - 1], "seq", 2 * m) for m in early]
+    cross, home, *same, far_same = pairs[-1]["kv"]
+    far_same = exchange(far_same, "seq", line)
     a, b = join(meta, total, got)
     b, cross = lax.optimization_barrier((b, cross))
     cross = exchange(cross, "seq", 1)
@@ -593,8 +592,8 @@
     w_outs = [w_out, w_core] + [w for one in w_outs_far for w in (one, exchange(one, "head", 1))]
     cut = lambda m: (0, m * per_owner, per_owner)
     regrouped = regroup(
-        [cross] + [same[m - 1] for m in others],
-        [[(1 + i, 0, per_owner), cut(m)] for i, m in enumerate(others)] + [[cut(m)] for m in early] + [[cut(0)]],
+        [cross, far_same] + same,
+        [[(1 + m, 0, per_owner), cut(m), (1, m * per_owner, per_owner)] for m in others] + [[cut(m)] for m in early] + [[cut(0)]],
     )
     regrouped = list(regrouped)
     retrieved = list(recall(meta, got, state, pairs))
@@ -602,11 +601,11 @@
     pieces[1], regrouped = lax.optimization_barrier((pieces[1], regrouped))
     arrived = [exchange(one, "seq", 2 * m) for one, m in zip(regrouped, others + early)]
     mixed = ffn(tokens, ffn_gain.reshape(1, -1), w_outs, pieces, w_gate, w_up, w_down)
-    held = [regrouped[-1], home] + far_same + arrived
+    held = [regrouped[-1], home, far_same] + arrived
     mixed, held = lax.optimization_barrier((mixed, held))
     of = lambda e, m: [e * half + m * per_owner + i for i in range(per_owner)]
-    taken = [of(0, 0), of(1, 0)] + [of(1, m) for m in early]
-    taken += [of(1, m) + of(0, m) for m in others] + [of(0, m) for m in early]
+    taken = [of(0, 0), of(1, 0), of(1, line // 2)]
+    taken += [of(1, m) + of(0, m) + of(1, m + line // 2) for m in others] + [of(0, m) for m in early]
     return mixed, place(rows, held, taken)
 
 

time: 85.6 us -> 83.8 us (0.979)
  waiting for transfers between devices: 9.81 us -> 12.7 us
  local copies, waits for them, and re-layouts: 11.6 us -> 9.04 us
  starting transfers between devices: 28.3 us -> 26.5 us
    unnamed x47 -> x37, local copies, waits for them, and re-layouts: 9.63 us -> 7.07 us
    ppermute x16 -> x15, waiting for transfers between devices: 7.03 us -> 9.45 us  [exchange(): return lax.ppermute(value, axis, [(i, i ^ bit) for i in range(count)])]
    ppermute x16 -> x15, starting transfers between devices: 20.3 us -> 18.4 us  [exchange(): return lax.ppermute(value, axis, [(i, i ^ bit) for i in range(count)])]
  transfers between devices with their start and end apart: 18 -> 17, of which waited for: 4 -> 6; matrix products, arithmetic and copies ran while one was open for 8% -> 8% of each run, Pallas kernels for 26% -> 26%
where the time goes in v2:
time: 83.8 us; the launch traced here: 83.3 us
  Pallas kernels  31.1 us (37%)
  starting transfers between devices  26.5 us (32%)
  waiting for transfers between devices  12.7 us (15%)
  local copies, waits for them, and re-layouts  9.04 us (11%)
  other arithmetic  1.99 us (2%)
  between operations  1.05 us (1%)
  matrix products  0.91 us (1%)
    ppermute x15, starting transfers between devices, exchange(): return lax.ppermute(value, axis, [(i, i ^ bit) for i in range(count)])  18.4 us
    pallas_call x2, Pallas kernels, pair_call(): pl.pallas_call(functools.partial(pair_kernel, heads, d, blocks, rel, is_l...  12.5 us
    pallas_call x1, Pallas kernels, ffn(): pl.pallas_call(functools.partial(ffn_kernel, shards, tile), out_shape=jax...  10.5 us
    ppermute x15, waiting for transfers between devices, exchange(): return lax.ppermute(value, axis, [(i, i ^ bit) for i in range(count)])  9.45 us
    ppermute x2, starting transfers between devices, per_device(): state = lax.ppermute(state, 'seq', onward)  8.07 us
    unnamed x37, local copies, waits for them, and re-layouts  7.07 us
    ppermute x2, waiting for transfers between devices, per_device(): state = lax.ppermute(state, 'seq', onward)  3.26 us
    pallas_call x1, Pallas kernels, recall(): pl.pallas_call(functools.partial(recall_kernel, heads, d, groups), out_sh...  2.86 us
  transfers between devices with their start and end apart: 17, of which 6 were waited for; matrix products, arithmetic and copies ran while one was open for 8% of the time, Pallas kernels for 26%

profile of v2, /device:TPU:0, one launch (start us, length us, event | category | flops | bytes accessed | tf_op | source)
XLA Modules:
  0.0 83.3 jit_solution(11773003678178431981)
XLA Ops:
  0.6 0.5 collective-permute-start
  1.2 2.6 %collective-permute-start.1 = (bf16[256,1024]{1,0:T(8,128)(2,1)}, bf16[256,1024]{1,0:T(8,128)(2,1)S(1)}, u32[]{:S(2)}, u32[]{:S(2)}) collective-permute-start(bf16[256,1024]{1,0:T(8,128)(2,1)} %refs_0_.1), channel_id=1, source_target_pairs={{0,2},{1,3},{2,0},{3,1},{4,6},{5,7},{6,4},{7,5},{8,10},{9,11},{10,... | collective-permute-start | bytes 1572872 | tf_op jit(solution)/shard_map/ppermute | solution.py:42
  3.8 0.2 collective-permute-start.2
  3.9 0.8 reshape.91
  4.8 0.1 fusion
  4.9 1.7 %copy.38 = bf16[128,8,2,384]{3,1,2,0:T(8,128)(2,1)S(1)} copy(bf16[128,8,2,384]{3,2,1,0:T(2,128)(2,1)} %bitcast.26) | data formatting | bytes 3145728
  6.6 0.7 copy.31
  7.3 0.2 copy.34.refs_7_
  7.7 0.7 pad_maximum_fusion.refs_1_
  8.5 0.9 %convolution_multiply_fusion.refs_8_ = f32[2,128,128]{2,1,0:T(8,128)S(1)} fusion(bf16[16,256]{1,0:T(8,128)(2,1)S(1)} %copy-done, bf16[16,256]{1,0:T(8,128)(2,1)} %param.19), kind=kOutput, calls=%fused_computation | convolution fusion | flops 1081344 | bytes 147456 | tf_op jit(solution)/shard_map/phd,phe->hde/dot_general | solution.py:554
  9.4 1.0 %copy-done.2 = bf16[256,1024]{1,0:T(8,128)(2,1)S(1)} copy-done((bf16[256,1024]{1,0:T(8,128)(2,1)S(1)}, bf16[256,1024]{1,0:T(8,128)(2,1)}, u32[]{:S(2)}) %copy-start.2) | copy-done | bytes 524312
  10.5 0.7 copy-done.7
  11.1 0.7 copy-done.8
  11.8 6.2 %pair_first.1 = (bf16[112,2,256,512]{3,2,1,0:T(8,128)(2,1)}, bf16[2,256,384]{2,1,0:T(8,128)(2,1)S(1)}, bf16[8,64,512]{2,1,0:T(8,128)(2,1)S(1)}, s32[16]{0:T(128)S(1)}) custom-call(s32[2]{0:T(128)S(1)} %pad_add_fusion.refs_0_.meta_ref, f32[20]{0:T(128)S(1)} %pad_maximum_fusion.refs_1_, s32[128]{0:T(128)S(1)} %copy-done.8, bf16[256,1024]{1,0:T(8,128)(2,1)S(1)} %copy-done.2, ...), custom_call_target="tpu_custom_call" | custom-call | flops 2500000 | bytes 8000 | tf_op jit(solution)/shard_map/pair_first/pallas_call | solution.py:226
  18.0 0.4 collective-permute-start.3
  18.4 1.6 %collective-permute-done.3.refs_4_ = bf16[256,1024]{1,0:T(8,128)(2,1)S(1)} collective-permute-done((bf16[256,1024]{1,0:T(8,128)(2,1)S(1)}, bf16[256,1024]{1,0:T(8,128)(2,1)S(1)}, u32[]{:S(2)}, u32[]{:S(2)}) %collective-permute-start.3) | collective-permute-done | bytes 524320 | tf_op jit(solution)/shard_map/ppermute | solution.py:42
  20.0 6.3 %pair_last.1 = (bf16[112,2,256,512]{3,2,1,0:T(8,128)(2,1)}, bf16[2,256,384]{2,1,0:T(8,128)(2,1)S(1)}, bf16[8,64,512]{2,1,0:T(8,128)(2,1)S(1)}, bf16[2,64,512]{2,...) custom-call(s32[2]{0:T(128)S(1)} %pad_add_fusion.refs_0_.meta_ref, ...), custom_call_target="tpu_custom_call", output_to_operand_aliasing={{0}: (11, {})} | custom-call | flops 2500000 | bytes 8000 | tf_op jit(solution)/shard_map/pair_last/pallas_call | solution.py:226
  26.3 1.6 %collective-permute-start.4 = (bf16[2,256,384]{2,1,0:T(8,128)(2,1)S(1)}, bf16[2,256,384]{2,1,0:T(8,128)(2,1)S(1)}, u32[]{:S(2)}, u32[]{:S(2)}) collective-permute-start(bf16[2,256,384]{2,1,0:T(8,128)(2,1)S(1)} %get-tuple-element.53.own_ref), channel_id=1, source_target_pairs={{0,4},{4,0},{8,12},{12,8},{16,20},{20,16},{24,28},{28,24},{1,5},{5... | collective-permute-start | bytes 1179656 | tf_op jit(solution)/shard_map/ppermute | solution.py:42
  27.9 0.5 collective-permute-start.7
  28.4 2.6 %collective-permute-start.6 = (bf16[4,64,512]{2,1,0:T(8,128)(2,1)S(1)}, bf16[4,64,512]{2,1,0:T(8,128)(2,1)S(1)}, u32[]{:S(2)}, u32[]{:S(2)}) collective-permute-start(bf16[4,64,512]{2,1,0:T(8,128)(2,1)S(1)} %get-tuple-element.58), channel_id=1, source_target_pairs={{0,16},{4,20},{8,24},{12,28},{16,0},{20,4},{24,8},{28,12},{1,17},{... | collective-permute-start | bytes 786440 | tf_op jit(solution)/shard_map/ppermute | solution.py:42
  31.0 6.8 %collective-permute-done.4.got_ref.refs_1_ = bf16[2,256,384]{2,1,0:T(8,128)(2,1)S(1)} collective-permute-done((bf16[2,256,384]{2,1,0:T(8,128)(2,1)S(1)}, bf16[2,256,384]{2,1,0:T(8,128)(2,1)S(1)}, u32[]{:S(2)}, u32[]{:S(2)}) %collective-permute-start.4) | collective-permute-done | bytes 393248 | tf_op jit(solution)/shard_map/ppermute | solution.py:42
  37.8 0.9 %join.1 = (bf16[2,256,256]{2,1,0:T(8,128)(2,1)S(1)}, bf16[2,256,128]{2,1,0:T(8,128)(2,1)S(1)}) custom-call(s32[2]{0:T(128)S(1)} %pad_add_fusion.refs_0_.meta_ref, bf16[2,256,384]{2,1,0:T(8,128)(2,1)S(1)} %get-tuple-element.53.own_ref, bf16[2,256,384]{2,1,0:T(8,128)(2,1)S(1)} %collective-permute-done.4.got_ref.refs_1_), custom_call_target="tpu_custom_call" | custom-call | flops 100000 | bytes 1200 | tf_op jit(solution)/shard_map/join/pallas_call | solution.py:258
  38.7 3.5 %collective-permute-start.5 = (bf16[2,256,128]{2,1,0:T(8,128)(2,1)S(1)}, bf16[2,256,128]{2,1,0:T(8,128)(2,1)S(1)}, u32[]{:S(2)}, u32[]{:S(2)}) collective-permute-start(bf16[2,256,128]{2,1,0:T(8,128)(2,1)S(1)} %get-tuple-element.57.b_ref), channel_id=1, source_target_pairs={{0,8},{4,12},{8,16},{12,20},{16,24},{20,28},{1,9},{5,13},{9,17},{1... | collective-permute-start | bytes 393224 | tf_op jit(solution)/shard_map/ppermute | solution.py:587
  42.1 1.6 %collective-permute-start.10 = (bf16[8,64,512]{2,1,0:T(8,128)(2,1)}, bf16[8,64,512]{2,1,0:T(8,128)(2,1)S(1)}, u32[]{:S(2)}, u32[]{:S(2)}) collective-permute-start(bf16[8,64,512]{2,1,0:T(8,128)(2,1)} %copy-done.10), channel_id=1, source_target_pairs={{0,4},{4,0},{8,12},{12,8},{16,20},{20,16},{24,28},{28,24},{1,5},{5... | collective-permute-start | bytes 1572872 | tf_op jit(solution)/shard_map/ppermute | solution.py:42
  43.7 1.0 %collective-permute-done.5.state_ref = bf16[2,256,128]{2,1,0:T(8,128)(2,1)S(1)} collective-permute-done((bf16[2,256,128]{2,1,0:T(8,128)(2,1)S(1)}, bf16[2,256,128]{2,1,0:T(8,128)(2,1)S(1)}, u32[]{:S(2)}, u32[]{:S(2)}) %collective-permute-start.5) | collective-permute-done | bytes 131104 | tf_op jit(solution)/shard_map/ppermute | solution.py:587
  44.7 0.2 step.1
  44.9 4.6 %collective-permute-start.8 = (bf16[2,256,128]{2,1,0:T(8,128)(2,1)S(1)}, bf16[2,256,128]{2,1,0:T(8,128)(2,1)S(1)}, u32[]{:S(2)}, u32[]{:S(2)}) collective-permute-start(bf16[2,256,128]{2,1,0:T(8,128)(2,1)S(1)} %step.1), channel_id=1, source_target_pairs={{0,8},{4,12},{8,16},{12,20},{16,24},{20,28},{1,9},{5,13},{9,17},{1... | collective-permute-start | bytes 393224 | tf_op jit(solution)/shard_map/ppermute | solution.py:587
  49.5 2.3 %collective-permute-done.8.refs_2_ = bf16[2,256,128]{2,1,0:T(8,128)(2,1)S(1)} collective-permute-done((bf16[2,256,128]{2,1,0:T(8,128)(2,1)S(1)}, bf16[2,256,128]{2,1,0:T(8,128)(2,1)S(1)}, u32[]{:S(2)}, u32[]{:S(2)}) %collective-permute-start.8) | collective-permute-done | bytes 131104 | tf_op jit(solution)/shard_map/ppermute | solution.py:587
  51.8 2.9 %recall.1 = (bf16[256,256]{1,0:T(8,128)(2,1)S(1)}, bf16[256,256]{1,0:T(8,128)(2,1)S(1)}, bf16[256,256]{1,0:T(8,128)(2,1)S(1)}, bf16[256,256]{1,0:T(8,128)(2,1)S(1)}) custom-call(s32[2]{0:T(128)S(1)} %pad_add_fusion.refs_0_.meta_ref, bf16[2,256,384]{2,1,0:T(8,128)(2,1)S(1)} %collective-permute-done.4.got_ref.refs_1_, ...), custom_call_target="tpu_custom_call" | custom-call | flops 200000 | bytes 3000 | tf_op jit(solution)/shard_map/recall/pallas_call | solution.py:332
  54.7 0.6 copy-done.4
  55.4 0.2 convert_reduce_fusion
  55.7 0.6 collective-permute-start.13
  56.3 1.0 %collective-permute-start.11 = (bf16[256,256]{1,0:T(8,128)(2,1)S(1)}, bf16[256,256]{1,0:T(8,128)(2,1)S(1)}, u32[]{:S(2)}, u32[]{:S(2)}) collective-permute-start(bf16[256,256]{1,0:T(8,128)(2,1)S(1)} %get-tuple-element.73), channel_id=1, source_target_pairs={{0,2},{1,3},{2,0},{3,1},{4,6},{5,7},{6,4},{7,5},{8,10},{9,11},{10,... | collective-permute-start | bytes 393224 | tf_op jit(solution)/shard_map/ppermute | solution.py:42
  57.2 1.3 %regroup.1 = (bf16[6,64,512]{2,1,0:T(8,128)(2,1)S(1)}, bf16[2,64,512]{2,1,0:T(8,128)(2,1)S(1)}, bf16[2,64,512]{2,1,0:T(8,128)(2,1)S(1)}, bf16[2,64,512]{2,1,0:T(8,128)(2,1)S(1)}) custom-call(bf16[8,64,512]{2,1,0:T(8,128)(2,1)S(1)} %collective-permute-done.10.refs_0_, bf16[4,64,512]{2,1,0:T(8,128)(2,1)S(1)} %collective-permute-done.6.refs_1_.refs_2_, ...), custom_call_target="tpu_custom_call" | custom-call | bytes 4000 | tf_op jit(solution)/shard_map/regroup/pallas_call | solution.py:448
  58.6 0.6 copy-done.6
  59.2 2.5 %collective-permute-start.14 = (bf16[6,64,512]{2,1,0:T(8,128)(2,1)S(1)}, bf16[6,64,512]{2,1,0:T(8,128)(2,1)S(1)}, u32[]{:S(2)}, u32[]{:S(2)}) collective-permute-start(bf16[6,64,512]{2,1,0:T(8,128)(2,1)S(1)} %get-tuple-element.79), channel_id=1, source_target_pairs={{0,8},{4,12},{8,0},{12,4},{16,24},{20,28},{24,16},{28,20},{1,9},{5... | collective-permute-start | bytes 1179656 | tf_op jit(solution)/shard_map/ppermute | solution.py:42
  61.8 0.1 collective-permute-start.12
  61.9 3.2 %collective-permute-start.15 = (bf16[2,64,512]{2,1,0:T(8,128)(2,1)S(1)}, bf16[2,64,512]{2,1,0:T(8,128)(2,1)S(1)}, u32[]{:S(2)}, u32[]{:S(2)}) collective-permute-start(bf16[2,64,512]{2,1,0:T(8,128)(2,1)S(1)} %get-tuple-element.80), channel_id=1, source_target_pairs={{0,16},{4,20},{8,24},{12,28},{16,0},{20,4},{24,8},{28,12},{1,17},{... | collective-permute-start | bytes 393224 | tf_op jit(solution)/shard_map/ppermute | solution.py:42
  65.1 1.1 %collective-permute-start.16 = (bf16[2,64,512]{2,1,0:T(8,128)(2,1)S(1)}, bf16[2,64,512]{2,1,0:T(8,128)(2,1)S(1)}, u32[]{:S(2)}, u32[]{:S(2)}) collective-permute-start(bf16[2,64,512]{2,1,0:T(8,128)(2,1)S(1)} %get-tuple-element.81), channel_id=1, source_target_pairs={{0,24},{4,28},{8,16},{12,20},{16,8},{20,12},{24,0},{28,4},{1,25},{... | collective-permute-start | bytes 393224 | tf_op jit(solution)/shard_map/ppermute | solution.py:42
  66.3 0.6 select_reduce_fusion.rows_ref
  67.0 0.3 collective-permute-done.12.refs_5_
  67.3 0.6 copy-done.15
  67.9 0.2 copy-done.11
  68.1 10.5 %ffn.1 = bf16[256,1024]{1,0:T(8,128)(2,1)} custom-call(bf16[256,1024]{1,0:T(8,128)(2,1)} %refs_0_.1, f32[1,1024]{1,0:T(1,128)} %bitcast.28, bf16[256,256]{1,0:T(8,128)(2,1)} %copy-done.4, bf16[256,256]{1,0:T(8,128)(2,1)} %copy-done.13, bf16[256,256]{1,0:T(8,128)(2,1)} %copy-done.14, bf16[256,256]{1,0:T(8,128)(2,1)} %copy-done.15, bf16[256,1024]{1,0:T(8,128)(2,1)} %refs_6_, ...), custom_call_target="tpu_custom_call" | custom-call | flops 5000000 | bytes 22000 | tf_op jit(solution)/shard_map/ffn/pallas_call | solution.py:396
  78.7 0.8 collective-permute-done.16.refs_5_
  79.5 0.6 copy-done.17
  80.1 0.2 copy-done.12
  80.3 2.8 %place.1 = bf16[16,64,512]{2,1,0:T(8,128)(2,1)} custom-call(s32[16]{0:T(128)} %select_reduce_fusion.rows_ref, bf16[2,64,512]{2,1,0:T(8,128)(2,1)} %copy-done.6, bf16[2,64,512]{2,1,0:T(8,128)(2,1)} %copy-done.5, bf16[4,64,512]{2,1,0:T(8,128)(2,1)} %copy-done.3, bf16[6,64,512]{2,1,0:T(8,128)(2,1)} %copy-done.12, bf16[2,64,512]{2,1,0:T(8,128)(2,1)} %copy-done.16, ...), custom_call_target="tpu_custom_call" | custom-call | bytes 1572 | tf_op jit(solution)/shard_map/place/pallas_call | solution.py:484
  (50 shorter events, 0.6 us)
Async XLA Ops:
  0.6 7.9 %copy-start = (bf16[16,256]{1,0:T(8,128)(2,1)S(1)}, bf16[16,256]{1,0:T(8,128)(2,1)}, u32[]{:S(2)}) copy-start(bf16[16,256]{1,0:T(8,128)(2,1)} %param.20) | copy-start | bytes 24580
  0.6 8.8 %collective-permute-start = (bf16[256,1024]{1,0:T(8,128)(2,1)}, bf16[256,1024]{1,0:T(8,128)(2,1)S(1)}, u32[]{:S(2)}, u32[]{:S(2)}) collective-permute-start(bf16[256,1024]{1,0:T(8,128)(2,1)} %refs_0_.1), channel_id=1, source_target_pairs={{0,1},{1,0},{2,3},{3,2},{4,5},{5,4},{6,7},{7,6},{8,9},{9,8},{10,11... | collective-permute-start | bytes 1572872 | tf_op jit(solution)/shard_map/ppermute | solution.py:42
  1.2 16.8 %collective-permute-start.1 = (bf16[256,1024]{1,0:T(8,128)(2,1)}, bf16[256,1024]{1,0:T(8,128)(2,1)S(1)}, u32[]{:S(2)}, u32[]{:S(2)}) collective-permute-start(bf16[256,1024]{1,0:T(8,128)(2,1)} %refs_0_.1), channel_id=1, source_target_pairs={{0,2},{1,3},{2,0},{3,1},{4,6},{5,7},{6,4},{7,5},{8,10},{9,11},{10,... | collective-permute-start | bytes 1572872 | tf_op jit(solution)/shard_map/ppermute | solution.py:42
  3.8 14.2 %collective-permute-start.2 = (bf16[256,1024]{1,0:T(8,128)(2,1)}, bf16[256,1024]{1,0:T(8,128)(2,1)}, u32[]{:S(2)}, u32[]{:S(2)}) collective-permute-start(bf16[256,1024]{1,0:T(8,128)(2,1)} %refs_6_), channel_id=1, source_target_pairs={{0,1},{1,0},{2,3},{3,2},{4,5},{5,4},{6,7},{7,6},{8,9},{9,8},{10,11... | collective-permute-start | bytes 1572872 | tf_op jit(solution)/shard_map/ppermute | solution.py:42
  9.4 1.0 %copy-start.2 = (bf16[256,1024]{1,0:T(8,128)(2,1)S(1)}, bf16[256,1024]{1,0:T(8,128)(2,1)}, u32[]{:S(2)}) copy-start(bf16[256,1024]{1,0:T(8,128)(2,1)} %refs_0_.1) | copy-start | bytes 1572868
  10.5 0.7 copy-start.7
  11.1 0.7 copy-start.8
  18.0 2.0 %collective-permute-start.3 = (bf16[256,1024]{1,0:T(8,128)(2,1)S(1)}, bf16[256,1024]{1,0:T(8,128)(2,1)S(1)}, u32[]{:S(2)}, u32[]{:S(2)}) collective-permute-start(bf16[256,1024]{1,0:T(8,128)(2,1)S(1)} %collective-permute-done.1.refs_3_), channel_id=1, source_target_pairs={{0,1},{1,0},{2,3},{3,2},{4,5},{5,4},{6,7},{7,6},{8,9},{9,8},{10,11... | collective-permute-start | bytes 1572872 | tf_op jit(solution)/shard_map/ppermute | solution.py:42
  26.3 12.3 %copy-start.5 = (bf16[2,64,512]{2,1,0:T(8,128)(2,1)}, bf16[2,64,512]{2,1,0:T(8,128)(2,1)S(1)}, u32[]{:S(2)}) copy-start(bf16[2,64,512]{2,1,0:T(8,128)(2,1)S(1)} %get-tuple-element.85.refs_1_) | copy-start | bytes 393220
  26.3 12.3 %copy-start.10 = (bf16[8,64,512]{2,1,0:T(8,128)(2,1)}, bf16[8,64,512]{2,1,0:T(8,128)(2,1)S(1)}, u32[]{:S(2)}) copy-start(bf16[8,64,512]{2,1,0:T(8,128)(2,1)S(1)} %get-tuple-element.65) | copy-start | bytes 1572868
  26.3 11.4 %collective-permute-start.4 = (bf16[2,256,384]{2,1,0:T(8,128)(2,1)S(1)}, bf16[2,256,384]{2,1,0:T(8,128)(2,1)S(1)}, u32[]{:S(2)}, u32[]{:S(2)}) collective-permute-start(bf16[2,256,384]{2,1,0:T(8,128)(2,1)S(1)} %get-tuple-element.53.own_ref), channel_id=1, source_target_pairs={{0,4},{4,0},{8,12},{12,8},{16,20},{20,16},{24,28},{28,24},{1,5},{5... | collective-permute-start | bytes 1179656 | tf_op jit(solution)/shard_map/ppermute | solution.py:42
  27.9 16.8 %collective-permute-start.7 = (bf16[256,1024]{1,0:T(8,128)(2,1)}, bf16[256,1024]{1,0:T(8,128)(2,1)}, u32[]{:S(2)}, u32[]{:S(2)}) collective-permute-start(bf16[256,1024]{1,0:T(8,128)(2,1)} %refs_6_), channel_id=1, source_target_pairs={{0,2},{1,3},{2,0},{3,1},{4,6},{5,7},{6,4},{7,5},{8,10},{9,11},{10,... | collective-permute-start | bytes 1572872 | tf_op jit(solution)/shard_map/ppermute | solution.py:42
  28.4 15.3 %collective-permute-start.6 = (bf16[4,64,512]{2,1,0:T(8,128)(2,1)S(1)}, bf16[4,64,512]{2,1,0:T(8,128)(2,1)S(1)}, u32[]{:S(2)}, u32[]{:S(2)}) collective-permute-start(bf16[4,64,512]{2,1,0:T(8,128)(2,1)S(1)} %get-tuple-element.58), channel_id=1, source_target_pairs={{0,16},{4,20},{8,24},{12,28},{16,0},{20,4},{24,8},{28,12},{1,17},{... | collective-permute-start | bytes 786440 | tf_op jit(solution)/shard_map/ppermute | solution.py:42
  38.7 6.0 %collective-permute-start.5 = (bf16[2,256,128]{2,1,0:T(8,128)(2,1)S(1)}, bf16[2,256,128]{2,1,0:T(8,128)(2,1)S(1)}, u32[]{:S(2)}, u32[]{:S(2)}) collective-permute-start(bf16[2,256,128]{2,1,0:T(8,128)(2,1)S(1)} %get-tuple-element.57.b_ref), channel_id=1, source_target_pairs={{0,8},{4,12},{8,16},{12,20},{16,24},{20,28},{1,9},{5,13},{9,17},{1... | collective-permute-start | bytes 393224 | tf_op jit(solution)/shard_map/ppermute | solution.py:587
  42.1 15.1 %collective-permute-start.10 = (bf16[8,64,512]{2,1,0:T(8,128)(2,1)}, bf16[8,64,512]{2,1,0:T(8,128)(2,1)S(1)}, u32[]{:S(2)}, u32[]{:S(2)}) collective-permute-start(bf16[8,64,512]{2,1,0:T(8,128)(2,1)} %copy-done.10), channel_id=1, source_target_pairs={{0,4},{4,0},{8,12},{12,8},{16,20},{20,16},{24,28},{28,24},{1,5},{5... | collective-permute-start | bytes 1572872 | tf_op jit(solution)/shard_map/ppermute | solution.py:42
  43.7 13.5 %copy-start.3 = (bf16[4,64,512]{2,1,0:T(8,128)(2,1)}, bf16[4,64,512]{2,1,0:T(8,128)(2,1)S(1)}, u32[]{:S(2)}) copy-start(bf16[4,64,512]{2,1,0:T(8,128)(2,1)S(1)} %collective-permute-done.6.refs_1_.refs_2_) | copy-start | bytes 786436
  44.9 6.9 %collective-permute-start.8 = (bf16[2,256,128]{2,1,0:T(8,128)(2,1)S(1)}, bf16[2,256,128]{2,1,0:T(8,128)(2,1)S(1)}, u32[]{:S(2)}, u32[]{:S(2)}) collective-permute-start(bf16[2,256,128]{2,1,0:T(8,128)(2,1)S(1)} %step.1), channel_id=1, source_target_pairs={{0,8},{4,12},{8,16},{12,20},{16,24},{20,28},{1,9},{5,13},{9,17},{1... | collective-permute-start | bytes 393224 | tf_op jit(solution)/shard_map/ppermute | solution.py:587
  51.8 3.5 %copy-start.9 = (s32[128]{0:T(128)S(1)}, s32[128]{0:T(128)}, u32[]{:S(2)}) copy-start(s32[128]{0:T(128)} %refs_2_.1) | copy-start | bytes 1540
  54.7 0.7 copy-start.4
  55.3 3.9 %collective-permute-start.9 = (bf16[256,256]{1,0:T(8,128)(2,1)S(1)}, bf16[256,256]{1,0:T(8,128)(2,1)S(1)}, u32[]{:S(2)}, u32[]{:S(2)}) collective-permute-start(bf16[256,256]{1,0:T(8,128)(2,1)S(1)} %get-tuple-element.64), channel_id=1, source_target_pairs={{0,1},{1,0},{2,3},{3,2},{4,5},{5,4},{6,7},{7,6},{8,9},{9,8},{10,11... | collective-permute-start | bytes 393224 | tf_op jit(solution)/shard_map/ppermute | solution.py:42
  55.7 11.6 %collective-permute-start.13 = (bf16[256,1024]{1,0:T(8,128)(2,1)}, bf16[256,1024]{1,0:T(8,128)(2,1)S(1)}, u32[]{:S(2)}, u32[]{:S(2)}) collective-permute-start(bf16[256,1024]{1,0:T(8,128)(2,1)} %collective-permute-done.7.refs_8_), channel_id=1, source_target_pairs={{0,1},{1,0},{2,3},{3,2},{4,5},{5,4},{6,7},{7,6},{8,9},{9,8},{10,11... | collective-permute-start | bytes 1572872 | tf_op jit(solution)/shard_map/ppermute | solution.py:42
  56.3 8.9 %collective-permute-start.11 = (bf16[256,256]{1,0:T(8,128)(2,1)S(1)}, bf16[256,256]{1,0:T(8,128)(2,1)S(1)}, u32[]{:S(2)}, u32[]{:S(2)}) collective-permute-start(bf16[256,256]{1,0:T(8,128)(2,1)S(1)} %get-tuple-element.73), channel_id=1, source_target_pairs={{0,2},{1,3},{2,0},{3,1},{4,6},{5,7},{6,4},{7,5},{8,10},{9,11},{10,... | collective-permute-start | bytes 393224 | tf_op jit(solution)/shard_map/ppermute | solution.py:42
  58.6 0.7 copy-start.6
  59.2 8.1 %copy-start.13 = (bf16[256,256]{1,0:T(8,128)(2,1)}, bf16[256,256]{1,0:T(8,128)(2,1)S(1)}, u32[]{:S(2)}) copy-start(bf16[256,256]{1,0:T(8,128)(2,1)S(1)} %collective-permute-done.9.refs_3_) | copy-start | bytes 393220
  59.2 20.3 %collective-permute-start.14 = (bf16[6,64,512]{2,1,0:T(8,128)(2,1)S(1)}, bf16[6,64,512]{2,1,0:T(8,128)(2,1)S(1)}, u32[]{:S(2)}, u32[]{:S(2)}) collective-permute-start(bf16[6,64,512]{2,1,0:T(8,128)(2,1)S(1)} %get-tuple-element.79), channel_id=1, source_target_pairs={{0,8},{4,12},{8,0},{12,4},{16,24},{20,28},{24,16},{28,20},{1,9},{5... | collective-permute-start | bytes 1179656 | tf_op jit(solution)/shard_map/ppermute | solution.py:42
  61.8 5.5 %collective-permute-start.12 = (bf16[256,256]{1,0:T(8,128)(2,1)S(1)}, bf16[256,256]{1,0:T(8,128)(2,1)S(1)}, u32[]{:S(2)}, u32[]{:S(2)}) collective-permute-start(bf16[256,256]{1,0:T(8,128)(2,1)S(1)} %get-tuple-element.74), channel_id=1, source_target_pairs={{0,3},{1,2},{2,1},{3,0},{4,7},{5,6},{6,5},{7,4},{8,11},{9,10},{10,... | collective-permute-start | bytes 393224 | tf_op jit(solution)/shard_map/ppermute | solution.py:42
  61.9 16.8 %collective-permute-start.15 = (bf16[2,64,512]{2,1,0:T(8,128)(2,1)S(1)}, bf16[2,64,512]{2,1,0:T(8,128)(2,1)S(1)}, u32[]{:S(2)}, u32[]{:S(2)}) collective-permute-start(bf16[2,64,512]{2,1,0:T(8,128)(2,1)S(1)} %get-tuple-element.80), channel_id=1, source_target_pairs={{0,16},{4,20},{8,24},{12,28},{16,0},{20,4},{24,8},{28,12},{1,17},{... | collective-permute-start | bytes 393224 | tf_op jit(solution)/shard_map/ppermute | solution.py:42
  65.1 2.2 %copy-start.14 = (bf16[256,256]{1,0:T(8,128)(2,1)}, bf16[256,256]{1,0:T(8,128)(2,1)S(1)}, u32[]{:S(2)}) copy-start(bf16[256,256]{1,0:T(8,128)(2,1)S(1)} %collective-permute-done.11.refs_4_) | copy-start | bytes 393220
  65.1 14.4 %collective-permute-start.16 = (bf16[2,64,512]{2,1,0:T(8,128)(2,1)S(1)}, bf16[2,64,512]{2,1,0:T(8,128)(2,1)S(1)}, u32[]{:S(2)}, u32[]{:S(2)}) collective-permute-start(bf16[2,64,512]{2,1,0:T(8,128)(2,1)S(1)} %get-tuple-element.81), channel_id=1, source_target_pairs={{0,24},{4,28},{8,16},{12,20},{16,8},{20,12},{24,0},{28,4},{1,25},{... | collective-permute-start | bytes 393224 | tf_op jit(solution)/shard_map/ppermute | solution.py:42
  67.3 0.7 copy-start.15
  67.3 0.8 copy-start.11
  68.1 15.0 %copy-start.1 = (bf16[16,256]{1,0:T(8,128)(2,1)S(1)}, bf16[16,256]{1,0:T(8,128)(2,1)}, u32[]{:S(2)}) copy-start(bf16[16,256]{1,0:T(8,128)(2,1)} %param.20) | copy-start | bytes 24580
  78.7 0.8 copy-start.16
  79.5 0.7 copy-start.17
  79.5 0.8 copy-start.12

commit v3 on v2

--- a/solution.py
+++ b/solution.py
@@ -14,7 +14,7 @@
 TINY = 1e-06
 BF = jnp.bfloat16
 F32 = jnp.float32
-SCALE = 0.001
+SCALE = 0.0
 VMEM_LIMIT = 12 * 1024 * 1024
 MOST_VMEM = 60 * 1024 * 1024
 STORE_BYTES = 56 * 1024 * 1024
@@ -164,6 +164,8 @@
                 moment = eta * (keep * moment) - dot(products[:, :d].astype(BF), held_low) + cross
                 state[s, h] = (stay * held + moment, moment)
     late = 1 - (me & 1)
+    copies.append(pltpu.make_async_copy(r_ref.at[1 - late], store_ref.at[rel + 1 - late], sem.at[packs]))
+    copies[-1].start()
     for h in range(heads):
         maps = [jnp.concatenate(state[s, h], axis=0) for s in range(2)]
         earlier, later = ordered(me & 1, maps[0], maps[1])
@@ -188,8 +190,10 @@
         r_ref[late, h, :, : 2 * d] = folded[:, : 2 * d].astype(BF)
         r_ref[late, h, :, 2 * d : 3 * d] = high
         r_ref[late, h, :, 3 * d :] = (shift - high.astype(F32)).astype(BF)
-    copies.append(pltpu.make_async_copy(r_ref, store_ref.at[pl.ds(rel, 2)], sem.at[packs]))
-    copies[-1].start()
+        copies.append(
+            pltpu.make_async_copy(r_ref.at[late, h], store_ref.at[rel + late, h], sem.at[packs + 1 + h])
+        )
+        copies[-1].start()
     for one in copies:
         one.wait()
 
@@ -235,7 +239,7 @@
         scratch_shapes=[
             pltpu.VMEM((sum(counts), SPAN, row), BF),
             pltpu.VMEM((2, heads, rows, 4 * d), BF),
-            pltpu.SemaphoreType.DMA((len(counts) + 1,)),
+            pltpu.SemaphoreType.DMA((len(counts) + 1 + heads,)),
         ],
         compiler_params=params(),
         cost_estimate=cost(2.5e9, 8e6),

time: 83.8 us -> 83.3 us (level)
  no operation moved by 1% of the time
where the time goes in v3:
time: 83.3 us; the launch traced here: 82.8 us
  Pallas kernels  30.7 us (37%)
  starting transfers between devices  26.5 us (32%)
  waiting for transfers between devices  12.7 us (15%)
  local copies, waits for them, and re-layouts  9.04 us (11%)
  other arithmetic  1.99 us (2%)
  between operations  1.05 us (1%)
  matrix products  0.91 us (1%)
    ppermute x15, starting transfers between devices, exchange(): return lax.ppermute(value, axis, [(i, i ^ bit) for i in range(count)])  18.4 us
    pallas_call x2, Pallas kernels, pair_call(): pl.pallas_call(functools.partial(pair_kernel, heads, d, blocks, rel, is_l...  12 us
    pallas_call x1, Pallas kernels, ffn(): pl.pallas_call(functools.partial(ffn_kernel, shards, tile), out_shape=jax...  10.5 us
    ppermute x15, waiting for transfers between devices, exchange(): return lax.ppermute(value, axis, [(i, i ^ bit) for i in range(count)])  9.46 us
    ppermute x2, starting transfers between devices, per_device(): state = lax.ppermute(state, 'seq', onward)  8.06 us
    unnamed x37, local copies, waits for them, and re-layouts  7.07 us
    ppermute x2, waiting for transfers between devices, per_device(): state = lax.ppermute(state, 'seq', onward)  3.24 us
    pallas_call x1, Pallas kernels, recall(): pl.pallas_call(functools.partial(recall_kernel, heads, d, groups), out_sh...  2.86 us
  transfers between devices with their start and end apart: 17, of which 6 were waited for; matrix products, arithmetic and copies ran while one was open for 8% of the time, Pallas kernels for 26%

profile of v3, /device:TPU:0, one launch (start us, length us, event | category | flops | bytes accessed | tf_op | source)
XLA Modules:
  0.0 82.8 jit_solution(890987385053598653)
XLA Ops:
  0.6 0.5 collective-permute-start
  1.2 2.6 %collective-permute-start.1 = (bf16[256,1024]{1,0:T(8,128)(2,1)}, bf16[256,1024]{1,0:T(8,128)(2,1)S(1)}, u32[]{:S(2)}, u32[]{:S(2)}) collective-permute-start(bf16[256,1024]{1,0:T(8,128)(2,1)} %refs_0_.1), channel_id=1, source_target_pairs={{0,2},{1,3},{2,0},{3,1},{4,6},{5,7},{6,4},{7,5},{8,10},{9,11},{10,... | collective-permute-start | bytes 1572872 | tf_op jit(solution)/shard_map/ppermute | solution.py:42
  3.8 0.2 collective-permute-start.2
  3.9 0.8 %reshape.91 = s32[128,64]{1,0:T(8,128)S(1)} reshape(s32[8192]{0:T(1024)} %param.28) | data formatting | bytes 65536 | tf_op jit(solution)/shard_map/reshape | solution.py:539
  4.8 0.1 fusion
  4.9 1.7 %copy.38 = bf16[128,8,2,384]{3,1,2,0:T(8,128)(2,1)S(1)} copy(bf16[128,8,2,384]{3,2,1,0:T(2,128)(2,1)} %bitcast.26) | data formatting | bytes 3145728
  6.6 0.7 copy.31
  7.3 0.2 copy.34.refs_7_
  7.7 0.7 pad_maximum_fusion.refs_1_
  8.5 0.9 %convolution_multiply_fusion.refs_8_ = f32[2,128,128]{2,1,0:T(8,128)S(1)} fusion(bf16[16,256]{1,0:T(8,128)(2,1)S(1)} %copy-done, bf16[16,256]{1,0:T(8,128)(2,1)} %param.19), kind=kOutput, calls=%fused_computation | convolution fusion | flops 1081344 | bytes 147456 | tf_op jit(solution)/shard_map/phd,phe->hde/dot_general | solution.py:558
  9.4 1.0 %copy-done.2 = bf16[256,1024]{1,0:T(8,128)(2,1)S(1)} copy-done((bf16[256,1024]{1,0:T(8,128)(2,1)S(1)}, bf16[256,1024]{1,0:T(8,128)(2,1)}, u32[]{:S(2)}) %copy-start.2) | copy-done | bytes 524312
  10.5 0.7 copy-done.7
  11.1 0.7 copy-done.8
  11.8 5.9 %pair_first.1 = (bf16[112,2,256,512]{3,2,1,0:T(8,128)(2,1)}, bf16[2,256,384]{2,1,0:T(8,128)(2,1)S(1)}, bf16[8,64,512]{2,1,0:T(8,128)(2,1)S(1)}, s32[16]{0:T(128)S(1)}) custom-call(s32[2]{0:T(128)S(1)} %pad_add_fusion.refs_0_.meta_ref, f32[20]{0:T(128)S(1)} %pad_maximum_fusion.refs_1_, s32[128]{0:T(128)S(1)} %copy-done.8, bf16[256,1024]{1,0:T(8,128)(2,1)S(1)} %copy-done.2, ...), custom_call_target="tpu_custom_call" | custom-call | tf_op jit(solution)/shard_map/pair_first/pallas_call | solution.py:230
  17.8 0.4 collective-permute-start.3
  18.2 1.6 %collective-permute-done.3.refs_4_ = bf16[256,1024]{1,0:T(8,128)(2,1)S(1)} collective-permute-done((bf16[256,1024]{1,0:T(8,128)(2,1)S(1)}, bf16[256,1024]{1,0:T(8,128)(2,1)S(1)}, u32[]{:S(2)}, u32[]{:S(2)}) %collective-permute-start.3) | collective-permute-done | bytes 524320 | tf_op jit(solution)/shard_map/ppermute | solution.py:42
  19.7 6.1 %pair_last.1 = (bf16[112,2,256,512]{3,2,1,0:T(8,128)(2,1)}, bf16[2,256,384]{2,1,0:T(8,128)(2,1)S(1)}, bf16[8,64,512]{2,1,0:T(8,128)(2,1)S(1)}, bf16[2,64,512]{2,...) custom-call(s32[2]{0:T(128)S(1)} %pad_add_fusion.refs_0_.meta_ref, ...), custom_call_target="tpu_custom_call", output_to_operand_aliasing={{0}: (11, {})} | custom-call | tf_op jit(solution)/shard_map/pair_last/pallas_call | solution.py:230
  25.9 1.6 %collective-permute-start.4 = (bf16[2,256,384]{2,1,0:T(8,128)(2,1)S(1)}, bf16[2,256,384]{2,1,0:T(8,128)(2,1)S(1)}, u32[]{:S(2)}, u32[]{:S(2)}) collective-permute-start(bf16[2,256,384]{2,1,0:T(8,128)(2,1)S(1)} %get-tuple-element.53.own_ref), channel_id=1, source_target_pairs={{0,4},{4,0},{8,12},{12,8},{16,20},{20,16},{24,28},{28,24},{1,5},{5... | collective-permute-start | bytes 1179656 | tf_op jit(solution)/shard_map/ppermute | solution.py:42
  27.4 0.5 collective-permute-start.7
  27.9 2.6 %collective-permute-start.6 = (bf16[4,64,512]{2,1,0:T(8,128)(2,1)S(1)}, bf16[4,64,512]{2,1,0:T(8,128)(2,1)S(1)}, u32[]{:S(2)}, u32[]{:S(2)}) collective-permute-start(bf16[4,64,512]{2,1,0:T(8,128)(2,1)S(1)} %get-tuple-element.58), channel_id=1, source_target_pairs={{0,16},{4,20},{8,24},{12,28},{16,0},{20,4},{24,8},{28,12},{1,17},{... | collective-permute-start | bytes 786440 | tf_op jit(solution)/shard_map/ppermute | solution.py:42
  30.5 6.8 %collective-permute-done.4.got_ref.refs_1_ = bf16[2,256,384]{2,1,0:T(8,128)(2,1)S(1)} collective-permute-done((bf16[2,256,384]{2,1,0:T(8,128)(2,1)S(1)}, bf16[2,256,384]{2,1,0:T(8,128)(2,1)S(1)}, u32[]{:S(2)}, u32[]{:S(2)}) %collective-permute-start.4) | collective-permute-done | bytes 393248 | tf_op jit(solution)/shard_map/ppermute | solution.py:42
  37.3 0.9 %join.1 = (bf16[2,256,256]{2,1,0:T(8,128)(2,1)S(1)}, bf16[2,256,128]{2,1,0:T(8,128)(2,1)S(1)}) custom-call(s32[2]{0:T(128)S(1)} %pad_add_fusion.refs_0_.meta_ref, bf16[2,256,384]{2,1,0:T(8,128)(2,1)S(1)} %get-tuple-element.53.own_ref, bf16[2,256,384]{2,1,0:T(8,128)(2,1)S(1)} %collective-permute-done.4.got_ref.refs_1_), custom_call_target="tpu_custom_call" | custom-call | tf_op jit(solution)/shard_map/join/pallas_call | solution.py:262
  38.2 3.5 %collective-permute-start.5 = (bf16[2,256,128]{2,1,0:T(8,128)(2,1)S(1)}, bf16[2,256,128]{2,1,0:T(8,128)(2,1)S(1)}, u32[]{:S(2)}, u32[]{:S(2)}) collective-permute-start(bf16[2,256,128]{2,1,0:T(8,128)(2,1)S(1)} %get-tuple-element.57.b_ref), channel_id=1, source_target_pairs={{0,8},{4,12},{8,16},{12,20},{16,24},{20,28},{1,9},{5,13},{9,17},{1... | collective-permute-start | bytes 393224 | tf_op jit(solution)/shard_map/ppermute | solution.py:591
  41.7 1.6 %collective-permute-start.10 = (bf16[8,64,512]{2,1,0:T(8,128)(2,1)}, bf16[8,64,512]{2,1,0:T(8,128)(2,1)S(1)}, u32[]{:S(2)}, u32[]{:S(2)}) collective-permute-start(bf16[8,64,512]{2,1,0:T(8,128)(2,1)} %copy-done.10), channel_id=1, source_target_pairs={{0,4},{4,0},{8,12},{12,8},{16,20},{20,16},{24,28},{28,24},{1,5},{5... | collective-permute-start | bytes 1572872 | tf_op jit(solution)/shard_map/ppermute | solution.py:42
  43.2 1.0 %collective-permute-done.5.state_ref = bf16[2,256,128]{2,1,0:T(8,128)(2,1)S(1)} collective-permute-done((bf16[2,256,128]{2,1,0:T(8,128)(2,1)S(1)}, bf16[2,256,128]{2,1,0:T(8,128)(2,1)S(1)}, u32[]{:S(2)}, u32[]{:S(2)}) %collective-permute-start.5) | collective-permute-done | bytes 131104 | tf_op jit(solution)/shard_map/ppermute | solution.py:591
  44.2 0.2 step.1
  44.4 4.6 %collective-permute-start.8 = (bf16[2,256,128]{2,1,0:T(8,128)(2,1)S(1)}, bf16[2,256,128]{2,1,0:T(8,128)(2,1)S(1)}, u32[]{:S(2)}, u32[]{:S(2)}) collective-permute-start(bf16[2,256,128]{2,1,0:T(8,128)(2,1)S(1)} %step.1), channel_id=1, source_target_pairs={{0,8},{4,12},{8,16},{12,20},{16,24},{20,28},{1,9},{5,13},{9,17},{1... | collective-permute-start | bytes 393224 | tf_op jit(solution)/shard_map/ppermute | solution.py:591
  49.0 2.3 %collective-permute-done.8.refs_2_ = bf16[2,256,128]{2,1,0:T(8,128)(2,1)S(1)} collective-permute-done((bf16[2,256,128]{2,1,0:T(8,128)(2,1)S(1)}, bf16[2,256,128]{2,1,0:T(8,128)(2,1)S(1)}, u32[]{:S(2)}, u32[]{:S(2)}) %collective-permute-start.8) | collective-permute-done | bytes 131104 | tf_op jit(solution)/shard_map/ppermute | solution.py:591
  51.3 2.9 %recall.1 = (bf16[256,256]{1,0:T(8,128)(2,1)S(1)}, bf16[256,256]{1,0:T(8,128)(2,1)S(1)}, bf16[256,256]{1,0:T(8,128)(2,1)S(1)}, bf16[256,256]{1,0:T(8,128)(2,1)S(1)}) custom-call(s32[2]{0:T(128)S(1)} %pad_add_fusion.refs_0_.meta_ref, bf16[2,256,384]{2,1,0:T(8,128)(2,1)S(1)} %collective-permute-done.4.got_ref.refs_1_, ...), custom_call_target="tpu_custom_call" | custom-call | tf_op jit(solution)/shard_map/recall/pallas_call | solution.py:336
  54.2 0.6 copy-done.4
  54.9 0.2 convert_reduce_fusion
  55.2 0.6 collective-permute-start.13
  55.7 1.0 %collective-permute-start.11 = (bf16[256,256]{1,0:T(8,128)(2,1)S(1)}, bf16[256,256]{1,0:T(8,128)(2,1)S(1)}, u32[]{:S(2)}, u32[]{:S(2)}) collective-permute-start(bf16[256,256]{1,0:T(8,128)(2,1)S(1)} %get-tuple-element.73), channel_id=1, source_target_pairs={{0,2},{1,3},{2,0},{3,1},{4,6},{5,7},{6,4},{7,5},{8,10},{9,11},{10,... | collective-permute-start | bytes 393224 | tf_op jit(solution)/shard_map/ppermute | solution.py:42
  56.7 1.3 %regroup.1 = (bf16[6,64,512]{2,1,0:T(8,128)(2,1)S(1)}, bf16[2,64,512]{2,1,0:T(8,128)(2,1)S(1)}, bf16[2,64,512]{2,1,0:T(8,128)(2,1)S(1)}, bf16[2,64,512]{2,1,0:T(8,128)(2,1)S(1)}) custom-call(bf16[8,64,512]{2,1,0:T(8,128)(2,1)S(1)} %collective-permute-done.10.refs_0_, bf16[4,64,512]{2,1,0:T(8,128)(2,1)S(1)} %collective-permute-done.6.refs_1_.refs_2_, ...), custom_call_target="tpu_custom_call" | custom-call | tf_op jit(solution)/shard_map/regroup/pallas_call | solution.py:452
  58.1 0.6 copy-done.6
  58.7 2.5 %collective-permute-start.14 = (bf16[6,64,512]{2,1,0:T(8,128)(2,1)S(1)}, bf16[6,64,512]{2,1,0:T(8,128)(2,1)S(1)}, u32[]{:S(2)}, u32[]{:S(2)}) collective-permute-start(bf16[6,64,512]{2,1,0:T(8,128)(2,1)S(1)} %get-tuple-element.79), channel_id=1, source_target_pairs={{0,8},{4,12},{8,0},{12,4},{16,24},{20,28},{24,16},{28,20},{1,9},{5... | collective-permute-start | bytes 1179656 | tf_op jit(solution)/shard_map/ppermute | solution.py:42
  61.3 0.1 collective-permute-start.12
  61.4 3.2 %collective-permute-start.15 = (bf16[2,64,512]{2,1,0:T(8,128)(2,1)S(1)}, bf16[2,64,512]{2,1,0:T(8,128)(2,1)S(1)}, u32[]{:S(2)}, u32[]{:S(2)}) collective-permute-start(bf16[2,64,512]{2,1,0:T(8,128)(2,1)S(1)} %get-tuple-element.80), channel_id=1, source_target_pairs={{0,16},{4,20},{8,24},{12,28},{16,0},{20,4},{24,8},{28,12},{1,17},{... | collective-permute-start | bytes 393224 | tf_op jit(solution)/shard_map/ppermute | solution.py:42
  64.6 1.1 %collective-permute-start.16 = (bf16[2,64,512]{2,1,0:T(8,128)(2,1)S(1)}, bf16[2,64,512]{2,1,0:T(8,128)(2,1)S(1)}, u32[]{:S(2)}, u32[]{:S(2)}) collective-permute-start(bf16[2,64,512]{2,1,0:T(8,128)(2,1)S(1)} %get-tuple-element.81), channel_id=1, source_target_pairs={{0,24},{4,28},{8,16},{12,20},{16,8},{20,12},{24,0},{28,4},{1,25},{... | collective-permute-start | bytes 393224 | tf_op jit(solution)/shard_map/ppermute | solution.py:42
  65.8 0.6 select_reduce_fusion.rows_ref
  66.5 0.3 collective-permute-done.12.refs_5_
  66.8 0.6 copy-done.15
  67.4 0.2 copy-done.11
  67.6 10.5 %ffn.1 = bf16[256,1024]{1,0:T(8,128)(2,1)} custom-call(bf16[256,1024]{1,0:T(8,128)(2,1)} %refs_0_.1, f32[1,1024]{1,0:T(1,128)} %bitcast.28, bf16[256,256]{1,0:T(8,128)(2,1)} %copy-done.4, bf16[256,256]{1,0:T(8,128)(2,1)} %copy-done.13, bf16[256,256]{1,0:T(8,128)(2,1)} %copy-done.14, bf16[256,256]{1,0:T(8,128)(2,1)} %copy-done.15, bf16[256,1024]{1,0:T(8,128)(2,1)} %refs_6_, ...), custom_call_target="tpu_custom_call" | custom-call | tf_op jit(solution)/shard_map/ffn/pallas_call | solution.py:400
  78.2 0.8 collective-permute-done.16.refs_5_
  79.0 0.6 copy-done.17
  79.7 0.2 copy-done.12
  79.8 2.8 %place.1 = bf16[16,64,512]{2,1,0:T(8,128)(2,1)} custom-call(s32[16]{0:T(128)} %select_reduce_fusion.rows_ref, bf16[2,64,512]{2,1,0:T(8,128)(2,1)} %copy-done.6, bf16[2,64,512]{2,1,0:T(8,128)(2,1)} %copy-done.5, bf16[4,64,512]{2,1,0:T(8,128)(2,1)} %copy-done.3, bf16[6,64,512]{2,1,0:T(8,128)(2,1)} %copy-done.12, bf16[2,64,512]{2,1,0:T(8,128)(2,1)} %copy-done.16, ...), custom_call_target="tpu_custom_call" | custom-call | tf_op jit(solution)/shard_map/place/pallas_call | solution.py:488
  (50 shorter events, 0.6 us)
Async XLA Ops:
  0.6 7.9 %copy-start = (bf16[16,256]{1,0:T(8,128)(2,1)S(1)}, bf16[16,256]{1,0:T(8,128)(2,1)}, u32[]{:S(2)}) copy-start(bf16[16,256]{1,0:T(8,128)(2,1)} %param.20) | copy-start | bytes 24580
  0.6 8.8 %collective-permute-start = (bf16[256,1024]{1,0:T(8,128)(2,1)}, bf16[256,1024]{1,0:T(8,128)(2,1)S(1)}, u32[]{:S(2)}, u32[]{:S(2)}) collective-permute-start(bf16[256,1024]{1,0:T(8,128)(2,1)} %refs_0_.1), channel_id=1, source_target_pairs={{0,1},{1,0},{2,3},{3,2},{4,5},{5,4},{6,7},{7,6},{8,9},{9,8},{10,11... | collective-permute-start | bytes 1572872 | tf_op jit(solution)/shard_map/ppermute | solution.py:42
  1.2 16.6 %collective-permute-start.1 = (bf16[256,1024]{1,0:T(8,128)(2,1)}, bf16[256,1024]{1,0:T(8,128)(2,1)S(1)}, u32[]{:S(2)}, u32[]{:S(2)}) collective-permute-start(bf16[256,1024]{1,0:T(8,128)(2,1)} %refs_0_.1), channel_id=1, source_target_pairs={{0,2},{1,3},{2,0},{3,1},{4,6},{5,7},{6,4},{7,5},{8,10},{9,11},{10,... | collective-permute-start | bytes 1572872 | tf_op jit(solution)/shard_map/ppermute | solution.py:42
  3.8 14.0 %collective-permute-start.2 = (bf16[256,1024]{1,0:T(8,128)(2,1)}, bf16[256,1024]{1,0:T(8,128)(2,1)}, u32[]{:S(2)}, u32[]{:S(2)}) collective-permute-start(bf16[256,1024]{1,0:T(8,128)(2,1)} %refs_6_), channel_id=1, source_target_pairs={{0,1},{1,0},{2,3},{3,2},{4,5},{5,4},{6,7},{7,6},{8,9},{9,8},{10,11... | collective-permute-start | bytes 1572872 | tf_op jit(solution)/shard_map/ppermute | solution.py:42
  9.4 1.0 %copy-start.2 = (bf16[256,1024]{1,0:T(8,128)(2,1)S(1)}, bf16[256,1024]{1,0:T(8,128)(2,1)}, u32[]{:S(2)}) copy-start(bf16[256,1024]{1,0:T(8,128)(2,1)} %refs_0_.1) | copy-start | bytes 1572868
  10.5 0.7 copy-start.7
  11.1 0.7 copy-start.8
  17.8 2.0 %collective-permute-start.3 = (bf16[256,1024]{1,0:T(8,128)(2,1)S(1)}, bf16[256,1024]{1,0:T(8,128)(2,1)S(1)}, u32[]{:S(2)}, u32[]{:S(2)}) collective-permute-start(bf16[256,1024]{1,0:T(8,128)(2,1)S(1)} %collective-permute-done.1.refs_3_), channel_id=1, source_target_pairs={{0,1},{1,0},{2,3},{3,2},{4,5},{5,4},{6,7},{7,6},{8,9},{9,8},{10,11... | collective-permute-start | bytes 1572872 | tf_op jit(solution)/shard_map/ppermute | solution.py:42
  25.8 12.3 %copy-start.5 = (bf16[2,64,512]{2,1,0:T(8,128)(2,1)}, bf16[2,64,512]{2,1,0:T(8,128)(2,1)S(1)}, u32[]{:S(2)}) copy-start(bf16[2,64,512]{2,1,0:T(8,128)(2,1)S(1)} %get-tuple-element.85.refs_1_) | copy-start | bytes 393220
  25.8 12.3 %copy-start.10 = (bf16[8,64,512]{2,1,0:T(8,128)(2,1)}, bf16[8,64,512]{2,1,0:T(8,128)(2,1)S(1)}, u32[]{:S(2)}) copy-start(bf16[8,64,512]{2,1,0:T(8,128)(2,1)S(1)} %get-tuple-element.65) | copy-start | bytes 1572868
  25.9 11.4 %collective-permute-start.4 = (bf16[2,256,384]{2,1,0:T(8,128)(2,1)S(1)}, bf16[2,256,384]{2,1,0:T(8,128)(2,1)S(1)}, u32[]{:S(2)}, u32[]{:S(2)}) collective-permute-start(bf16[2,256,384]{2,1,0:T(8,128)(2,1)S(1)} %get-tuple-element.53.own_ref), channel_id=1, source_target_pairs={{0,4},{4,0},{8,12},{12,8},{16,20},{20,16},{24,28},{28,24},{1,5},{5... | collective-permute-start | bytes 1179656 | tf_op jit(solution)/shard_map/ppermute | solution.py:42
  27.4 16.8 %collective-permute-start.7 = (bf16[256,1024]{1,0:T(8,128)(2,1)}, bf16[256,1024]{1,0:T(8,128)(2,1)}, u32[]{:S(2)}, u32[]{:S(2)}) collective-permute-start(bf16[256,1024]{1,0:T(8,128)(2,1)} %refs_6_), channel_id=1, source_target_pairs={{0,2},{1,3},{2,0},{3,1},{4,6},{5,7},{6,4},{7,5},{8,10},{9,11},{10,... | collective-permute-start | bytes 1572872 | tf_op jit(solution)/shard_map/ppermute | solution.py:42
  27.9 15.3 %collective-permute-start.6 = (bf16[4,64,512]{2,1,0:T(8,128)(2,1)S(1)}, bf16[4,64,512]{2,1,0:T(8,128)(2,1)S(1)}, u32[]{:S(2)}, u32[]{:S(2)}) collective-permute-start(bf16[4,64,512]{2,1,0:T(8,128)(2,1)S(1)} %get-tuple-element.58), channel_id=1, source_target_pairs={{0,16},{4,20},{8,24},{12,28},{16,0},{20,4},{24,8},{28,12},{1,17},{... | collective-permute-start | bytes 786440 | tf_op jit(solution)/shard_map/ppermute | solution.py:42
  38.2 6.0 %collective-permute-start.5 = (bf16[2,256,128]{2,1,0:T(8,128)(2,1)S(1)}, bf16[2,256,128]{2,1,0:T(8,128)(2,1)S(1)}, u32[]{:S(2)}, u32[]{:S(2)}) collective-permute-start(bf16[2,256,128]{2,1,0:T(8,128)(2,1)S(1)} %get-tuple-element.57.b_ref), channel_id=1, source_target_pairs={{0,8},{4,12},{8,16},{12,20},{16,24},{20,28},{1,9},{5,13},{9,17},{1... | collective-permute-start | bytes 393224 | tf_op jit(solution)/shard_map/ppermute | solution.py:591
  41.7 15.1 %collective-permute-start.10 = (bf16[8,64,512]{2,1,0:T(8,128)(2,1)}, bf16[8,64,512]{2,1,0:T(8,128)(2,1)S(1)}, u32[]{:S(2)}, u32[]{:S(2)}) collective-permute-start(bf16[8,64,512]{2,1,0:T(8,128)(2,1)} %copy-done.10), channel_id=1, source_target_pairs={{0,4},{4,0},{8,12},{12,8},{16,20},{20,16},{24,28},{28,24},{1,5},{5... | collective-permute-start | bytes 1572872 | tf_op jit(solution)/shard_map/ppermute | solution.py:42
  43.2 13.5 %copy-start.3 = (bf16[4,64,512]{2,1,0:T(8,128)(2,1)}, bf16[4,64,512]{2,1,0:T(8,128)(2,1)S(1)}, u32[]{:S(2)}) copy-start(bf16[4,64,512]{2,1,0:T(8,128)(2,1)S(1)} %collective-permute-done.6.refs_1_.refs_2_) | copy-start | bytes 786436
  44.4 6.9 %collective-permute-start.8 = (bf16[2,256,128]{2,1,0:T(8,128)(2,1)S(1)}, bf16[2,256,128]{2,1,0:T(8,128)(2,1)S(1)}, u32[]{:S(2)}, u32[]{:S(2)}) collective-permute-start(bf16[2,256,128]{2,1,0:T(8,128)(2,1)S(1)} %step.1), channel_id=1, source_target_pairs={{0,8},{4,12},{8,16},{12,20},{16,24},{20,28},{1,9},{5,13},{9,17},{1... | collective-permute-start | bytes 393224 | tf_op jit(solution)/shard_map/ppermute | solution.py:591
  51.3 3.5 %copy-start.9 = (s32[128]{0:T(128)S(1)}, s32[128]{0:T(128)}, u32[]{:S(2)}) copy-start(s32[128]{0:T(128)} %refs_2_.1) | copy-start | bytes 1540
  54.2 0.7 copy-start.4
  54.8 3.9 %collective-permute-start.9 = (bf16[256,256]{1,0:T(8,128)(2,1)S(1)}, bf16[256,256]{1,0:T(8,128)(2,1)S(1)}, u32[]{:S(2)}, u32[]{:S(2)}) collective-permute-start(bf16[256,256]{1,0:T(8,128)(2,1)S(1)} %get-tuple-element.64), channel_id=1, source_target_pairs={{0,1},{1,0},{2,3},{3,2},{4,5},{5,4},{6,7},{7,6},{8,9},{9,8},{10,11... | collective-permute-start | bytes 393224 | tf_op jit(solution)/shard_map/ppermute | solution.py:42
  55.2 11.6 %collective-permute-start.13 = (bf16[256,1024]{1,0:T(8,128)(2,1)}, bf16[256,1024]{1,0:T(8,128)(2,1)S(1)}, u32[]{:S(2)}, u32[]{:S(2)}) collective-permute-start(bf16[256,1024]{1,0:T(8,128)(2,1)} %collective-permute-done.7.refs_8_), channel_id=1, source_target_pairs={{0,1},{1,0},{2,3},{3,2},{4,5},{5,4},{6,7},{7,6},{8,9},{9,8},{10,11... | collective-permute-start | bytes 1572872 | tf_op jit(solution)/shard_map/ppermute | solution.py:42
  55.7 8.9 %collective-permute-start.11 = (bf16[256,256]{1,0:T(8,128)(2,1)S(1)}, bf16[256,256]{1,0:T(8,128)(2,1)S(1)}, u32[]{:S(2)}, u32[]{:S(2)}) collective-permute-start(bf16[256,256]{1,0:T(8,128)(2,1)S(1)} %get-tuple-element.73), channel_id=1, source_target_pairs={{0,2},{1,3},{2,0},{3,1},{4,6},{5,7},{6,4},{7,5},{8,10},{9,11},{10,... | collective-permute-start | bytes 393224 | tf_op jit(solution)/shard_map/ppermute | solution.py:42
  58.1 0.7 copy-start.6
  58.7 8.1 %copy-start.13 = (bf16[256,256]{1,0:T(8,128)(2,1)}, bf16[256,256]{1,0:T(8,128)(2,1)S(1)}, u32[]{:S(2)}) copy-start(bf16[256,256]{1,0:T(8,128)(2,1)S(1)} %collective-permute-done.9.refs_3_) | copy-start | bytes 393220
  58.7 20.3 %collective-permute-start.14 = (bf16[6,64,512]{2,1,0:T(8,128)(2,1)S(1)}, bf16[6,64,512]{2,1,0:T(8,128)(2,1)S(1)}, u32[]{:S(2)}, u32[]{:S(2)}) collective-permute-start(bf16[6,64,512]{2,1,0:T(8,128)(2,1)S(1)} %get-tuple-element.79), channel_id=1, source_target_pairs={{0,8},{4,12},{8,0},{12,4},{16,24},{20,28},{24,16},{28,20},{1,9},{5... | collective-permute-start | bytes 1179656 | tf_op jit(solution)/shard_map/ppermute | solution.py:42
  61.3 5.5 %collective-permute-start.12 = (bf16[256,256]{1,0:T(8,128)(2,1)S(1)}, bf16[256,256]{1,0:T(8,128)(2,1)S(1)}, u32[]{:S(2)}, u32[]{:S(2)}) collective-permute-start(bf16[256,256]{1,0:T(8,128)(2,1)S(1)} %get-tuple-element.74), channel_id=1, source_target_pairs={{0,3},{1,2},{2,1},{3,0},{4,7},{5,6},{6,5},{7,4},{8,11},{9,10},{10,... | collective-permute-start | bytes 393224 | tf_op jit(solution)/shard_map/ppermute | solution.py:42
  61.4 16.8 %collective-permute-start.15 = (bf16[2,64,512]{2,1,0:T(8,128)(2,1)S(1)}, bf16[2,64,512]{2,1,0:T(8,128)(2,1)S(1)}, u32[]{:S(2)}, u32[]{:S(2)}) collective-permute-start(bf16[2,64,512]{2,1,0:T(8,128)(2,1)S(1)} %get-tuple-element.80), channel_id=1, source_target_pairs={{0,16},{4,20},{8,24},{12,28},{16,0},{20,4},{24,8},{28,12},{1,17},{... | collective-permute-start | bytes 393224 | tf_op jit(solution)/shard_map/ppermute | solution.py:42
  64.6 2.2 %copy-start.14 = (bf16[256,256]{1,0:T(8,128)(2,1)}, bf16[256,256]{1,0:T(8,128)(2,1)S(1)}, u32[]{:S(2)}) copy-start(bf16[256,256]{1,0:T(8,128)(2,1)S(1)} %collective-permute-done.11.refs_4_) | copy-start | bytes 393220
  64.6 14.4 %collective-permute-start.16 = (bf16[2,64,512]{2,1,0:T(8,128)(2,1)S(1)}, bf16[2,64,512]{2,1,0:T(8,128)(2,1)S(1)}, u32[]{:S(2)}, u32[]{:S(2)}) collective-permute-start(bf16[2,64,512]{2,1,0:T(8,128)(2,1)S(1)} %get-tuple-element.81), channel_id=1, source_target_pairs={{0,24},{4,28},{8,16},{12,20},{16,8},{20,12},{24,0},{28,4},{1,25},{... | collective-permute-start | bytes 393224 | tf_op jit(solution)/shard_map/ppermute | solution.py:42
  66.8 0.7 copy-start.15
  66.8 0.8 %copy-start.11 = (bf16[256,1024]{1,0:T(8,128)(2,1)}, bf16[256,1024]{1,0:T(8,128)(2,1)S(1)}, u32[]{:S(2)}) copy-start(bf16[256,1024]{1,0:T(8,128)(2,1)S(1)} %collective-permute-done.13.refs_9_) | copy-start | bytes 1572868
  67.6 15.0 %copy-start.1 = (bf16[16,256]{1,0:T(8,128)(2,1)S(1)}, bf16[16,256]{1,0:T(8,128)(2,1)}, u32[]{:S(2)}) copy-start(bf16[16,256]{1,0:T(8,128)(2,1)} %param.20) | copy-start | bytes 24580
  78.2 0.8 %copy-start.16 = (bf16[2,64,512]{2,1,0:T(8,128)(2,1)}, bf16[2,64,512]{2,1,0:T(8,128)(2,1)S(1)}, u32[]{:S(2)}) copy-start(bf16[2,64,512]{2,1,0:T(8,128)(2,1)S(1)} %collective-permute-done.15.refs_4_) | copy-start | bytes 393220
  79.0 0.7 copy-start.17
  79.0 0.8 copy-start.12
